TPU v7x, 32 devices: a whole 2x2x4 slice. The times are simulated.
32 devices in a mesh: cell: 16 (over z, y, core), brick: 2 (over x).
Axes of the slice: x: 2, y: 2, z: 4, core: 2. Of those that a mesh axis runs over, the one named last changes fastest.
Arguments:
- features: bfloat16 [16, 2, 128, 256], P('cell', 'brick'), may hold values from -6 to 6
- species: int32 [16, 2, 128], P('cell', 'brick'), may hold values from 0 to 3
- species_table: bfloat16 [4, 256], replicated, may hold values from -3 to 3
- neighbours: int32 [16, 2, 64, 128], P('cell', 'brick'), may hold values from 0 to 191
- counts: int32 [16, 2, 128], P('cell', 'brick'), may hold values from 1 to 64
- send_lists: int32 [16, 2, 2, 32], P('cell', 'brick'), may hold values from 0 to 127
- distances: float32 [16, 2, 64, 128], P('cell', 'brick'), may hold values from 0.05 to 1
- head_decay: float32 [8], replicated, may hold values from 0.25 to 4
- norm_gain: float32 [256], replicated, may hold values from 0.5 to 1.5
- readout: float32 [256], replicated, may hold values from -0.375 to 0.375
- targets: float32 [16, 2, 128], P('cell', 'brick'), may hold values from -6 to 6
- master: float32 [4, 256, 256], P(None, 'cell'), as said below
- moment: float32 [4, 256, 256], P(None, 'cell'), may hold values from -3 to 3
- second: float32 [4, 256, 256], P(None, 'cell'), may hold values from 0.1 to 1
Outputs:
- energies: float32 [16, 2, 128], P('cell', 'brick')
- moment_new: float32 [4, 256, 256], P(None, 'cell')
- second_new: float32 [4, 256, 256], P(None, 'cell')
- adam_step: float32 [4, 256, 256], P(None, 'cell')
Inputs may be any that keep to these rules, and one draw needn't show every extreme that they name: `master`: projection entries lie within -48 * 256^-0.5 and 48 * 256^-0.5.
All inputs are finite; a program needn't handle non-finite values.
Results may differ from a plain program's by a relative error of at most 0.0045.
The roundings to bfloat16 on the way count: a program that leaves them out, or rounds other values in their place, can miss the bound.
Values may be sent and summed in bfloat16 or wider, within the bound.
No kernel may reach another device: no remote copies, remote signals or barrier semaphores. Data moves between devices by JAX's collectives and lax.ppermute only.
A program may use at most 64 MiB of HBM per device.

v0:
```python
import math

import jax
import jax.numpy as jnp
from jax import lax
from jax.sharding import PartitionSpec as P

TILE = 128


loss_weight = 0.0625
epsilon_norm = 1e-06


def silu_slope(inputs):
    sigmoid_val = jax.nn.sigmoid(inputs)
    return sigmoid_val * (1.0 + inputs * (1.0 - sigmoid_val))


def normalize(embedded, norm_gain):
    rms_scale = lax.rsqrt(jnp.mean(embedded * embedded, axis=-1, keepdims=True) + epsilon_norm)
    return (embedded * rms_scale * norm_gain).astype(jnp.bfloat16)


def brick_sweep(
    query,
    key_table,
    value_table,
    embedded,
    neighbour_rows,
    local_count,
    local_dist,
    local_target,
    out_proj,
    head_decay,
    readout,
):
    atom_count, model_width = query.shape
    head_count = head_decay.shape[0]
    head_size = model_width // head_count
    slot_count = neighbour_rows.shape[0]
    score_scale = 1.0 / math.sqrt(head_size)
    table_rows = key_table.shape[0]

    def tile_step(grad_carry, tile_index):
        key_grads, value_grads = grad_carry
        key_rows = key_table[neighbour_rows].reshape(slot_count, TILE, head_count, head_size)
        value_rows = value_table[neighbour_rows].reshape(slot_count, TILE, head_count, head_size)
        query_heads = query.reshape(TILE, head_count, head_size)
        is_valid = (jnp.arange(slot_count)[:, None] < local_count[None, :])[:, :, None]
        score = (
            jnp.einsum("ahd,kahd->kah", query_heads, key_rows, preferred_element_type=jnp.float32)
            * score_scale
        )
        score = score - head_decay[None, None, :] * local_dist[:, :, None]
        score = jnp.where(is_valid, score, -1e30)
        row_max = jnp.max(score, axis=0, keepdims=True)
        exp_terms = jnp.where(is_valid, jnp.exp(score - row_max), 0.0)
        attention = exp_terms / jnp.sum(exp_terms, axis=0, keepdims=True)
        attention_half = attention.astype(jnp.bfloat16)
        attended = jnp.einsum(
            "kah,kahd->ahd", attention_half, value_rows, preferred_element_type=jnp.float32
        )
        attended = attended.astype(jnp.bfloat16).reshape(TILE, model_width)
        updated = embedded + jnp.dot(attended, out_proj, preferred_element_type=jnp.float32)
        energy = jnp.sum(readout * jax.nn.silu(updated), axis=-1)
        grad_energy = loss_weight * (energy - local_target)
        grad_updated = (grad_energy[:, None] * readout * silu_slope(updated)).astype(jnp.bfloat16)
        grad_attended = jnp.einsum(
            "ad,cd->ac", grad_updated, out_proj, preferred_element_type=jnp.float32
        ).astype(jnp.bfloat16)
        grad_att_heads = grad_attended.reshape(TILE, head_count, head_size)
        grad_weights = jnp.einsum(
            "ahd,kahd->kah", grad_att_heads, value_rows, preferred_element_type=jnp.float32
        )
        grad_score = attention * (
            grad_weights - jnp.sum(attention * grad_weights, axis=0, keepdims=True)
        )
        grad_score = grad_score.astype(jnp.bfloat16)
        grad_query = (
            jnp.einsum("kah,kahd->ahd", grad_score, key_rows, preferred_element_type=jnp.float32)
            * score_scale
        )
        grad_query = grad_query.astype(jnp.bfloat16).reshape(TILE, model_width)
        key_edge = (
            grad_score.astype(jnp.float32)[..., None]
            * query_heads.astype(jnp.float32)[None]
            * score_scale
        )
        value_edge = (
            attention_half.astype(jnp.float32)[..., None] * grad_att_heads.astype(jnp.float32)[None]
        )
        flattened_rows = neighbour_rows.reshape(-1)
        key_grads = key_grads.at[flattened_rows].add(key_edge.reshape(-1, model_width))
        value_grads = value_grads.at[flattened_rows].add(value_edge.reshape(-1, model_width))
        return ((key_grads, value_grads), (energy, attended, grad_updated, grad_query))

    start_grads = (
        jnp.zeros((table_rows, model_width), jnp.float32),
        jnp.zeros((table_rows, model_width), jnp.float32),
    )
    (key_grads, value_grads), stacked = lax.scan(
        tile_step, start_grads, jnp.arange(atom_count // TILE, dtype=jnp.int32)
    )
    energy, attended, grad_updated, grad_query = stacked
    return (
        key_grads,
        value_grads,
        energy.reshape(atom_count),
        attended.reshape(atom_count, model_width),
        grad_updated.reshape(atom_count, model_width),
        grad_query.reshape(atom_count, model_width),
    )


def body(
    features,
    species,
    species_table,
    neighbours,
    counts,
    send_lists,
    distances,
    head_decay,
    norm_gain,
    readout,
    targets,
    master,
    moment,
    second,
):
    local_feat = features[0, 0]
    local_species = species[0, 0]
    neighbour_rows = neighbours[0, 0]
    local_count = counts[0, 0]
    send_rows = send_lists[0, 0]
    local_dist = distances[0, 0]
    local_target = targets[0, 0]
    atom_count, model_width = local_feat.shape
    bricks, ghost_position = send_rows.shape
    species_count = species_table.shape[0]
    picked = (local_species[:, None] == jnp.arange(species_count)[None, :]).astype(jnp.bfloat16)
    embedded = local_feat.astype(jnp.float32) + jnp.dot(
        picked, species_table, preferred_element_type=jnp.float32
    )
    normed_features = normalize(embedded, norm_gain)
    attention_weights = lax.all_gather(master.astype(jnp.bfloat16), "cell", axis=1, tiled=True)
    projected = jnp.einsum(
        "pe,mer->mpr", normed_features, attention_weights[0:3], preferred_element_type=jnp.float32
    ).astype(jnp.bfloat16)
    flat_send = send_rows.reshape(-1)
    parcel = normed_features[flat_send].reshape(bricks, ghost_position, model_width)
    arrived = lax.all_to_all(parcel, "brick", split_axis=0, concat_axis=0, tiled=True).reshape(
        -1, model_width
    )
    ghost_pair = jnp.einsum(
        "pe,mer->mpr", arrived, attention_weights[1:3], preferred_element_type=jnp.float32
    ).astype(jnp.bfloat16)
    ghost_keys = ghost_pair[0]
    ghost_values = ghost_pair[1]
    key_table = jnp.concatenate([projected[1], ghost_keys], axis=0)
    value_table = jnp.concatenate([projected[2], ghost_values], axis=0)
    key_grads, value_grads, energy, attended, grad_updated, grad_query = brick_sweep(
        projected[0],
        key_table,
        value_table,
        embedded,
        neighbour_rows,
        local_count,
        local_dist,
        local_target,
        attention_weights[3],
        head_decay,
        readout,
    )
    ghost_grads = jnp.stack([key_grads[atom_count:], value_grads[atom_count:]]).reshape(
        2, bricks, ghost_position, model_width
    )
    returned = lax.all_to_all(
        ghost_grads.astype(jnp.bfloat16), "brick", split_axis=1, concat_axis=1, tiled=True
    ).astype(ghost_grads.dtype)
    local_portion = jnp.stack([key_grads[:atom_count], value_grads[:atom_count]])
    totals = (
        local_portion.at[:, flat_send]
        .add(returned.reshape(2, -1, model_width))
        .astype(jnp.bfloat16)
    )
    grad_q = jnp.einsum(
        "ac,ad->cd", normed_features, grad_query, preferred_element_type=jnp.float32
    )
    key_gradient = jnp.einsum(
        "ac,ad->cd", normed_features, totals[0], preferred_element_type=jnp.float32
    )
    grad_v = jnp.einsum("ac,ad->cd", normed_features, totals[1], preferred_element_type=jnp.float32)
    grad_o = jnp.einsum("ac,ad->cd", attended, grad_updated, preferred_element_type=jnp.float32)
    grads = jnp.stack([grad_q, key_gradient, grad_v, grad_o])
    summed = lax.psum(grads.astype(jnp.bfloat16), "brick")
    owned = lax.psum_scatter(summed, "cell", scatter_dimension=1, tiled=True).astype(jnp.float32)
    moment_new = 0.9 * moment + 0.1 * owned
    second_new = 0.999 * second + 0.001 * owned * owned
    adam_step = moment_new / (jnp.sqrt(second_new) + 1e-08)
    return (energy[None, None, :], moment_new, second_new, adam_step)


def solution(mesh):
    return jax.shard_map(
        body,
        mesh=mesh,
        in_specs=(
            P("cell", "brick", None, None),
            P("cell", "brick", None),
            P(),
            P("cell", "brick", None, None),
            P("cell", "brick", None),
            P("cell", "brick", None, None),
            P("cell", "brick", None, None),
            P(),
            P(),
            P(),
            P("cell", "brick", None),
            P(None, "cell", None),
            P(None, "cell", None),
            P(None, "cell", None),
        ),
        out_specs=(
            P("cell", "brick", None),
            P(None, "cell", None),
            P(None, "cell", None),
            P(None, "cell", None),
        ),
        check_vma=False,
    )
```

profile of v0, /device:TPU:0, one launch (start us, length us, event | category | flops | bytes accessed | tf_op | source)
XLA Modules:
  0.0 372.3 jit_solution(16421749308818817945)
XLA Ops:
  7.2 0.0 copy-start
  7.2 0.8 reshape_squeeze.11
  8.0 1.2 multiply_reduce_fusion.5
  9.1 0.8 multiply_convert_fusion.2
  9.9 1.3 gather_fusion
  11.2 4.2 %all-to-all-start = ((bf16[2,32,256]{2,1,0:T(8,128)(2,1)}), bf16[2,32,256]{2,1,0:T(8,128)(2,1)S(1)}, u32[]{:S(2)}, u32[]{:S(2)}) async-start(bf16[2,32,256]{2,1,0:T(8,128)(2,1)} %bitcast.13), calls=%async_computation | async-start | bytes 65536 | tf_op jit(solution)/shard_map/all_to_all | solution.py:153
  15.4 0.8 fusion.39
  16.2 0.8 convert_element_type.85
  17.1 0.8 compare_select_fusion
  17.9 23.6 %all_gather.3 = bf16[4,256,256]{2,1,0:T(8,128)(2,1)S(1)} all-gather(bf16[4,16,256]{2,1,0:T(8,128)(2,1)S(1)} %convert_element_type.85), channel_id=1, replica_groups=mesh['cell'=16,'brick'=2] {'cell'}, dimensions={1}, use_global_device_ids=true | all-gather | bytes 557056 | tf_op jit(solution)/shard_map/all_gather | solution.py:147
  41.5 0.2 fusion.10
  41.7 0.7 iota_compare_fusion.2
  42.4 0.1 copy.38
  42.5 0.0 all-to-all-done
  42.6 0.2 fusion.15
  42.8 32.9 %gather_fusion.1 = bf16[8192,256]{1,0:T(8,128)(2,1)} fusion(bf16[192,256]{1,0:T(8,128)(2,1)S(1)} %get-tuple-element.81, s32[8192]{0:T(1024)S(1)} %fusion.39), kind=kCustom, calls=%fused_computation.1 | custom fusion | bytes 8421376 | tf_op jit(solution)/shard_map/while/body/eval_jaxpr/gather | solution.py:47
  75.7 6.4 %copy.37 = bf16[8192,256]{0,1:T(8,128)(2,1)} copy(bf16[8192,256]{1,0:T(8,128)(2,1)} %gather_fusion.1) | data formatting | bytes 8388608 | tf_op jit(solution)/shard_map/while/body/eval_jaxpr/gather | solution.py:47
  82.1 5.3 %copy.80 = bf16[32,8,64,128]{3,2,1,0:T(8,128)(2,1)} copy(bf16[32,8,64,128]{3,1,2,0:T(8,128)(2,1)} %bitcast.151) | data formatting | bytes 8388608
  87.4 32.9 %gather_fusion.2 = bf16[8192,256]{1,0:T(8,128)(2,1)} fusion(bf16[192,256]{1,0:T(8,128)(2,1)S(1)} %get-tuple-element.82, s32[8192]{0:T(1024)S(1)} %fusion.39), kind=kCustom, calls=%fused_computation.2 | custom fusion | bytes 8421376 | tf_op jit(solution)/shard_map/while/body/eval_jaxpr/gather | solution.py:48
  120.3 6.7 %copy.39 = bf16[8192,256]{0,1:T(8,128)(2,1)} copy(bf16[8192,256]{1,0:T(8,128)(2,1)} %gather_fusion.2) | data formatting | bytes 8388608 | tf_op jit(solution)/shard_map/while/body/eval_jaxpr/gather | solution.py:48
  127.1 0.0 copy-start.6
  127.1 0.0 copy-start.5
  127.1 0.0 copy-start.7
  127.1 5.5 %copy.81 = bf16[32,8,64,128]{3,2,1,0:T(8,128)(2,1)} copy(bf16[32,8,64,128]{3,1,2,0:T(8,128)(2,1)} %bitcast.152) | data formatting | bytes 8388608
  132.6 1.2 multiply_reduce_fusion.3
  133.8 1.1 convert_convert_fusion
  134.9 4.0 %multiply_reduce_fusion.2 = bf16[128,8,32]{0,2,1:T(8,128)(2,1)S(1)} fusion(f32[128,8,64]{0,2,1:T(8,128)S(1)} %get-tuple-element.46, bf16[64,128,8,32]{1,0,3,2:T(8,128)(2,1)} %bitcast.145), kind=kLoop, calls=%fused_computation.13 | loop fusion | flops 6258688 | bytes 4521984 | tf_op jit(solution)/shard_map/while/body/eval_jaxpr/kah,kahd->ahd/dot_general | solution.py:61
  138.9 0.3 multiply_reduce_fusion.4
  139.2 0.0 copy-start.8
  139.3 0.2 convolution_convert_fusion.5
  139.5 0.2 fusion.14
  139.7 0.1 copy.40
  139.9 3.4 multiply_reduce_fusion.1
  143.3 1.1 broadcast_multiply_fusion
  144.4 22.6 %copy.94 = f32[32,8,64,128]{3,1,2,0:T(8,128)} copy(f32[32,8,64,128]{3,2,1,0:T(8,128)S(1)} %bitcast.147) | data formatting | bytes 16777216
  167.0 0.0 copy-done.8
  167.0 9.0 %copy.42 = f32[8192,256]{1,0:T(8,128)} copy(f32[8192,256]{0,1:T(8,128)} %bitcast.149) | data formatting | bytes 16777216 | tf_op jit(solution)/shard_map/while/body/eval_jaxpr/mul | solution.py:91
  176.0 44.7 %scatter_custom_fusion.1 = f32[192,256]{1,0:T(8,128)S(1)} fusion(s32[8192]{0:T(1024)S(1)} %bitcast.161, f32[8192,256]{1,0:T(8,128)} %copy.42, f32[]{:T(128)} %constant.16.clone.1), kind=kCustom, calls=%fused_computation.69 | custom fusion | flops 2097152 | bytes 197120 | tf_op jit(solution)/shard_map/while/body/eval_jaxpr/scatter-add | solution.py:95
  220.7 0.2 bitcast_convert_fusion
  221.0 1.2 multiply_multiply_fusion
  222.2 10.9 %copy.95 = f32[32,8,64,128]{3,1,2,0:T(8,128)} copy(f32[32,8,64,128]{3,2,1,0:T(8,128)S(1)} %bitcast.148) | data formatting | bytes 16777216
  233.1 9.0 %copy.41 = f32[8192,256]{1,0:T(8,128)} copy(f32[8192,256]{0,1:T(8,128)} %bitcast.150) | data formatting | bytes 16777216 | tf_op jit(solution)/shard_map/while/body/eval_jaxpr/mul | solution.py:86
  242.1 44.9 %scatter_custom_fusion = f32[192,256]{1,0:T(8,128)S(1)} fusion(s32[8192]{0:T(1024)S(1)} %bitcast.162, f32[8192,256]{1,0:T(8,128)} %copy.41, f32[]{:T(128)} %constant.16.clone.1), kind=kCustom, calls=%fused_computation.71 | custom fusion | flops 2097152 | bytes 197120 | tf_op jit(solution)/shard_map/while/body/eval_jaxpr/scatter-add | solution.py:94
  287.0 4.0 %multiply_reduce_fusion = f32[128,8,32]{0,2,1:T(8,128)S(1)} fusion(f32[128,8,64]{0,2,1:T(8,128)S(1)} %get-tuple-element.50, bf16[64,128,8,32]{1,0,3,2:T(8,128)(2,1)} %bitcast.143), kind=kLoop, calls=%fused_computation.11 | loop fusion | flops 6258688 | bytes 4587520 | tf_op jit(solution)/shard_map/while/body/eval_jaxpr/kah,kahd->ahd/dot_general | solution.py:81
  291.0 0.6 pad_maximum_fusion.4
  291.7 3.3 all-to-all-start.1
  295.0 0.0 reduce-scatter.2.cloned.1.call-start
  295.1 0.2 fusion.11
  295.3 0.2 copy.46
  295.5 3.6 all-to-all-done.1
  299.1 0.1 copy.47
  299.2 2.9 scatter_fusion
  302.1 0.1 convert_element_type.100
  302.2 0.2 fusion.55
  302.4 0.2 fusion.12
  302.6 0.2 fusion.13
  302.8 0.9 pad_maximum_fusion
  303.7 0.0 reduce-scatter.2.cloned.1.call-update
  303.7 51.8 %reduce-scatter.2.cloned.1.call-done = bf16[4,16,256]{2,1,0:T(8,128)(2,1)} async-done(((bf16[4,256,256]{2,1,0:T(8,128)(2,1)}), bf16[4,16,256]{2,1,0:T(8,128)(2,1)}) %reduce-scatter.2.cloned.1.call-update) | async-done | bytes 32784 | tf_op jit(solution)/shard_map/reduce_scatter | solution.py:198
  355.5 8.9 %psum.8 = bf16[4,16,256]{2,1,0:T(8,128)(2,1)S(1)} all-reduce(bf16[4,16,256]{2,1,0:T(8,128)(2,1)} %reduce-scatter.2.cloned.1.call-done), channel_id=1, replica_groups=mesh['cell'=16,'brick'=2] {'brick'}, use_global_device_ids=true, to_apply=%region_8.9 | all-reduce | flops 16384 | bytes 65536 | tf_op jit(solution)/shard_map/psum | solution.py:197
  364.5 0.0 copy-done.3
  364.5 0.0 copy-done.4
  364.5 0.7 add_divide_fusion.1
  365.2 0.0 copy-done.1
  (26 shorter events, 0.2 us)
Async XLA Ops:
  7.2 0.8 copy-start
  11.2 31.3 %all-to-all-start = ((bf16[2,32,256]{2,1,0:T(8,128)(2,1)}), bf16[2,32,256]{2,1,0:T(8,128)(2,1)S(1)}, u32[]{:S(2)}, u32[]{:S(2)}) async-start(bf16[2,32,256]{2,1,0:T(8,128)(2,1)} %bitcast.13), calls=%async_computation | async-start | bytes 65536 | tf_op jit(solution)/shard_map/all_to_all | solution.py:153
  127.1 5.6 %copy-start.2 = (bf16[32,8,64,128]{3,2,1,0:T(8,128)(2,1)S(1)}, bf16[32,8,64,128]{3,2,1,0:T(8,128)(2,1)}, u32[]{:S(2)}) copy-start(bf16[32,8,64,128]{3,2,1,0:T(8,128)(2,1)} %copy.80) | copy-start | bytes 12582916
  127.1 6.7 %copy-start.6 = (f32[8]{0:T(128)S(1)}, f32[8]{0:T(128)}, u32[]{:S(2)}) copy-start(f32[8]{0:T(128)} %param.21) | copy-start | bytes 100
  127.1 11.8 %copy-start.5 = (f32[256]{0:T(256)S(1)}, f32[256]{0:T(256)}, u32[]{:S(2)}) copy-start(f32[256]{0:T(256)} %param.23) | copy-start | bytes 3076
  127.1 12.1 %copy-start.7 = (f32[1,1,128]{2,1,0:T(1,128)S(1)}, f32[1,1,128]{2,1,0:T(1,128)}, u32[]{:S(2)}) copy-start(f32[1,1,128]{2,1,0:T(1,128)} %param.24) | copy-start | bytes 1540
  139.2 27.8 %copy-start.8 = (f32[128]{0:T(128)}, f32[128]{0:T(128)S(1)}, u32[]{:S(2)}) copy-start(f32[128]{0:T(128)S(1)} %get-tuple-element.78) | copy-start | bytes 1540
  233.1 132.1 %copy-start.1 = (bf16[4,256]{1,0:T(4,128)(2,1)S(1)}, bf16[4,256]{1,0:T(4,128)(2,1)}, u32[]{:S(2)}) copy-start(bf16[4,256]{1,0:T(4,128)(2,1)} %param.16) | copy-start | bytes 6148
  242.1 122.4 %copy-start.3 = (f32[4,16,256]{2,1,0:T(8,128)S(1)}, f32[4,16,256]{2,1,0:T(8,128)}, u32[]{:S(2)}) copy-start(f32[4,16,256]{2,1,0:T(8,128)} %param.27) | copy-start | bytes 196612
  242.1 122.4 %copy-start.4 = (f32[4,16,256]{2,1,0:T(8,128)S(1)}, f32[4,16,256]{2,1,0:T(8,128)}, u32[]{:S(2)}) copy-start(f32[4,16,256]{2,1,0:T(8,128)} %param.26) | copy-start | bytes 196612
  291.7 7.4 %all-to-all-start.1 = ((bf16[2,2,32,256]{3,2,0,1:T(8,128)(2,1)}), bf16[2,2,32,256]{3,2,0,1:T(8,128)(2,1)S(1)}, u32[]{:S(2)}, u32[]{:S(2)}) async-start(bf16[2,2,32,256]{3,2,0,1:T(8,128)(2,1)} %pad_maximum_fusion.4), calls=%async_computation.1 | async-start | bytes 131072 | tf_op jit(solution)/shard_map/all_to_all | solution.py:179
  295.0 60.6 %reduce-scatter.2.cloned.1.call-start = ((), (), s32[]{:S(2)}) async-start(), calls=%async_computation.3 | async-start | bytes 557056 | tf_op jit(solution)/shard_map/reduce_scatter | solution.py:198
Sparse Core Ops, SparseCore 0:
  303.8 51.6 reduce-scatter.1
where the time goes:
time: 371 us; the launch traced here: 372 us
  local copies, waits for them, and re-layouts  144 us (39%)
  other arithmetic  115 us (31%)
  waiting for transfers between devices  55.5 us (15%)
  blocking collectives  32.6 us (9%)
  between operations  14.7 us (4%)
  starting transfers between devices  7.54 us (2%)
    reduce_scatter x1, waiting for transfers between devices, body(): lax.psum_scatter(summed, 'cell', scatter_dimension=1, tiled=True)  51.8 us
    scatter-add x1, other arithmetic, tile_step(): key_grads.at[flattened_rows].add(key_edge.reshape(-1, model_width))  44.9 us
    scatter-add x1, other arithmetic, tile_step(): value_grads.at[flattened_rows].add(value_edge.reshape(-1, model_width))  44.7 us
    unnamed x22, local copies, waits for them, and re-layouts  44.4 us
    gather x2, local copies, waits for them, and re-layouts, tile_step(): value_table[neighbour_rows].reshape(slot_count, TILE, head_count, head_size)  39.7 us
    gather x2, local copies, waits for them, and re-layouts, tile_step(): key_table[neighbour_rows].reshape(slot_count, TILE, head_count, head_size)  39.3 us
    all_gather x1, blocking collectives, body(): lax.all_gather(master.astype(jnp.bfloat16), 'cell', axis=1, tiled=True)  23.6 us
    mul x1, local copies, waits for them, and re-layouts, tile_step(): grad_score.astype(jnp.float32)[..., None]  9.02 us
  transfers between devices with their start and end apart: 3, of which 2 were waited for; matrix products, arithmetic and copies ran while one was open for 1% of the time, Pallas kernels for 0%

commit v1 on v0

v1 whole, which is shorter than its diff:
```python
import functools
import math

import jax
import jax.numpy as jnp
from jax import lax
from jax.experimental import pallas as pl
from jax.experimental.pallas import tpu as pltpu
from jax.sharding import PartitionSpec as P

LANES = 128
FAR = 1e30

loss_weight = 0.0625
epsilon_norm = 1e-06

F32 = jnp.float32
BF16 = jnp.bfloat16
NT = (((1,), (1,)), ((), ()))
TN = (((0,), (0,)), ((), ()))


def dot(a, b):
    return jnp.dot(a, b, preferred_element_type=F32)


def dot_nt(a, b):
    return lax.dot_general(a, b, NT, preferred_element_type=F32)


def dot_tn(a, b):
    return lax.dot_general(a, b, TN, preferred_element_type=F32)


def lane_gather(table, index):
    return jnp.take_along_axis(table, index, axis=1, mode="promise_in_bounds")


def to_column(row):
    n = row.shape[1]
    eye = lax.broadcasted_iota(jnp.int32, (n, n), 0) == lax.broadcasted_iota(jnp.int32, (n, n), 1)
    return jnp.sum(jnp.where(eye, row, jnp.zeros_like(row)), axis=1, keepdims=True)


def to_row(column):
    n = column.shape[0]
    eye = lax.broadcasted_iota(jnp.int32, (n, n), 0) == lax.broadcasted_iota(jnp.int32, (n, n), 1)
    return jnp.sum(jnp.where(eye, column, jnp.zeros_like(column)), axis=0, keepdims=True)


def embed_kernel(features, species, species_table, norm_gain, send_rows, embedded, normed, parcel):
    atoms = features.shape[0]
    kinds = species_table.shape[0]
    column = to_column(species[...])
    total = features[...].astype(F32)
    picked = jnp.zeros_like(total)
    for kind in range(kinds):
        row = species_table[kind : kind + 1, :].astype(F32)
        picked = jnp.where(column == kind, row, picked)
    total = total + picked
    embedded[...] = total
    scale = lax.rsqrt(jnp.mean(total * total, axis=-1, keepdims=True) + epsilon_norm)
    norm = (total * scale * norm_gain[...]).astype(BF16)
    normed[...] = norm
    bricks, slots = send_rows.shape
    for brick in range(bricks):
        chosen = send_rows[brick : brick + 1, :]
        picks = (lax.broadcasted_iota(jnp.int32, (atoms, slots), 0) == chosen).astype(F32).astype(BF16)
        parcel[brick] = dot_tn(picks, norm).astype(BF16)


def index_kernel(neighbours, counts, distances, rows, far, pointers, inverse, rounds):
    slots, atoms = neighbours.shape
    none = LANES - 1
    blocks = inverse.shape[0]
    slot = lax.broadcasted_iota(jnp.int32, (slots, atoms), 0)
    valid = slot < counts[...]
    own = neighbours[...]
    held = jnp.where(valid, own, -1 - slot)
    back = jnp.full((slots, atoms), none, jnp.int32)
    table_row = lax.broadcasted_iota(jnp.int32, (blocks * LANES, atoms), 0)
    last = jnp.full((blocks * LANES, atoms), none, jnp.int32)
    for j in range(slots):
        row = held[j : j + 1, :]
        back = jnp.where((held == row) & (slot > j), j, back)
        last = jnp.where(table_row == row, j, last)

    def turned(array, fill):
        padded = jnp.concatenate([array, jnp.full((LANES - slots, atoms), fill, array.dtype)], axis=0)
        return padded.T

    rows[...] = turned(own, 0)
    far[...] = turned(jnp.where(valid, distances[...], FAR), FAR)
    pointer = turned(back, none)
    steps = jnp.int32(0)
    for k in range(pointers.shape[0]):
        pointers[k] = pointer
        steps += (jnp.min(pointer) < none).astype(jnp.int32)
        if k + 1 < pointers.shape[0]:
            pointer = lane_gather(pointer, pointer)
    rounds[0] = steps
    for block in range(blocks):
        inverse[block] = last[block * LANES : (block + 1) * LANES].T


def gathered(dense, index, blocks, rows):
    result = lane_gather(dense[:, :LANES], index)
    for block in range(1, blocks):
        part = lane_gather(dense[:, block * LANES : (block + 1) * LANES], index)
        result = jnp.where(rows >= block * LANES, part, result)
    return result


def sweep_kernel(
    rounds,
    decay,
    weights,
    normed,
    ghosts,
    embedded,
    rows,
    far,
    pointers,
    inverse,
    readout,
    targets,
    energies,
    grads,
    slot_ref,
    att_ref,
    dense_ref,
    score_ref,
    *,
    table_rows,
):
    atoms, width = normed.shape
    heads = decay.shape[0]
    head_size = width // heads
    blocks = inverse.shape[0]
    padded = blocks * LANES
    scale = 1.0 / math.sqrt(head_size)
    head_of = lax.broadcasted_iota(jnp.int32, (atoms, width), 1) // head_size

    def stacked(array):
        zero = jnp.zeros_like(array)
        return jnp.concatenate([jnp.where(head_of == h, array, zero) for h in range(heads)], axis=0)

    def own_lanes(wide):
        result = wide[:atoms]
        for h in range(1, heads):
            result = jnp.where(head_of == h, wide[h * atoms : (h + 1) * atoms], result)
        return result

    def merge_duplicates():
        def step(k, carry):
            pointer = pointers[k]
            for h in range(heads):
                part = slot_ref[pl.ds(h * atoms, atoms), :]
                slot_ref[pl.ds(h * atoms, atoms), :] = part + lane_gather(part, pointer)
            return carry

        lax.fori_loop(0, rounds[0], step, 0)

    def to_table():
        for h in range(heads):
            part = slot_ref[pl.ds(h * atoms, atoms), :]
            for block in range(blocks):
                value = lane_gather(part, inverse[block])
                high = value.astype(BF16)
                at = (pl.ds(h * atoms, atoms), pl.ds(block * LANES, LANES))
                dense_ref[0, at[0], at[1]] = high
                dense_ref[1, at[0], at[1]] = (value - high.astype(F32)).astype(BF16)
        return dense_ref[0], dense_ref[1]

    norm = normed[...]
    pieces = [norm, ghosts[...]]
    if padded > table_rows:
        pieces.append(jnp.zeros((padded - table_rows, width), BF16))
    table = jnp.concatenate(pieces, axis=0)
    query = dot(norm, weights[0]).astype(BF16)
    keys = dot(table, weights[1]).astype(BF16)
    values = dot(table, weights[2]).astype(BF16)

    row_ids = rows[...]
    index = jnp.bitwise_and(row_ids, LANES - 1)
    away = far[...]
    query_stack = stacked(query)
    score_ref[...] = dot_nt(query_stack, keys)
    for h in range(heads):
        at = pl.ds(h * atoms, atoms)
        score = gathered(score_ref[at, :], index, blocks, row_ids) * scale - decay[h] * away
        terms = jnp.exp(score - jnp.max(score, axis=1, keepdims=True))
        attention = terms / jnp.sum(terms, axis=1, keepdims=True)
        att_ref[at, :] = attention
        slot_ref[at, :] = attention.astype(BF16).astype(F32)
    merge_duplicates()
    high, low = to_table()
    attended = own_lanes(dot(high, values) + dot(low, values)).astype(BF16)

    out_proj = weights[3]
    updated = embedded[...] + dot(attended, out_proj)
    sigmoid = 1.0 / (1.0 + jnp.exp(-updated))
    energy = jnp.sum(readout[...] * (updated * sigmoid), axis=1, keepdims=True)
    energies[...] = to_row(energy)
    grad_energy = loss_weight * (energy - to_column(targets[...]))
    slope = sigmoid * (1.0 + updated * (1.0 - sigmoid))
    grad_updated = (grad_energy * readout[...] * slope).astype(BF16)
    grads[3] = dot_tn(attended, grad_updated)
    grad_attended = dot_nt(grad_updated, out_proj).astype(BF16)

    attended_stack = stacked(grad_attended)
    value_grads = dot_tn(high, attended_stack) + dot_tn(low, attended_stack)
    grads[2] = dot_tn(table, value_grads.astype(BF16))
    score_ref[...] = dot_nt(attended_stack, values)
    for h in range(heads):
        at = pl.ds(h * atoms, atoms)
        grad_weights = gathered(score_ref[at, :], index, blocks, row_ids)
        attention = att_ref[at, :]
        mean = jnp.sum(attention * grad_weights, axis=1, keepdims=True)
        slot_ref[at, :] = (attention * (grad_weights - mean)).astype(BF16).astype(F32)
    merge_duplicates()
    high, low = to_table()
    grad_query = own_lanes(dot(high, keys) + dot(low, keys)) * scale
    grads[0] = dot_tn(norm, grad_query.astype(BF16))
    key_grads = (dot_tn(high, query_stack) + dot_tn(low, query_stack)) * scale
    grads[1] = dot_tn(table, key_grads.astype(BF16))


def vmem(count):
    return [pl.BlockSpec(memory_space=pltpu.VMEM)] * count


SMEM = pl.BlockSpec(memory_space=pltpu.SMEM)


def struct(shape, dtype):
    return jax.ShapeDtypeStruct(shape, dtype)


def flips(size, offset):
    return [(i, i ^ offset) for i in range(size)]


def halvings(size):
    offsets = []
    offset = size // 2
    while offset:
        offsets.append(offset)
        offset //= 2
    return offsets


def gather_cells(shard, cells):
    place = lax.axis_index("cell")
    offsets = halvings(cells)
    held = shard[None]
    for offset in offsets:
        other = lax.ppermute(held, "cell", flips(cells, offset))
        first = (place // offset) % 2 == 0
        held = jnp.where(first, jnp.concatenate([held, other]), jnp.concatenate([other, held]))
    bits = len(offsets)
    matrices, rows, width = shard.shape
    held = held.reshape((2,) * bits + shard.shape)
    held = held.transpose((bits,) + tuple(reversed(range(bits))) + (bits + 1, bits + 2))
    return held.reshape(matrices, cells * rows, width)


def reduce_cells(parts, cells):
    place = lax.axis_index("cell")
    tail = parts.shape[1:]
    for offset in reversed(halvings(cells)):
        bit = (place // offset) % 2
        pairs = parts.reshape((-1, 2) + tail)
        keep = lax.dynamic_index_in_dim(pairs, bit, 1, False)
        send = lax.dynamic_index_in_dim(pairs, 1 - bit, 1, False)
        parts = keep + lax.ppermute(send.astype(BF16), "cell", flips(cells, offset)).astype(F32)
    return parts[0]


def reduce_bricks(total, bricks):
    for offset in halvings(bricks):
        mine = total.astype(BF16)
        total = mine.astype(F32) + lax.ppermute(mine, "brick", flips(bricks, offset)).astype(F32)
    return total


def body(
    cells,
    bricks,
    features,
    species,
    species_table,
    neighbours,
    counts,
    send_lists,
    distances,
    head_decay,
    norm_gain,
    readout,
    targets,
    master,
    moment,
    second,
):
    atoms, width = features.shape[2:]
    slots = neighbours.shape[2]
    ghost_slots = send_lists.shape[3]
    heads = head_decay.shape[0]
    table_rows = atoms + bricks * ghost_slots
    blocks = -(-table_rows // LANES)
    levels = max(1, math.ceil(math.log2(slots)))

    weights = gather_cells(master.astype(BF16), cells)

    embedded, normed, parcel = pl.pallas_call(
        embed_kernel,
        out_shape=(
            struct((atoms, width), F32),
            struct((atoms, width), BF16),
            struct((bricks, ghost_slots, width), BF16),
        ),
        in_specs=vmem(5),
        out_specs=tuple(vmem(3)),
        name="embed",
    )(features[0, 0], species[0], species_table, norm_gain[None], send_lists[0, 0])

    brick = lax.axis_index("brick")
    ghosts = parcel
    for offset in range(1, bricks):
        peer = brick ^ offset
        sent = lax.dynamic_index_in_dim(parcel, peer, 0, True)
        arrived = lax.ppermute(sent, "brick", flips(bricks, offset))
        ghosts = lax.dynamic_update_slice_in_dim(ghosts, arrived, peer, 0)
    ghosts = ghosts.reshape(bricks * ghost_slots, width)

    rows, far, pointers, inverse, rounds = pl.pallas_call(
        index_kernel,
        out_shape=(
            struct((atoms, LANES), jnp.int32),
            struct((atoms, LANES), F32),
            struct((levels, atoms, LANES), jnp.int32),
            struct((blocks, atoms, LANES), jnp.int32),
            struct((1,), jnp.int32),
        ),
        in_specs=vmem(3),
        out_specs=tuple(vmem(4)) + (SMEM,),
        name="index",
    )(neighbours[0, 0], counts[0], distances[0, 0])

    energies, grads = pl.pallas_call(
        functools.partial(sweep_kernel, table_rows=table_rows),
        out_shape=(struct((1, atoms), F32), struct((4, width, width), F32)),
        in_specs=[SMEM, SMEM] + vmem(10),
        out_specs=tuple(vmem(2)),
        scratch_shapes=[
            pltpu.VMEM((heads * atoms, LANES), F32),
            pltpu.VMEM((heads * atoms, LANES), F32),
            pltpu.VMEM((2, heads * atoms, blocks * LANES), BF16),
            pltpu.VMEM((heads * atoms, blocks * LANES), F32),
        ],
        compiler_params=pltpu.CompilerParams(vmem_limit_bytes=32 * 1024 * 1024),
        name="sweep",
    )(
        rounds,
        head_decay,
        weights,
        normed,
        ghosts,
        embedded,
        rows,
        far,
        pointers,
        inverse,
        readout[None],
        targets[0],
    )

    parts = grads.reshape(4, cells, width // cells, width).transpose(1, 0, 2, 3)
    owned = reduce_bricks(reduce_cells(parts, cells), bricks)
    moment_new = 0.9 * moment + 0.1 * owned
    second_new = 0.999 * second + 0.001 * owned * owned
    adam_step = moment_new / (jnp.sqrt(second_new) + 1e-08)
    return (energies[None], moment_new, second_new, adam_step)


def solution(mesh):
    return jax.shard_map(
        functools.partial(body, mesh.shape["cell"], mesh.shape["brick"]),
        mesh=mesh,
        in_specs=(
            P("cell", "brick", None, None),
            P("cell", "brick", None),
            P(),
            P("cell", "brick", None, None),
            P("cell", "brick", None),
            P("cell", "brick", None, None),
            P("cell", "brick", None, None),
            P(),
            P(),
            P(),
            P("cell", "brick", None),
            P(None, "cell", None),
            P(None, "cell", None),
            P(None, "cell", None),
        ),
        out_specs=(
            P("cell", "brick", None),
            P(None, "cell", None),
            P(None, "cell", None),
            P(None, "cell", None),
        ),
        check_vma=False,
    )
```

time: 371 us -> 61.1 us (0.16)
  local copies, waits for them, and re-layouts: 144 us -> 1.95 us
  other arithmetic: 115 us -> 1.81 us
  blocking collectives: 32.6 us -> 0 us
  waiting for transfers between devices: 55.5 us -> 24.6 us
  Pallas kernels: 0 us -> 17.4 us
  between operations: 14.7 us -> 0.89 us
  starting transfers between devices: 7.54 us -> 14.1 us
    scatter-add x3 -> x0, other arithmetic: 92.4 us -> none  [the longest x1 44.9 us: tile_step(): key_grads.at[flattened_rows].add(key_edge.reshape(-1, model_width))]
    gather x5 -> x0, local copies, waits for them, and re-layouts: 80.3 us -> none  [the longest x2 39.7 us: tile_step(): value_table[neighbour_rows].reshape(slot_count, TILE, head_count, head_size)]
    reduce_scatter x1 -> x0, waiting for transfers between devices: 51.8 us -> none  [body(): lax.psum_scatter(summed, 'cell', scatter_dimension=1, tiled=True)]
    unnamed x22 -> x24, local copies, waits for them, and re-layouts: 44.4 us -> 0.98 us
    ppermute x0 -> x10, waiting for transfers between devices: none -> 24.6 us  [the longest x4 12.5 us: reduce_cells(): lax.ppermute(send.astype(BF16), 'cell', flips(cells, offset)).astype(F32)]
    all_gather x1 -> x0, blocking collectives: 23.6 us -> none  [body(): lax.all_gather(master.astype(jnp.bfloat16), 'cell', axis=1, tiled=True)]
    mul x2 -> x0, local copies, waits for them, and re-layouts: 18 us -> none  [the longest x1 9.02 us: tile_step(): grad_score.astype(jnp.float32)[..., None]]
    pallas_call x0 -> x3, Pallas kernels: none -> 17.4 us  [the longest x1 12.7 us: body(): pl.pallas_call(functools.partial(sweep_kernel, table_rows=table_rows), ou...]
  transfers between devices with their start and end apart: 3 -> 10, of which waited for: 2 -> 8; matrix products, arithmetic and copies ran while one was open for 1% -> 1% of each run, Pallas kernels for 0% -> 8%
where the time goes in v1:
time: 61.1 us; the launch traced here: 60.8 us
  waiting for transfers between devices  24.6 us (40%)
  Pallas kernels  17.4 us (28%)
  starting transfers between devices  14.1 us (23%)
  local copies, waits for them, and re-layouts  1.95 us (3%)
  other arithmetic  1.81 us (3%)
  between operations  0.89 us (1%)
    pallas_call x1, Pallas kernels, body(): pl.pallas_call(functools.partial(sweep_kernel, table_rows=table_rows), ou...  12.7 us
    ppermute x4, waiting for transfers between devices, reduce_cells(): lax.ppermute(send.astype(BF16), 'cell', flips(cells, offset)).astype(F32)  12.5 us
    ppermute x4, waiting for transfers between devices, gather_cells(): other = lax.ppermute(held, 'cell', flips(cells, offset))  8.19 us
    ppermute x4, starting transfers between devices, gather_cells(): other = lax.ppermute(held, 'cell', flips(cells, offset))  7.53 us
    ppermute x4, starting transfers between devices, reduce_cells(): lax.ppermute(send.astype(BF16), 'cell', flips(cells, offset)).astype(F32)  4.81 us
    ppermute x1, waiting for transfers between devices, reduce_bricks(): lax.ppermute(mine, 'brick', flips(bricks, offset)).astype(F32)  3.9 us
    pallas_call x1, Pallas kernels, body(): pl.pallas_call(index_kernel, out_shape=(struct((atoms, LANES), jnp.int32)...  2.91 us
    pallas_call x1, Pallas kernels, body(): pl.pallas_call(embed_kernel, out_shape=(struct((atoms, width), F32), stru...  1.83 us
  transfers between devices with their start and end apart: 10, of which 8 were waited for; matrix products, arithmetic and copies ran while one was open for 1% of the time, Pallas kernels for 8%

profile of v1, /device:TPU:0, one launch (start us, length us, event | category | flops | bytes accessed | tf_op | source)
XLA Modules:
  0.0 60.8 jit_solution(15461404699613678467)
XLA Ops:
  0.6 0.8 %convert_bitcast_fusion = bf16[1,4,16,256]{3,2,1,0:T(8,128)(2,1)S(1)} fusion(f32[4,16,256]{2,1,0:T(8,128)} %param.25), kind=kLoop, calls=%fused_computation.21 | loop fusion | flops 16384 | bytes 98304 | tf_op jit(solution)/shard_map/broadcast_in_dim | solution.py:256
  1.5 4.0 %collective-permute-start = (bf16[1,4,16,256]{3,2,1,0:T(8,128)(2,1)S(1)}, bf16[1,4,16,256]{3,2,1,0:T(8,128)(2,1)S(1)}, u32[]{:S(2)}, u32[]{:S(2)}) collective-permute-start(bf16[1,4,16,256]{3,2,1,0:T(8,128)(2,1)S(1)} %convert_bitcast_fusion), channel_id=1, source_target_pairs={{0,16},{2,18},{4,20},{6,22},{8,24},{10,26},{12,28},{14,30},{16,0},... | collective-permute-start | bytes 98312 | tf_op jit(solution)/shard_map/ppermute | solution.py:258
  5.5 2.2 %collective-permute-done = bf16[1,4,16,256]{3,2,1,0:T(8,128)(2,1)S(1)} collective-permute-done((bf16[1,4,16,256]{3,2,1,0:T(8,128)(2,1)S(1)}, bf16[1,4,16,256]{3,2,1,0:T(8,128)(2,1)S(1)}, u32[]{:S(2)}, u32[]{:S(2)}) %collective-permute-start) | collective-permute-done | bytes 32800 | tf_op jit(solution)/shard_map/ppermute | solution.py:258
  7.8 1.6 %collective-permute-start.1 = (bf16[2,4,16,256]{3,2,1,0:T(8,128)(2,1)S(1)}, bf16[2,4,16,256]{3,2,1,0:T(8,128)(2,1)S(1)}, u32[]{:S(2)}, u32[]{:S(2)}) collective-permute-start(bf16[2,4,16,256]{3,2,1,0:T(8,128)(2,1)S(1)} %maximum_select_fusion.3), channel_id=1, source_target_pairs={{0,8},{2,10},{4,12},{6,14},{8,0},{10,2},{12,4},{14,6},{16,24},{18,... | collective-permute-start | bytes 196616 | tf_op jit(solution)/shard_map/ppermute | solution.py:258
  9.4 2.7 %collective-permute-done.1 = bf16[2,4,16,256]{3,2,1,0:T(8,128)(2,1)S(1)} collective-permute-done((bf16[2,4,16,256]{3,2,1,0:T(8,128)(2,1)S(1)}, bf16[2,4,16,256]{3,2,1,0:T(8,128)(2,1)S(1)}, u32[]{:S(2)}, u32[]{:S(2)}) %collective-permute-start.1) | collective-permute-done | bytes 65568 | tf_op jit(solution)/shard_map/ppermute | solution.py:258
  12.1 1.8 %collective-permute-start.2 = (bf16[4,4,16,256]{3,2,1,0:T(8,128)(2,1)S(1)}, bf16[4,4,16,256]{3,2,1,0:T(8,128)(2,1)S(1)}, u32[]{:S(2)}, u32[]{:S(2)}) collective-permute-start(bf16[4,4,16,256]{3,2,1,0:T(8,128)(2,1)S(1)} %maximum_select_fusion.2), channel_id=1, source_target_pairs={{0,4},{2,6},{4,0},{6,2},{8,12},{10,14},{12,8},{14,10},{16,20},{18,... | collective-permute-start | bytes 393224 | tf_op jit(solution)/shard_map/ppermute | solution.py:258
  13.9 3.2 %collective-permute-done.2 = bf16[4,4,16,256]{3,2,1,0:T(8,128)(2,1)S(1)} collective-permute-done((bf16[4,4,16,256]{3,2,1,0:T(8,128)(2,1)S(1)}, bf16[4,4,16,256]{3,2,1,0:T(8,128)(2,1)S(1)}, u32[]{:S(2)}, u32[]{:S(2)}) %collective-permute-start.2) | collective-permute-done | bytes 131104 | tf_op jit(solution)/shard_map/ppermute | solution.py:258
  17.2 0.1 collective-permute-start.3
  17.3 1.8 %embed.1 = (f32[128,256]{1,0:T(8,128)}, bf16[128,256]{1,0:T(8,128)(2,1)}, bf16[2,32,256]{2,1,0:T(8,128)(2,1)}) custom-call(bf16[128,256]{1,0:T(8,128)(2,1)} %bitcast.49, s32[1,128]{1,0:T(1,128)} %bitcast.54, bf16[4,256]{1,0:T(4,128)(2,1)} %species_table.1, f32[1,256]{1,0:T(1,128)} %bitcast.52, s32[2,32]{1,0:T(2,128)} %bitcast.53), custom_call_target="tpu_custom_call" | custom-call | tf_op jit(solution)/shard_map/embed/pallas_call | solution.py:315
  19.1 0.7 %constant_dynamic-slice_fusion = bf16[1,32,256]{2,1,0:T(8,128)(2,1)S(1)} fusion(bf16[2,32,256]{2,1,0:T(8,128)(2,1)} %get-tuple-element.16, s32[]{:T(128)S(6)} %select_n.127), kind=kLoop, calls=%fused_computation.23 | loop fusion | bytes 32772 | tf_op jit(solution)/shard_map/jit(dynamic_index_in_dim)/dynamic_slice | solution.py:331
  19.8 1.7 %collective-permute-start.4 = (bf16[1,32,256]{2,1,0:T(8,128)(2,1)S(1)}, bf16[1,32,256]{2,1,0:T(8,128)(2,1)S(1)}, u32[]{:S(2)}, u32[]{:S(2)}) collective-permute-start(bf16[1,32,256]{2,1,0:T(8,128)(2,1)S(1)} %constant_dynamic-slice_fusion), channel_id=1, source_target_pairs={{0,1},{1,0},{2,3},{3,2},{4,5},{5,4},{6,7},{7,6},{8,9},{9,8},{10,11... | collective-permute-start | bytes 49160 | tf_op jit(solution)/shard_map/ppermute | solution.py:332
  21.5 0.0 copy-start.3
  21.5 2.9 %index.1 = (s32[128,128]{1,0:T(8,128)}, f32[128,128]{1,0:T(8,128)}, s32[6,128,128]{2,1,0:T(8,128)}, s32[2,128,128]{2,1,0:T(8,128)}, s32[1]{0:T(128)}) custom-call(s32[64,128]{1,0:T(8,128)} %bitcast.50, s32[1,128]{1,0:T(1,128)} %bitcast.55, f32[64,128]{1,0:T(8,128)} %bitcast.51), custom_call_target="tpu_custom_call" | custom-call | tf_op jit(solution)/shard_map/index/pallas_call | solution.py:336
  24.4 0.0 collective-permute-done.4
  24.4 0.0 copy-done.3
  24.5 0.0 collective-permute-done.3
  24.5 0.1 maximum_select_fusion
  24.6 0.0 copy-start
  24.6 0.0 copy-start.1
  24.6 0.0 copy-start.2
  24.6 0.0 copy-start.4
  24.6 0.0 copy-start.5
  24.6 0.0 copy-start.6
  24.6 0.0 copy-start.9
  24.7 0.1 copy.21
  24.7 0.0 copy-start.7
  24.7 0.0 copy-start.8
  24.7 0.8 %copy-done = s32[6,128,128]{2,1,0:T(8,128)S(1)} copy-done((s32[6,128,128]{2,1,0:T(8,128)S(1)}, s32[6,128,128]{2,1,0:T(8,128)}, u32[]{:S(2)}) %copy-start) | copy-done | bytes 393240
  25.6 0.0 copy-done.1
  25.6 0.1 copy-done.2
  25.7 0.0 copy-done.4
  25.7 0.0 copy-done.5
  25.7 0.0 copy-done.6
  25.7 0.0 copy-done.9
  25.7 0.0 copy-done.7
  25.7 0.0 copy-done.8
  25.7 12.7 %sweep.1 = (f32[1,128]{1,0:T(1,128)}, f32[4,256,256]{2,1,0:T(8,128)S(1)}) custom-call(s32[1]{0:T(128)} %get-tuple-element.14.rounds, f32[8]{0:T(128)S(1)} %copy-done.8, bf16[4,256,256]{2,1,0:T(8,128)(2,1)S(1)} %bitcast.37, bf16[128,256]{1,0:T(8,128)(2,1)S(1)} %copy-done.4, bf16[64,256]{1,0:T(8,128)(2,1)S(1)} %bitcast.39, f32[128,256]{1,0:T(8,128)S(1)} %copy-done.1, ...), custom_call_target="tpu_custom_call" | custom-call | tf_op jit(solution)/shard_map/sweep/pallas_call | solution.py:350
  38.4 0.1 copy.22
  38.6 1.1 %collective-permute-start.5 = (bf16[8,4,16,256]{3,2,1,0:T(8,128)(2,1)S(1)}, bf16[8,4,16,256]{3,2,1,0:T(8,128)(2,1)S(1)}, u32[]{:S(2)}, u32[]{:S(2)}) collective-permute-start(bf16[8,4,16,256]{3,2,1,0:T(8,128)(2,1)S(1)} %fusion), channel_id=1, source_target_pairs={{0,2},{2,0},{4,6},{6,4},{8,10},{10,8},{12,14},{14,12},{16,18},{18,... | collective-permute-start | bytes 786440 | tf_op jit(solution)/shard_map/ppermute | solution.py:276
  39.7 1.2 %collective-permute-done.5 = bf16[8,4,16,256]{3,2,1,0:T(8,128)(2,1)S(1)} collective-permute-done((bf16[8,4,16,256]{3,2,1,0:T(8,128)(2,1)S(1)}, bf16[8,4,16,256]{3,2,1,0:T(8,128)(2,1)S(1)}, u32[]{:S(2)}, u32[]{:S(2)}) %collective-permute-start.5) | collective-permute-done | bytes 262176 | tf_op jit(solution)/shard_map/ppermute | solution.py:276
  40.8 0.1 bitcast_add_fusion
  41.0 0.9 %collective-permute-start.6 = (bf16[4,4,16,256]{3,2,1,0:T(8,128)(2,1)S(1)}, bf16[4,4,16,256]{3,2,1,0:T(8,128)(2,1)S(1)}, u32[]{:S(2)}, u32[]{:S(2)}) collective-permute-start(bf16[4,4,16,256]{3,2,1,0:T(8,128)(2,1)S(1)} %fusion.1), channel_id=1, source_target_pairs={{0,4},{2,6},{4,0},{6,2},{8,12},{10,14},{12,8},{14,10},{16,20},{18,... | collective-permute-start | bytes 393224 | tf_op jit(solution)/shard_map/ppermute | solution.py:276
  41.9 4.9 %collective-permute-done.6 = bf16[4,4,16,256]{3,2,1,0:T(8,128)(2,1)S(1)} collective-permute-done((bf16[4,4,16,256]{3,2,1,0:T(8,128)(2,1)S(1)}, bf16[4,4,16,256]{3,2,1,0:T(8,128)(2,1)S(1)}, u32[]{:S(2)}, u32[]{:S(2)}) %collective-permute-start.6) | collective-permute-done | bytes 131104 | tf_op jit(solution)/shard_map/ppermute | solution.py:276
  46.9 0.6 collective-permute-start.7
  47.4 3.8 %collective-permute-done.7 = bf16[2,4,16,256]{3,2,1,0:T(8,128)(2,1)S(1)} collective-permute-done((bf16[2,4,16,256]{3,2,1,0:T(8,128)(2,1)S(1)}, bf16[2,4,16,256]{3,2,1,0:T(8,128)(2,1)S(1)}, u32[]{:S(2)}, u32[]{:S(2)}) %collective-permute-start.7) | collective-permute-done | bytes 65568 | tf_op jit(solution)/shard_map/ppermute | solution.py:276
  51.2 2.2 %collective-permute-start.8 = (bf16[1,4,16,256]{3,2,1,0:T(8,128)(2,1)S(1)}, bf16[1,4,16,256]{3,2,1,0:T(8,128)(2,1)S(1)}, u32[]{:S(2)}, u32[]{:S(2)}) collective-permute-start(bf16[1,4,16,256]{3,2,1,0:T(8,128)(2,1)S(1)} %dynamic-slice_convert_fusion.3), channel_id=1, source_target_pairs={{0,16},{2,18},{4,20},{6,22},{8,24},{10,26},{12,28},{14,30},{16,0},... | collective-permute-start | bytes 98312 | tf_op jit(solution)/shard_map/ppermute | solution.py:276
  53.5 0.0 copy-start.10
  53.5 0.0 copy-start.11
  53.5 2.6 %collective-permute-done.8 = bf16[1,4,16,256]{3,2,1,0:T(8,128)(2,1)S(1)} collective-permute-done((bf16[1,4,16,256]{3,2,1,0:T(8,128)(2,1)S(1)}, bf16[1,4,16,256]{3,2,1,0:T(8,128)(2,1)S(1)}, u32[]{:S(2)}, u32[]{:S(2)}) %collective-permute-start.8) | collective-permute-done | bytes 32800 | tf_op jit(solution)/shard_map/ppermute | solution.py:276
  56.1 0.1 collective-permute-start.9
  56.2 3.9 %collective-permute-done.9 = bf16[4,16,256]{2,1,0:T(8,128)(2,1)S(1)} collective-permute-done((bf16[4,16,256]{2,1,0:T(8,128)(2,1)S(1)}, bf16[4,16,256]{2,1,0:T(8,128)(2,1)S(1)}, u32[]{:S(2)}, u32[]{:S(2)}) %collective-permute-start.9) | collective-permute-done | bytes 32800 | tf_op jit(solution)/shard_map/ppermute | solution.py:283
  60.1 0.0 copy-done.10
  60.1 0.0 copy-done.11
  60.1 0.7 %add_divide_fusion = (f32[4,16,256]{2,1,0:T(8,128)}, f32[4,16,256]{2,1,0:T(8,128)}, f32[4,16,256]{2,1,0:T(8,128)}) fusion(bf16[4,16,256]{2,1,0:T(8,128)(2,1)S(1)} %collective-permute-done.9, bf16[4,16,256]{2,1,0:T(8,128)(2,1)S(1)} %fusion.4, f32[4,16,256]{2,1,0:T(8,128)S(1)} %copy-done.10, f32[4,16,256]{2,1,0:T(8,128)S(1)} %copy-done.11), kind=kLoop, calls=%fused_computation.15 | loop fusion | flops 196608 | bytes 393216 | tf_op jit(solution)/shard_map/div | solution.py:382
  (11 shorter events, 0.2 us)
Async XLA Ops:
  1.5 6.3 %collective-permute-start = (bf16[1,4,16,256]{3,2,1,0:T(8,128)(2,1)S(1)}, bf16[1,4,16,256]{3,2,1,0:T(8,128)(2,1)S(1)}, u32[]{:S(2)}, u32[]{:S(2)}) collective-permute-start(bf16[1,4,16,256]{3,2,1,0:T(8,128)(2,1)S(1)} %convert_bitcast_fusion), channel_id=1, source_target_pairs={{0,16},{2,18},{4,20},{6,22},{8,24},{10,26},{12,28},{14,30},{16,0},... | collective-permute-start | bytes 98312 | tf_op jit(solution)/shard_map/ppermute | solution.py:258
  7.8 4.3 %collective-permute-start.1 = (bf16[2,4,16,256]{3,2,1,0:T(8,128)(2,1)S(1)}, bf16[2,4,16,256]{3,2,1,0:T(8,128)(2,1)S(1)}, u32[]{:S(2)}, u32[]{:S(2)}) collective-permute-start(bf16[2,4,16,256]{3,2,1,0:T(8,128)(2,1)S(1)} %maximum_select_fusion.3), channel_id=1, source_target_pairs={{0,8},{2,10},{4,12},{6,14},{8,0},{10,2},{12,4},{14,6},{16,24},{18,... | collective-permute-start | bytes 196616 | tf_op jit(solution)/shard_map/ppermute | solution.py:258
  12.1 5.0 %collective-permute-start.2 = (bf16[4,4,16,256]{3,2,1,0:T(8,128)(2,1)S(1)}, bf16[4,4,16,256]{3,2,1,0:T(8,128)(2,1)S(1)}, u32[]{:S(2)}, u32[]{:S(2)}) collective-permute-start(bf16[4,4,16,256]{3,2,1,0:T(8,128)(2,1)S(1)} %maximum_select_fusion.2), channel_id=1, source_target_pairs={{0,4},{2,6},{4,0},{6,2},{8,12},{10,14},{12,8},{14,10},{16,20},{18,... | collective-permute-start | bytes 393224 | tf_op jit(solution)/shard_map/ppermute | solution.py:258
  17.2 7.3 %collective-permute-start.3 = (bf16[8,4,16,256]{3,2,1,0:T(8,128)(2,1)S(1)}, bf16[8,4,16,256]{3,2,1,0:T(8,128)(2,1)S(1)}, u32[]{:S(2)}, u32[]{:S(2)}) collective-permute-start(bf16[8,4,16,256]{3,2,1,0:T(8,128)(2,1)S(1)} %maximum_select_fusion.1), channel_id=1, source_target_pairs={{0,2},{2,0},{4,6},{6,4},{8,10},{10,8},{12,14},{14,12},{16,18},{18,... | collective-permute-start | bytes 786440 | tf_op jit(solution)/shard_map/ppermute | solution.py:258
  19.8 4.6 %collective-permute-start.4 = (bf16[1,32,256]{2,1,0:T(8,128)(2,1)S(1)}, bf16[1,32,256]{2,1,0:T(8,128)(2,1)S(1)}, u32[]{:S(2)}, u32[]{:S(2)}) collective-permute-start(bf16[1,32,256]{2,1,0:T(8,128)(2,1)S(1)} %constant_dynamic-slice_fusion), channel_id=1, source_target_pairs={{0,1},{1,0},{2,3},{3,2},{4,5},{5,4},{6,7},{7,6},{8,9},{9,8},{10,11... | collective-permute-start | bytes 49160 | tf_op jit(solution)/shard_map/ppermute | solution.py:332
  21.5 2.9 %copy-start.3 = (bf16[2,32,256]{2,1,0:T(8,128)(2,1)S(1)}, bf16[2,32,256]{2,1,0:T(8,128)(2,1)}, u32[]{:S(2)}) copy-start(bf16[2,32,256]{2,1,0:T(8,128)(2,1)} %get-tuple-element.16) | copy-start | bytes 98308
  24.6 1.0 %copy-start = (s32[6,128,128]{2,1,0:T(8,128)S(1)}, s32[6,128,128]{2,1,0:T(8,128)}, u32[]{:S(2)}) copy-start(s32[6,128,128]{2,1,0:T(8,128)} %get-tuple-element.20.pointers) | copy-start | bytes 1179652
  24.6 1.0 %copy-start.1 = (f32[128,256]{1,0:T(8,128)S(1)}, f32[128,256]{1,0:T(8,128)}, u32[]{:S(2)}) copy-start(f32[128,256]{1,0:T(8,128)} %get-tuple-element.17.embedded) | copy-start | bytes 393220
  24.6 1.1 %copy-start.2 = (s32[2,128,128]{2,1,0:T(8,128)S(1)}, s32[2,128,128]{2,1,0:T(8,128)}, u32[]{:S(2)}) copy-start(s32[2,128,128]{2,1,0:T(8,128)} %get-tuple-element.21.inverse) | copy-start | bytes 393220
  24.6 1.1 %copy-start.4 = (bf16[128,256]{1,0:T(8,128)(2,1)S(1)}, bf16[128,256]{1,0:T(8,128)(2,1)}, u32[]{:S(2)}) copy-start(bf16[128,256]{1,0:T(8,128)(2,1)} %get-tuple-element.15.normed) | copy-start | bytes 196612
  24.6 1.1 %copy-start.5 = (s32[128,128]{1,0:T(8,128)S(1)}, s32[128,128]{1,0:T(8,128)}, u32[]{:S(2)}) copy-start(s32[128,128]{1,0:T(8,128)} %get-tuple-element.18.rows) | copy-start | bytes 196612
  24.6 1.0 %copy-start.6 = (f32[128,128]{1,0:T(8,128)S(1)}, f32[128,128]{1,0:T(8,128)}, u32[]{:S(2)}) copy-start(f32[128,128]{1,0:T(8,128)} %get-tuple-element.19.far) | copy-start | bytes 196612
  24.6 1.0 %copy-start.9 = (f32[1,1,128]{2,1,0:T(1,128)S(1)}, f32[1,1,128]{2,1,0:T(1,128)}, u32[]{:S(2)}) copy-start(f32[1,1,128]{2,1,0:T(1,128)} %param.24) | copy-start | bytes 1540
  24.7 1.0 %copy-start.7 = (f32[256]{0:T(256)S(1)}, f32[256]{0:T(256)}, u32[]{:S(2)}) copy-start(f32[256]{0:T(256)} %param.23) | copy-start | bytes 3076
  24.7 1.0 %copy-start.8 = (f32[8]{0:T(128)S(1)}, f32[8]{0:T(128)}, u32[]{:S(2)}) copy-start(f32[8]{0:T(128)} %decay.1) | copy-start | bytes 100
  38.6 2.3 %collective-permute-start.5 = (bf16[8,4,16,256]{3,2,1,0:T(8,128)(2,1)S(1)}, bf16[8,4,16,256]{3,2,1,0:T(8,128)(2,1)S(1)}, u32[]{:S(2)}, u32[]{:S(2)}) collective-permute-start(bf16[8,4,16,256]{3,2,1,0:T(8,128)(2,1)S(1)} %fusion), channel_id=1, source_target_pairs={{0,2},{2,0},{4,6},{6,4},{8,10},{10,8},{12,14},{14,12},{16,18},{18,... | collective-permute-start | bytes 786440 | tf_op jit(solution)/shard_map/ppermute | solution.py:276
  41.0 5.8 %collective-permute-start.6 = (bf16[4,4,16,256]{3,2,1,0:T(8,128)(2,1)S(1)}, bf16[4,4,16,256]{3,2,1,0:T(8,128)(2,1)S(1)}, u32[]{:S(2)}, u32[]{:S(2)}) collective-permute-start(bf16[4,4,16,256]{3,2,1,0:T(8,128)(2,1)S(1)} %fusion.1), channel_id=1, source_target_pairs={{0,4},{2,6},{4,0},{6,2},{8,12},{10,14},{12,8},{14,10},{16,20},{18,... | collective-permute-start | bytes 393224 | tf_op jit(solution)/shard_map/ppermute | solution.py:276
  46.9 4.3 %collective-permute-start.7 = (bf16[2,4,16,256]{3,2,1,0:T(8,128)(2,1)S(1)}, bf16[2,4,16,256]{3,2,1,0:T(8,128)(2,1)S(1)}, u32[]{:S(2)}, u32[]{:S(2)}) collective-permute-start(bf16[2,4,16,256]{3,2,1,0:T(8,128)(2,1)S(1)} %fusion.3), channel_id=1, source_target_pairs={{0,8},{2,10},{4,12},{6,14},{8,0},{10,2},{12,4},{14,6},{16,24},{18,... | collective-permute-start | bytes 196616 | tf_op jit(solution)/shard_map/ppermute | solution.py:276
  51.2 4.9 %collective-permute-start.8 = (bf16[1,4,16,256]{3,2,1,0:T(8,128)(2,1)S(1)}, bf16[1,4,16,256]{3,2,1,0:T(8,128)(2,1)S(1)}, u32[]{:S(2)}, u32[]{:S(2)}) collective-permute-start(bf16[1,4,16,256]{3,2,1,0:T(8,128)(2,1)S(1)} %dynamic-slice_convert_fusion.3), channel_id=1, source_target_pairs={{0,16},{2,18},{4,20},{6,22},{8,24},{10,26},{12,28},{14,30},{16,0},... | collective-permute-start | bytes 98312 | tf_op jit(solution)/shard_map/ppermute | solution.py:276
  53.5 6.6 %copy-start.10 = (f32[4,16,256]{2,1,0:T(8,128)S(1)}, f32[4,16,256]{2,1,0:T(8,128)}, u32[]{:S(2)}) copy-start(f32[4,16,256]{2,1,0:T(8,128)} %param.27) | copy-start | bytes 196612
  53.5 6.6 %copy-start.11 = (f32[4,16,256]{2,1,0:T(8,128)S(1)}, f32[4,16,256]{2,1,0:T(8,128)}, u32[]{:S(2)}) copy-start(f32[4,16,256]{2,1,0:T(8,128)} %param.26) | copy-start | bytes 196612
  56.1 4.0 %collective-permute-start.9 = (bf16[4,16,256]{2,1,0:T(8,128)(2,1)S(1)}, bf16[4,16,256]{2,1,0:T(8,128)(2,1)S(1)}, u32[]{:S(2)}, u32[]{:S(2)}) collective-permute-start(bf16[4,16,256]{2,1,0:T(8,128)(2,1)S(1)} %fusion.4), channel_id=1, source_target_pairs={{0,1},{1,0},{2,3},{3,2},{4,5},{5,4},{6,7},{7,6},{8,9},{9,8},{10,11... | collective-permute-start | bytes 98312 | tf_op jit(solution)/shard_map/ppermute | solution.py:283

commit v2 on v1

v2 whole, which is shorter than its diff:
```python
import functools
import math

import jax
import jax.numpy as jnp
from jax import lax
from jax.experimental import pallas as pl
from jax.experimental.pallas import tpu as pltpu
from jax.sharding import PartitionSpec as P

CHUNK = 64
FAR = 1e30

loss_weight = 0.0625
epsilon_norm = 1e-06

F32 = jnp.float32
BF16 = jnp.bfloat16
NT = (((1,), (1,)), ((), ()))
TN = (((0,), (0,)), ((), ()))


def dot(a, b):
    return jnp.dot(a, b, preferred_element_type=F32)


def dot_nt(a, b):
    return lax.dot_general(a, b, NT, preferred_element_type=F32)


def dot_tn(a, b):
    return lax.dot_general(a, b, TN, preferred_element_type=F32)


def to_column(row):
    n = row.shape[1]
    eye = lax.broadcasted_iota(jnp.int32, (n, n), 0) == lax.broadcasted_iota(jnp.int32, (n, n), 1)
    return jnp.sum(jnp.where(eye, row, jnp.zeros_like(row)), axis=1, keepdims=True)


def to_row(column):
    n = column.shape[0]
    eye = lax.broadcasted_iota(jnp.int32, (n, n), 0) == lax.broadcasted_iota(jnp.int32, (n, n), 1)
    return jnp.sum(jnp.where(eye, column, jnp.zeros_like(column)), axis=0, keepdims=True)


def embed_kernel(features, species, species_table, norm_gain, send_rows, embedded, normed, normed_t, parcel):
    atoms = features.shape[0]
    kinds = species_table.shape[0]
    column = to_column(species[...])
    total = features[...].astype(F32)
    picked = jnp.zeros_like(total)
    for kind in range(kinds):
        row = species_table[kind : kind + 1, :].astype(F32)
        picked = jnp.where(column == kind, row, picked)
    total = total + picked
    embedded[...] = total
    scale = lax.rsqrt(jnp.mean(total * total, axis=-1, keepdims=True) + epsilon_norm)
    norm = total * scale * norm_gain[...]
    half = norm.astype(BF16)
    normed[...] = half
    normed_t[...] = norm.T.astype(BF16)
    bricks, slots = send_rows.shape
    for brick in range(bricks):
        chosen = send_rows[brick : brick + 1, :]
        picks = (lax.broadcasted_iota(jnp.int32, (atoms, slots), 0) == chosen).astype(F32).astype(BF16)
        parcel[brick] = dot_tn(picks, half).astype(BF16)


def index_kernel(decay, neighbours, counts, distances, weight, absent, key_ref):
    slots, atoms = neighbours.shape
    heads, table_rows = weight.shape[:2]
    slot = lax.broadcasted_iota(jnp.int32, (slots, atoms), 0)
    valid = slot < counts[...]
    held = jnp.where(valid, neighbours[...], -1 - slot)
    rank = jnp.zeros((slots, atoms), jnp.int32)
    for j in range(slots):
        rank += ((held == held[j : j + 1, :]) & (slot > j)).astype(jnp.int32)
    key_ref[...] = jnp.where(valid, held + table_rows * rank, -1)
    weight[...] = jnp.zeros_like(weight)
    absent[...] = jnp.full_like(absent, -FAR)

    def layer(level, carry):
        for start in range(0, table_rows, CHUNK):
            at = pl.ds(start, CHUNK)
            row = lax.broadcasted_iota(jnp.int32, (CHUNK, atoms), 0) + (start + level * table_rows)
            distance = jnp.full((CHUNK, atoms), FAR, F32)
            for j in range(slots):
                distance = jnp.where(row == key_ref[j : j + 1, :], distances[j : j + 1, :], distance)
            absent[at, :] = jnp.where(distance < FAR, 0.0, absent[at, :])
            for h in range(heads):
                weight[h, at, :] += jnp.exp(-decay[h] * distance)
        return carry

    lax.fori_loop(0, jnp.max(rank) + 1, layer, 0)


def sweep_kernel(
    weights,
    normed,
    normed_t,
    ghosts,
    embedded,
    weight,
    absent,
    readout,
    targets,
    energies,
    grads,
    score_ref,
    att_ref,
    att_half,
    grad_score,
):
    atoms, width = normed.shape
    heads = weight.shape[0]
    head_size = width // heads
    scale = 1.0 / math.sqrt(head_size)
    head_of = lax.broadcasted_iota(jnp.int32, (atoms, width), 1) // head_size

    def stacked(array):
        zero = jnp.zeros_like(array)
        return jnp.concatenate([jnp.where(head_of == h, array, zero) for h in range(heads)], axis=0)

    def stacked_t(array):
        columns = []
        for h in range(heads):
            pieces = [array[h * head_size : (h + 1) * head_size]]
            if h > 0:
                pieces.insert(0, jnp.zeros((h * head_size, atoms), array.dtype))
            if h + 1 < heads:
                pieces.append(jnp.zeros((width - (h + 1) * head_size, atoms), array.dtype))
            columns.append(jnp.concatenate(pieces, axis=0))
        return jnp.concatenate(columns, axis=1)

    def own_channels(wide):
        return jnp.concatenate(
            [wide[h * head_size : (h + 1) * head_size, h * atoms : (h + 1) * atoms] for h in range(heads)], axis=0
        )

    norm = normed[...]
    table = jnp.concatenate([norm, ghosts[...]], axis=0)
    query = dot(norm, weights[0])
    keys = dot(table, weights[1]).astype(BF16)
    values = dot(table, weights[2]).astype(BF16)
    score_ref[...] = dot(keys, stacked_t(query.T.astype(BF16)))
    gone = absent[...]
    for h in range(heads):
        at = pl.ds(h * atoms, atoms)
        score = score_ref[:, at] * scale + gone
        terms = jnp.exp(score - jnp.max(score, axis=0, keepdims=True)) * weight[h]
        attention = terms * (1.0 / jnp.sum(terms, axis=0, keepdims=True))
        att_ref[:, at] = attention
        att_half[:, at] = attention.astype(BF16)
    attended_t = own_channels(dot_tn(values, att_half[...]))
    attended = attended_t.T.astype(BF16)

    out_proj = weights[3]
    updated = embedded[...] + dot(attended, out_proj)
    sigmoid = 1.0 / (1.0 + jnp.exp(-updated))
    energy = jnp.sum(readout[...] * (updated * sigmoid), axis=1, keepdims=True)
    energies[...] = to_row(energy)
    grad_energy = loss_weight * (energy - to_column(targets[...]))
    slope = sigmoid * (1.0 + updated * (1.0 - sigmoid))
    grad_updated = (grad_energy * readout[...] * slope).astype(BF16)
    grads[3] = dot(attended_t.astype(BF16), grad_updated)
    grad_attended = dot_nt(grad_updated, out_proj)

    score_ref[...] = dot(values, stacked_t(grad_attended.T.astype(BF16)))
    value_grads = dot(att_half[...], stacked(grad_attended.astype(BF16)))
    grads[2] = dot_tn(table, value_grads.astype(BF16))
    for h in range(heads):
        at = pl.ds(h * atoms, atoms)
        attention = att_ref[:, at]
        grad_weights = score_ref[:, at]
        mean = jnp.sum(attention * grad_weights, axis=0, keepdims=True)
        grad_score[:, at] = (attention * (grad_weights - mean)).astype(BF16)
    grad_query_t = own_channels(dot_tn(keys, grad_score[...])) * scale
    grads[0] = dot_nt(normed_t[...], grad_query_t.astype(BF16))
    key_grads = dot(grad_score[...], stacked(query.astype(BF16))) * scale
    grads[1] = dot_tn(table, key_grads.astype(BF16))


def vmem(count):
    return [pl.BlockSpec(memory_space=pltpu.VMEM)] * count


SMEM = pl.BlockSpec(memory_space=pltpu.SMEM)


def struct(shape, dtype):
    return jax.ShapeDtypeStruct(shape, dtype)


def flips(size, offset):
    return [(i, i ^ offset) for i in range(size)]


def halvings(size):
    offsets = []
    offset = size // 2
    while offset:
        offsets.append(offset)
        offset //= 2
    return offsets


def gather_cells(shard, cells):
    place = lax.axis_index("cell")
    offsets = halvings(cells)
    held = shard[None]
    for offset in offsets:
        other = lax.ppermute(held, "cell", flips(cells, offset))
        first = (place // offset) % 2 == 0
        held = jnp.where(first, jnp.concatenate([held, other]), jnp.concatenate([other, held]))
    bits = len(offsets)
    matrices, rows, width = shard.shape
    held = held.reshape((2,) * bits + shard.shape)
    held = held.transpose((bits,) + tuple(reversed(range(bits))) + (bits + 1, bits + 2))
    return held.reshape(matrices, cells * rows, width)


def reduce_cells(parts, cells):
    place = lax.axis_index("cell")
    tail = parts.shape[1:]
    for offset in reversed(halvings(cells)):
        bit = (place // offset) % 2
        pairs = parts.reshape((-1, 2) + tail)
        keep = lax.dynamic_index_in_dim(pairs, bit, 1, False)
        send = lax.dynamic_index_in_dim(pairs, 1 - bit, 1, False)
        parts = keep + lax.ppermute(send.astype(BF16), "cell", flips(cells, offset)).astype(F32)
    return parts[0]


def reduce_bricks(total, bricks):
    for offset in halvings(bricks):
        mine = total.astype(BF16)
        total = mine.astype(F32) + lax.ppermute(mine, "brick", flips(bricks, offset)).astype(F32)
    return total


def body(
    cells,
    bricks,
    features,
    species,
    species_table,
    neighbours,
    counts,
    send_lists,
    distances,
    head_decay,
    norm_gain,
    readout,
    targets,
    master,
    moment,
    second,
):
    atoms, width = features.shape[2:]
    slots = neighbours.shape[2]
    ghost_slots = send_lists.shape[3]
    heads = head_decay.shape[0]
    table_rows = atoms + bricks * ghost_slots

    weights = gather_cells(master.astype(BF16), cells)

    embedded, normed, normed_t, parcel = pl.pallas_call(
        embed_kernel,
        out_shape=(
            struct((atoms, width), F32),
            struct((atoms, width), BF16),
            struct((width, atoms), BF16),
            struct((bricks, ghost_slots, width), BF16),
        ),
        in_specs=vmem(5),
        out_specs=tuple(vmem(4)),
        name="embed",
    )(features[0, 0], species[0], species_table, norm_gain[None], send_lists[0, 0])

    brick = lax.axis_index("brick")
    ghosts = parcel
    for offset in range(1, bricks):
        peer = brick ^ offset
        sent = lax.dynamic_index_in_dim(parcel, peer, 0, True)
        arrived = lax.ppermute(sent, "brick", flips(bricks, offset))
        ghosts = lax.dynamic_update_slice_in_dim(ghosts, arrived, peer, 0)
    ghosts = ghosts.reshape(bricks * ghost_slots, width)

    weight, absent = pl.pallas_call(
        index_kernel,
        out_shape=(struct((heads, table_rows, atoms), F32), struct((table_rows, atoms), F32)),
        in_specs=[SMEM] + vmem(3),
        out_specs=tuple(vmem(2)),
        scratch_shapes=[pltpu.VMEM((slots, atoms), jnp.int32)],
        name="index",
    )(head_decay, neighbours[0, 0], counts[0], distances[0, 0])

    columns = heads * atoms
    energies, grads = pl.pallas_call(
        sweep_kernel,
        out_shape=(struct((1, atoms), F32), struct((4, width, width), F32)),
        in_specs=vmem(9),
        out_specs=tuple(vmem(2)),
        scratch_shapes=[
            pltpu.VMEM((table_rows, columns), F32),
            pltpu.VMEM((table_rows, columns), F32),
            pltpu.VMEM((table_rows, columns), BF16),
            pltpu.VMEM((table_rows, columns), BF16),
        ],
        compiler_params=pltpu.CompilerParams(vmem_limit_bytes=32 * 1024 * 1024),
        name="sweep",
    )(weights, normed, normed_t, ghosts, embedded, weight, absent, readout[None], targets[0])

    parts = grads.reshape(4, cells, width // cells, width).transpose(1, 0, 2, 3)
    owned = reduce_bricks(reduce_cells(parts, cells), bricks)
    moment_new = 0.9 * moment + 0.1 * owned
    second_new = 0.999 * second + 0.001 * owned * owned
    adam_step = moment_new / (jnp.sqrt(second_new) + 1e-08)
    return (energies[None], moment_new, second_new, adam_step)


def solution(mesh):
    return jax.shard_map(
        functools.partial(body, mesh.shape["cell"], mesh.shape["brick"]),
        mesh=mesh,
        in_specs=(
            P("cell", "brick", None, None),
            P("cell", "brick", None),
            P(),
            P("cell", "brick", None, None),
            P("cell", "brick", None),
            P("cell", "brick", None, None),
            P("cell", "brick", None, None),
            P(),
            P(),
            P(),
            P("cell", "brick", None),
            P(None, "cell", None),
            P(None, "cell", None),
            P(None, "cell", None),
        ),
        out_specs=(
            P("cell", "brick", None),
            P(None, "cell", None),
            P(None, "cell", None),
            P(None, "cell", None),
        ),
        check_vma=False,
    )
```

time: 61.1 us -> 52 us (0.85)
  Pallas kernels: 17.4 us -> 9.11 us
  waiting for transfers between devices: 24.6 us -> 21.7 us
  starting transfers between devices: 14.1 us -> 16.2 us
    pallas_call x2, Pallas kernels: 15.6 us -> 7.27 us  [the longest x1 4.58 us: body(): pl.pallas_call(index_kernel, out_shape=(struct((heads, table_rows, atoms)...]
    ppermute x4, waiting for transfers between devices: 12.5 us -> 10.2 us  [reduce_cells(): lax.ppermute(send.astype(BF16), 'cell', flips(cells, offset)).astype(F32)]
    ppermute x4, starting transfers between devices: 4.81 us -> 6.27 us  [reduce_cells(): lax.ppermute(send.astype(BF16), 'cell', flips(cells, offset)).astype(F32)]
    ppermute x1, starting transfers between devices: 0.07 us -> 0.69 us  [reduce_bricks(): lax.ppermute(mine, 'brick', flips(bricks, offset)).astype(F32)]
    ppermute x1, waiting for transfers between devices: 3.9 us -> 3.29 us  [reduce_bricks(): lax.ppermute(mine, 'brick', flips(bricks, offset)).astype(F32)]
  transfers between devices with their start and end apart: 10 -> 10, of which waited for: 8 -> 8; matrix products, arithmetic and copies ran while one was open for 1% -> 1% of each run, Pallas kernels for 8% -> 12%
where the time goes in v2:
time: 52 us; the launch traced here: 51.7 us
  waiting for transfers between devices  21.7 us (42%)
  starting transfers between devices  16.2 us (31%)
  Pallas kernels  9.11 us (18%)
  local copies, waits for them, and re-layouts  2.07 us (4%)
  other arithmetic  1.81 us (3%)
  between operations  0.83 us (2%)
    ppermute x4, waiting for transfers between devices, reduce_cells(): lax.ppermute(send.astype(BF16), 'cell', flips(cells, offset)).astype(F32)  10.2 us
    ppermute x4, waiting for transfers between devices, gather_cells(): other = lax.ppermute(held, 'cell', flips(cells, offset))  8.19 us
    ppermute x4, starting transfers between devices, gather_cells(): other = lax.ppermute(held, 'cell', flips(cells, offset))  7.53 us
    ppermute x4, starting transfers between devices, reduce_cells(): lax.ppermute(send.astype(BF16), 'cell', flips(cells, offset)).astype(F32)  6.27 us
    pallas_call x1, Pallas kernels, body(): pl.pallas_call(index_kernel, out_shape=(struct((heads, table_rows, atoms)...  4.58 us
    ppermute x1, waiting for transfers between devices, reduce_bricks(): lax.ppermute(mine, 'brick', flips(bricks, offset)).astype(F32)  3.29 us
    pallas_call x1, Pallas kernels, body(): pl.pallas_call(sweep_kernel, out_shape=(struct((1, atoms), F32), struct((...  2.69 us
    pallas_call x1, Pallas kernels, body(): pl.pallas_call(embed_kernel, out_shape=(struct((atoms, width), F32), stru...  1.84 us
  transfers between devices with their start and end apart: 10, of which 8 were waited for; matrix products, arithmetic and copies ran while one was open for 1% of the time, Pallas kernels for 12%

profile of v2, /device:TPU:0, one launch (start us, length us, event | category | flops | bytes accessed | tf_op | source)
XLA Modules:
  0.0 51.7 jit_solution(2018835956594931307)
XLA Ops:
  0.6 0.8 %convert_bitcast_fusion = bf16[1,4,16,256]{3,2,1,0:T(8,128)(2,1)S(1)} fusion(f32[4,16,256]{2,1,0:T(8,128)} %param.25), kind=kLoop, calls=%fused_computation.21 | loop fusion | flops 16384 | bytes 98304 | tf_op jit(solution)/shard_map/broadcast_in_dim | solution.py:211
  1.5 4.0 %collective-permute-start = (bf16[1,4,16,256]{3,2,1,0:T(8,128)(2,1)S(1)}, bf16[1,4,16,256]{3,2,1,0:T(8,128)(2,1)S(1)}, u32[]{:S(2)}, u32[]{:S(2)}) collective-permute-start(bf16[1,4,16,256]{3,2,1,0:T(8,128)(2,1)S(1)} %convert_bitcast_fusion), channel_id=1, source_target_pairs={{0,16},{2,18},{4,20},{6,22},{8,24},{10,26},{12,28},{14,30},{16,0},... | collective-permute-start | bytes 98312 | tf_op jit(solution)/shard_map/ppermute | solution.py:213
  5.5 2.2 %collective-permute-done = bf16[1,4,16,256]{3,2,1,0:T(8,128)(2,1)S(1)} collective-permute-done((bf16[1,4,16,256]{3,2,1,0:T(8,128)(2,1)S(1)}, bf16[1,4,16,256]{3,2,1,0:T(8,128)(2,1)S(1)}, u32[]{:S(2)}, u32[]{:S(2)}) %collective-permute-start) | collective-permute-done | bytes 32800 | tf_op jit(solution)/shard_map/ppermute | solution.py:213
  7.8 1.6 %collective-permute-start.1 = (bf16[2,4,16,256]{3,2,1,0:T(8,128)(2,1)S(1)}, bf16[2,4,16,256]{3,2,1,0:T(8,128)(2,1)S(1)}, u32[]{:S(2)}, u32[]{:S(2)}) collective-permute-start(bf16[2,4,16,256]{3,2,1,0:T(8,128)(2,1)S(1)} %maximum_select_fusion.3), channel_id=1, source_target_pairs={{0,8},{2,10},{4,12},{6,14},{8,0},{10,2},{12,4},{14,6},{16,24},{18,... | collective-permute-start | bytes 196616 | tf_op jit(solution)/shard_map/ppermute | solution.py:213
  9.4 2.7 %collective-permute-done.1 = bf16[2,4,16,256]{3,2,1,0:T(8,128)(2,1)S(1)} collective-permute-done((bf16[2,4,16,256]{3,2,1,0:T(8,128)(2,1)S(1)}, bf16[2,4,16,256]{3,2,1,0:T(8,128)(2,1)S(1)}, u32[]{:S(2)}, u32[]{:S(2)}) %collective-permute-start.1) | collective-permute-done | bytes 65568 | tf_op jit(solution)/shard_map/ppermute | solution.py:213
  12.1 1.8 %collective-permute-start.2 = (bf16[4,4,16,256]{3,2,1,0:T(8,128)(2,1)S(1)}, bf16[4,4,16,256]{3,2,1,0:T(8,128)(2,1)S(1)}, u32[]{:S(2)}, u32[]{:S(2)}) collective-permute-start(bf16[4,4,16,256]{3,2,1,0:T(8,128)(2,1)S(1)} %maximum_select_fusion.2), channel_id=1, source_target_pairs={{0,4},{2,6},{4,0},{6,2},{8,12},{10,14},{12,8},{14,10},{16,20},{18,... | collective-permute-start | bytes 393224 | tf_op jit(solution)/shard_map/ppermute | solution.py:213
  13.9 3.2 %collective-permute-done.2 = bf16[4,4,16,256]{3,2,1,0:T(8,128)(2,1)S(1)} collective-permute-done((bf16[4,4,16,256]{3,2,1,0:T(8,128)(2,1)S(1)}, bf16[4,4,16,256]{3,2,1,0:T(8,128)(2,1)S(1)}, u32[]{:S(2)}, u32[]{:S(2)}) %collective-permute-start.2) | collective-permute-done | bytes 131104 | tf_op jit(solution)/shard_map/ppermute | solution.py:213
  17.2 0.1 collective-permute-start.3
  17.3 1.8 %embed.1 = (f32[128,256]{1,0:T(8,128)}, bf16[128,256]{1,0:T(8,128)(2,1)}, bf16[256,128]{1,0:T(8,128)(2,1)}, bf16[2,32,256]{2,1,0:T(8,128)(2,1)}) custom-call(bf16[128,256]{1,0:T(8,128)(2,1)} %bitcast.49, s32[1,128]{1,0:T(1,128)} %bitcast.54, bf16[4,256]{1,0:T(4,128)(2,1)} %species_table.1, f32[1,256]{1,0:T(1,128)} %bitcast.52, s32[2,32]{1,0:T(2,128)} %bitcast.53), custom_call_target="tpu_custom_call" | custom-call | tf_op jit(solution)/shard_map/embed/pallas_call | solution.py:268
  19.1 0.7 %constant_dynamic-slice_fusion = bf16[1,32,256]{2,1,0:T(8,128)(2,1)S(1)} fusion(bf16[2,32,256]{2,1,0:T(8,128)(2,1)} %get-tuple-element.14, s32[]{:T(128)S(6)} %select_n.127), kind=kLoop, calls=%fused_computation.23 | loop fusion | bytes 32772 | tf_op jit(solution)/shard_map/jit(dynamic_index_in_dim)/dynamic_slice | solution.py:285
  19.8 1.7 %collective-permute-start.4 = (bf16[1,32,256]{2,1,0:T(8,128)(2,1)S(1)}, bf16[1,32,256]{2,1,0:T(8,128)(2,1)S(1)}, u32[]{:S(2)}, u32[]{:S(2)}) collective-permute-start(bf16[1,32,256]{2,1,0:T(8,128)(2,1)S(1)} %constant_dynamic-slice_fusion), channel_id=1, source_target_pairs={{0,1},{1,0},{2,3},{3,2},{4,5},{5,4},{6,7},{7,6},{8,9},{9,8},{10,11... | collective-permute-start | bytes 49160 | tf_op jit(solution)/shard_map/ppermute | solution.py:286
  21.5 0.0 copy-start.3
  21.5 4.6 %index.1 = (f32[8,192,128]{2,1,0:T(8,128)}, f32[192,128]{1,0:T(8,128)}) custom-call(f32[8]{0:T(128)} %decay.1, s32[64,128]{1,0:T(8,128)} %bitcast.50, s32[1,128]{1,0:T(1,128)} %bitcast.55, f32[64,128]{1,0:T(8,128)} %bitcast.51), custom_call_target="tpu_custom_call" | custom-call | tf_op jit(solution)/shard_map/index/pallas_call | solution.py:290
  26.1 0.0 collective-permute-done.4
  26.1 0.0 copy-done.3
  26.1 0.0 collective-permute-done.3
  26.1 0.0 copy-start.4
  26.1 0.0 copy-start.5
  26.2 0.1 maximum_select_fusion
  26.3 0.0 copy-start
  26.3 0.0 copy-start.1
  26.3 0.0 copy-start.2
  26.3 0.1 copy.21
  26.3 0.0 copy-start.6
  26.4 0.0 copy-start.7
  26.4 0.6 %copy-done.4 = bf16[128,256]{1,0:T(8,128)(2,1)S(1)} copy-done((bf16[128,256]{1,0:T(8,128)(2,1)S(1)}, bf16[128,256]{1,0:T(8,128)(2,1)}, u32[]{:S(2)}) %copy-start.4) | copy-done | bytes 65560
  27.0 0.0 copy-done.5
  27.0 0.4 copy-done
  27.4 0.0 copy-done.1
  27.4 0.0 copy-done.2
  27.4 0.0 copy-done.6
  27.4 0.0 copy-done.7
  27.4 2.7 %sweep.1 = (f32[1,128]{1,0:T(1,128)}, f32[4,256,256]{2,1,0:T(8,128)S(1)}) custom-call(bf16[4,256,256]{2,1,0:T(8,128)(2,1)S(1)} %bitcast.37, bf16[128,256]{1,0:T(8,128)(2,1)S(1)} %copy-done.4, bf16[256,128]{1,0:T(8,128)(2,1)S(1)} %copy-done.5, bf16[64,256]{1,0:T(8,128)(2,1)S(1)} %bitcast.39, f32[128,256]{1,0:T(8,128)S(1)} %copy-done.1, ...), custom_call_target="tpu_custom_call" | custom-call | tf_op jit(solution)/shard_map/sweep/pallas_call | solution.py:300
  30.1 0.1 copy.22
  30.3 0.3 collective-permute-start.5
  30.6 1.3 %collective-permute-done.5 = bf16[8,4,16,256]{3,2,1,0:T(8,128)(2,1)S(1)} collective-permute-done((bf16[8,4,16,256]{3,2,1,0:T(8,128)(2,1)S(1)}, bf16[8,4,16,256]{3,2,1,0:T(8,128)(2,1)S(1)}, u32[]{:S(2)}, u32[]{:S(2)}) %collective-permute-start.5) | collective-permute-done | bytes 262176 | tf_op jit(solution)/shard_map/ppermute | solution.py:231
  31.9 0.1 bitcast_add_fusion
  32.0 1.6 %collective-permute-start.6 = (bf16[4,4,16,256]{3,2,1,0:T(8,128)(2,1)S(1)}, bf16[4,4,16,256]{3,2,1,0:T(8,128)(2,1)S(1)}, u32[]{:S(2)}, u32[]{:S(2)}) collective-permute-start(bf16[4,4,16,256]{3,2,1,0:T(8,128)(2,1)S(1)} %fusion.1), channel_id=1, source_target_pairs={{0,4},{2,6},{4,0},{6,2},{8,12},{10,14},{12,8},{14,10},{16,20},{18,... | collective-permute-start | bytes 393224 | tf_op jit(solution)/shard_map/ppermute | solution.py:231
  33.6 4.1 %collective-permute-done.6 = bf16[4,4,16,256]{3,2,1,0:T(8,128)(2,1)S(1)} collective-permute-done((bf16[4,4,16,256]{3,2,1,0:T(8,128)(2,1)S(1)}, bf16[4,4,16,256]{3,2,1,0:T(8,128)(2,1)S(1)}, u32[]{:S(2)}, u32[]{:S(2)}) %collective-permute-start.6) | collective-permute-done | bytes 131104 | tf_op jit(solution)/shard_map/ppermute | solution.py:231
  37.7 2.0 %collective-permute-start.7 = (bf16[2,4,16,256]{3,2,1,0:T(8,128)(2,1)S(1)}, bf16[2,4,16,256]{3,2,1,0:T(8,128)(2,1)S(1)}, u32[]{:S(2)}, u32[]{:S(2)}) collective-permute-start(bf16[2,4,16,256]{3,2,1,0:T(8,128)(2,1)S(1)} %fusion.3), channel_id=1, source_target_pairs={{0,8},{2,10},{4,12},{6,14},{8,0},{10,2},{12,4},{14,6},{16,24},{18,... | collective-permute-start | bytes 196616 | tf_op jit(solution)/shard_map/ppermute | solution.py:231
  39.7 2.4 %collective-permute-done.7 = bf16[2,4,16,256]{3,2,1,0:T(8,128)(2,1)S(1)} collective-permute-done((bf16[2,4,16,256]{3,2,1,0:T(8,128)(2,1)S(1)}, bf16[2,4,16,256]{3,2,1,0:T(8,128)(2,1)S(1)}, u32[]{:S(2)}, u32[]{:S(2)}) %collective-permute-start.7) | collective-permute-done | bytes 65568 | tf_op jit(solution)/shard_map/ppermute | solution.py:231
  42.1 2.4 %collective-permute-start.8 = (bf16[1,4,16,256]{3,2,1,0:T(8,128)(2,1)S(1)}, bf16[1,4,16,256]{3,2,1,0:T(8,128)(2,1)S(1)}, u32[]{:S(2)}, u32[]{:S(2)}) collective-permute-start(bf16[1,4,16,256]{3,2,1,0:T(8,128)(2,1)S(1)} %dynamic-slice_convert_fusion.3), channel_id=1, source_target_pairs={{0,16},{2,18},{4,20},{6,22},{8,24},{10,26},{12,28},{14,30},{16,0},... | collective-permute-start | bytes 98312 | tf_op jit(solution)/shard_map/ppermute | solution.py:231
  44.6 0.0 copy-start.8
  44.6 0.0 copy-start.9
  44.6 2.4 %collective-permute-done.8 = bf16[1,4,16,256]{3,2,1,0:T(8,128)(2,1)S(1)} collective-permute-done((bf16[1,4,16,256]{3,2,1,0:T(8,128)(2,1)S(1)}, bf16[1,4,16,256]{3,2,1,0:T(8,128)(2,1)S(1)}, u32[]{:S(2)}, u32[]{:S(2)}) %collective-permute-start.8) | collective-permute-done | bytes 32800 | tf_op jit(solution)/shard_map/ppermute | solution.py:231
  47.0 0.7 %collective-permute-start.9 = (bf16[4,16,256]{2,1,0:T(8,128)(2,1)S(1)}, bf16[4,16,256]{2,1,0:T(8,128)(2,1)S(1)}, u32[]{:S(2)}, u32[]{:S(2)}) collective-permute-start(bf16[4,16,256]{2,1,0:T(8,128)(2,1)S(1)} %fusion.4), channel_id=1, source_target_pairs={{0,1},{1,0},{2,3},{3,2},{4,5},{5,4},{6,7},{7,6},{8,9},{9,8},{10,11... | collective-permute-start | bytes 98312 | tf_op jit(solution)/shard_map/ppermute | solution.py:238
  47.7 3.3 %collective-permute-done.9 = bf16[4,16,256]{2,1,0:T(8,128)(2,1)S(1)} collective-permute-done((bf16[4,16,256]{2,1,0:T(8,128)(2,1)S(1)}, bf16[4,16,256]{2,1,0:T(8,128)(2,1)S(1)}, u32[]{:S(2)}, u32[]{:S(2)}) %collective-permute-start.9) | collective-permute-done | bytes 32800 | tf_op jit(solution)/shard_map/ppermute | solution.py:238
  51.0 0.0 copy-done.8
  51.0 0.0 copy-done.9
  51.0 0.7 %add_divide_fusion = (f32[4,16,256]{2,1,0:T(8,128)}, f32[4,16,256]{2,1,0:T(8,128)}, f32[4,16,256]{2,1,0:T(8,128)}) fusion(bf16[4,16,256]{2,1,0:T(8,128)(2,1)S(1)} %collective-permute-done.9, bf16[4,16,256]{2,1,0:T(8,128)(2,1)S(1)} %fusion.4, f32[4,16,256]{2,1,0:T(8,128)S(1)} %copy-done.8, f32[4,16,256]{2,1,0:T(8,128)S(1)} %copy-done.9), kind=kLoop, calls=%fused_computation.15 | loop fusion | flops 196608 | bytes 393216 | tf_op jit(solution)/shard_map/div | solution.py:319
  (11 shorter events, 0.2 us)
Async XLA Ops:
  1.5 6.3 %collective-permute-start = (bf16[1,4,16,256]{3,2,1,0:T(8,128)(2,1)S(1)}, bf16[1,4,16,256]{3,2,1,0:T(8,128)(2,1)S(1)}, u32[]{:S(2)}, u32[]{:S(2)}) collective-permute-start(bf16[1,4,16,256]{3,2,1,0:T(8,128)(2,1)S(1)} %convert_bitcast_fusion), channel_id=1, source_target_pairs={{0,16},{2,18},{4,20},{6,22},{8,24},{10,26},{12,28},{14,30},{16,0},... | collective-permute-start | bytes 98312 | tf_op jit(solution)/shard_map/ppermute | solution.py:213
  7.8 4.3 %collective-permute-start.1 = (bf16[2,4,16,256]{3,2,1,0:T(8,128)(2,1)S(1)}, bf16[2,4,16,256]{3,2,1,0:T(8,128)(2,1)S(1)}, u32[]{:S(2)}, u32[]{:S(2)}) collective-permute-start(bf16[2,4,16,256]{3,2,1,0:T(8,128)(2,1)S(1)} %maximum_select_fusion.3), channel_id=1, source_target_pairs={{0,8},{2,10},{4,12},{6,14},{8,0},{10,2},{12,4},{14,6},{16,24},{18,... | collective-permute-start | bytes 196616 | tf_op jit(solution)/shard_map/ppermute | solution.py:213
  12.1 5.0 %collective-permute-start.2 = (bf16[4,4,16,256]{3,2,1,0:T(8,128)(2,1)S(1)}, bf16[4,4,16,256]{3,2,1,0:T(8,128)(2,1)S(1)}, u32[]{:S(2)}, u32[]{:S(2)}) collective-permute-start(bf16[4,4,16,256]{3,2,1,0:T(8,128)(2,1)S(1)} %maximum_select_fusion.2), channel_id=1, source_target_pairs={{0,4},{2,6},{4,0},{6,2},{8,12},{10,14},{12,8},{14,10},{16,20},{18,... | collective-permute-start | bytes 393224 | tf_op jit(solution)/shard_map/ppermute | solution.py:213
  17.2 8.9 %collective-permute-start.3 = (bf16[8,4,16,256]{3,2,1,0:T(8,128)(2,1)S(1)}, bf16[8,4,16,256]{3,2,1,0:T(8,128)(2,1)S(1)}, u32[]{:S(2)}, u32[]{:S(2)}) collective-permute-start(bf16[8,4,16,256]{3,2,1,0:T(8,128)(2,1)S(1)} %maximum_select_fusion.1), channel_id=1, source_target_pairs={{0,2},{2,0},{4,6},{6,4},{8,10},{10,8},{12,14},{14,12},{16,18},{18,... | collective-permute-start | bytes 786440 | tf_op jit(solution)/shard_map/ppermute | solution.py:213
  19.8 6.3 %collective-permute-start.4 = (bf16[1,32,256]{2,1,0:T(8,128)(2,1)S(1)}, bf16[1,32,256]{2,1,0:T(8,128)(2,1)S(1)}, u32[]{:S(2)}, u32[]{:S(2)}) collective-permute-start(bf16[1,32,256]{2,1,0:T(8,128)(2,1)S(1)} %constant_dynamic-slice_fusion), channel_id=1, source_target_pairs={{0,1},{1,0},{2,3},{3,2},{4,5},{5,4},{6,7},{7,6},{8,9},{9,8},{10,11... | collective-permute-start | bytes 49160 | tf_op jit(solution)/shard_map/ppermute | solution.py:286
  21.5 4.6 %copy-start.3 = (bf16[2,32,256]{2,1,0:T(8,128)(2,1)S(1)}, bf16[2,32,256]{2,1,0:T(8,128)(2,1)}, u32[]{:S(2)}) copy-start(bf16[2,32,256]{2,1,0:T(8,128)(2,1)} %get-tuple-element.14) | copy-start | bytes 98308
  26.1 0.8 %copy-start.4 = (bf16[128,256]{1,0:T(8,128)(2,1)S(1)}, bf16[128,256]{1,0:T(8,128)(2,1)}, u32[]{:S(2)}) copy-start(bf16[128,256]{1,0:T(8,128)(2,1)} %get-tuple-element.12.normed) | copy-start | bytes 196612
  26.1 0.9 %copy-start.5 = (bf16[256,128]{1,0:T(8,128)(2,1)S(1)}, bf16[256,128]{1,0:T(8,128)(2,1)}, u32[]{:S(2)}) copy-start(bf16[256,128]{1,0:T(8,128)(2,1)} %get-tuple-element.13.normed_t) | copy-start | bytes 196612
  26.3 1.1 %copy-start = (f32[8,192,128]{2,1,0:T(8,128)S(1)}, f32[8,192,128]{2,1,0:T(8,128)}, u32[]{:S(2)}) copy-start(f32[8,192,128]{2,1,0:T(8,128)} %get-tuple-element.16.weight) | copy-start | bytes 2359300
  26.3 1.1 %copy-start.1 = (f32[128,256]{1,0:T(8,128)S(1)}, f32[128,256]{1,0:T(8,128)}, u32[]{:S(2)}) copy-start(f32[128,256]{1,0:T(8,128)} %get-tuple-element.15.embedded) | copy-start | bytes 393220
  26.3 1.2 %copy-start.2 = (f32[192,128]{1,0:T(8,128)S(1)}, f32[192,128]{1,0:T(8,128)}, u32[]{:S(2)}) copy-start(f32[192,128]{1,0:T(8,128)} %get-tuple-element.17.absent) | copy-start | bytes 294916
  26.3 1.1 %copy-start.6 = (f32[256]{0:T(256)S(1)}, f32[256]{0:T(256)}, u32[]{:S(2)}) copy-start(f32[256]{0:T(256)} %param.23) | copy-start | bytes 3076
  26.4 1.1 %copy-start.7 = (f32[1,1,128]{2,1,0:T(1,128)S(1)}, f32[1,1,128]{2,1,0:T(1,128)}, u32[]{:S(2)}) copy-start(f32[1,1,128]{2,1,0:T(1,128)} %param.24) | copy-start | bytes 1540
  30.3 1.6 %collective-permute-start.5 = (bf16[8,4,16,256]{3,2,1,0:T(8,128)(2,1)S(1)}, bf16[8,4,16,256]{3,2,1,0:T(8,128)(2,1)S(1)}, u32[]{:S(2)}, u32[]{:S(2)}) collective-permute-start(bf16[8,4,16,256]{3,2,1,0:T(8,128)(2,1)S(1)} %fusion), channel_id=1, source_target_pairs={{0,2},{2,0},{4,6},{6,4},{8,10},{10,8},{12,14},{14,12},{16,18},{18,... | collective-permute-start | bytes 786440 | tf_op jit(solution)/shard_map/ppermute | solution.py:231
  32.0 5.7 %collective-permute-start.6 = (bf16[4,4,16,256]{3,2,1,0:T(8,128)(2,1)S(1)}, bf16[4,4,16,256]{3,2,1,0:T(8,128)(2,1)S(1)}, u32[]{:S(2)}, u32[]{:S(2)}) collective-permute-start(bf16[4,4,16,256]{3,2,1,0:T(8,128)(2,1)S(1)} %fusion.1), channel_id=1, source_target_pairs={{0,4},{2,6},{4,0},{6,2},{8,12},{10,14},{12,8},{14,10},{16,20},{18,... | collective-permute-start | bytes 393224 | tf_op jit(solution)/shard_map/ppermute | solution.py:231
  37.7 4.3 %collective-permute-start.7 = (bf16[2,4,16,256]{3,2,1,0:T(8,128)(2,1)S(1)}, bf16[2,4,16,256]{3,2,1,0:T(8,128)(2,1)S(1)}, u32[]{:S(2)}, u32[]{:S(2)}) collective-permute-start(bf16[2,4,16,256]{3,2,1,0:T(8,128)(2,1)S(1)} %fusion.3), channel_id=1, source_target_pairs={{0,8},{2,10},{4,12},{6,14},{8,0},{10,2},{12,4},{14,6},{16,24},{18,... | collective-permute-start | bytes 196616 | tf_op jit(solution)/shard_map/ppermute | solution.py:231
  42.1 4.9 %collective-permute-start.8 = (bf16[1,4,16,256]{3,2,1,0:T(8,128)(2,1)S(1)}, bf16[1,4,16,256]{3,2,1,0:T(8,128)(2,1)S(1)}, u32[]{:S(2)}, u32[]{:S(2)}) collective-permute-start(bf16[1,4,16,256]{3,2,1,0:T(8,128)(2,1)S(1)} %dynamic-slice_convert_fusion.3), channel_id=1, source_target_pairs={{0,16},{2,18},{4,20},{6,22},{8,24},{10,26},{12,28},{14,30},{16,0},... | collective-permute-start | bytes 98312 | tf_op jit(solution)/shard_map/ppermute | solution.py:231
  44.6 6.4 %copy-start.8 = (f32[4,16,256]{2,1,0:T(8,128)S(1)}, f32[4,16,256]{2,1,0:T(8,128)}, u32[]{:S(2)}) copy-start(f32[4,16,256]{2,1,0:T(8,128)} %param.27) | copy-start | bytes 196612
  44.6 6.4 %copy-start.9 = (f32[4,16,256]{2,1,0:T(8,128)S(1)}, f32[4,16,256]{2,1,0:T(8,128)}, u32[]{:S(2)}) copy-start(f32[4,16,256]{2,1,0:T(8,128)} %param.26) | copy-start | bytes 196612
  47.0 4.0 %collective-permute-start.9 = (bf16[4,16,256]{2,1,0:T(8,128)(2,1)S(1)}, bf16[4,16,256]{2,1,0:T(8,128)(2,1)S(1)}, u32[]{:S(2)}, u32[]{:S(2)}) collective-permute-start(bf16[4,16,256]{2,1,0:T(8,128)(2,1)S(1)} %fusion.4), channel_id=1, source_target_pairs={{0,1},{1,0},{2,3},{3,2},{4,5},{5,4},{6,7},{7,6},{8,9},{9,8},{10,11... | collective-permute-start | bytes 98312 | tf_op jit(solution)/shard_map/ppermute | solution.py:238

commit v3 on v2

--- a/solution.py
+++ b/solution.py
@@ -8,7 +8,8 @@
 from jax.experimental.pallas import tpu as pltpu
 from jax.sharding import PartitionSpec as P
 
-CHUNK = 64
+CHUNK = 32
+DEPTH = 5
 FAR = 1e30
 
 loss_weight = 0.0625
@@ -73,26 +74,44 @@
     slot = lax.broadcasted_iota(jnp.int32, (slots, atoms), 0)
     valid = slot < counts[...]
     held = jnp.where(valid, neighbours[...], -1 - slot)
-    rank = jnp.zeros((slots, atoms), jnp.int32)
-    for j in range(slots):
-        rank += ((held == held[j : j + 1, :]) & (slot > j)).astype(jnp.int32)
-    key_ref[...] = jnp.where(valid, held + table_rows * rank, -1)
-    weight[...] = jnp.zeros_like(weight)
-    absent[...] = jnp.full_like(absent, -FAR)
-
-    def layer(level, carry):
-        for start in range(0, table_rows, CHUNK):
-            at = pl.ds(start, CHUNK)
-            row = lax.broadcasted_iota(jnp.int32, (CHUNK, atoms), 0) + (start + level * table_rows)
-            distance = jnp.full((CHUNK, atoms), FAR, F32)
-            for j in range(slots):
-                distance = jnp.where(row == key_ref[j : j + 1, :], distances[j : j + 1, :], distance)
-            absent[at, :] = jnp.where(distance < FAR, 0.0, absent[at, :])
-            for h in range(heads):
-                weight[h, at, :] += jnp.exp(-decay[h] * distance)
-        return carry
-
-    lax.fori_loop(0, jnp.max(rank) + 1, layer, 0)
+    key_ref[...] = held
+
+    def chunk(step, nearest):
+        start = pl.multiple_of(step * CHUNK, CHUNK)
+        at = pl.ds(start, CHUNK)
+        row = lax.broadcasted_iota(jnp.int32, (CHUNK, atoms), 0) + start
+        layers = [jnp.full((CHUNK, atoms), FAR, F32) for _ in range(DEPTH)]
+        for j in range(slots):
+            hit = row == key_ref[j : j + 1, :]
+            entering = distances[j : j + 1, :]
+            for k in range(DEPTH):
+                entering, layers[k] = layers[k], jnp.where(hit, entering, layers[k])
+        absent[at, :] = jnp.where(layers[0] < FAR, 0.0, -FAR)
+        for h in range(heads):
+            weight[h, at, :] = sum(jnp.exp(-decay[h] * layer) for layer in layers)
+        return jnp.minimum(nearest, jnp.min(layers[-1], axis=0, keepdims=True))
+
+    nearest = lax.fori_loop(0, table_rows // CHUNK, chunk, jnp.full((1, atoms), FAR, F32))
+
+    @pl.when(jnp.min(nearest) < FAR)
+    def _():
+        rank = jnp.zeros((slots, atoms), jnp.int32)
+        for j in range(slots):
+            rank += ((held == key_ref[j : j + 1, :]) & (slot < j)).astype(jnp.int32)
+        key_ref[...] = jnp.where(valid, held + table_rows * rank, -1)
+
+        def layer(level, carry):
+            for start in range(0, table_rows, CHUNK):
+                at = pl.ds(start, CHUNK)
+                row = lax.broadcasted_iota(jnp.int32, (CHUNK, atoms), 0) + (start + level * table_rows)
+                distance = jnp.full((CHUNK, atoms), FAR, F32)
+                for j in range(slots):
+                    distance = jnp.where(row == key_ref[j : j + 1, :], distances[j : j + 1, :], distance)
+                for h in range(heads):
+                    weight[h, at, :] += jnp.exp(-decay[h] * distance)
+            return carry
+
+        lax.fori_loop(DEPTH, jnp.max(rank) + 1, layer, 0)
 
 
 def sweep_kernel(
@@ -192,8 +211,8 @@
     return jax.ShapeDtypeStruct(shape, dtype)
 
 
-def flips(size, offset):
-    return [(i, i ^ offset) for i in range(size)]
+def pinned(shape, dtype):
+    return pltpu.VMEM(shape, dtype)
 
 
 def halvings(size):
@@ -205,37 +224,106 @@
     return offsets
 
 
-def gather_cells(shard, cells):
+def crossing(offset, crossed):
+    return offset | 1 if offset in crossed else offset
+
+
+def own_core(cells, crossed):
     place = lax.axis_index("cell")
-    offsets = halvings(cells)
-    held = shard[None]
-    for offset in offsets:
-        other = lax.ppermute(held, "cell", flips(cells, offset))
-        first = (place // offset) % 2 == 0
-        held = jnp.where(first, jnp.concatenate([held, other]), jnp.concatenate([other, held]))
-    bits = len(offsets)
-    matrices, rows, width = shard.shape
-    held = held.reshape((2,) * bits + shard.shape)
-    held = held.transpose((bits,) + tuple(reversed(range(bits))) + (bits + 1, bits + 2))
-    return held.reshape(matrices, cells * rows, width)
-
-
-def reduce_cells(parts, cells):
+    blocks = 2 * jnp.arange(cells // 2)
+    core = jnp.full((cells // 2,), place % 2)
+    for offset in crossed:
+        core = core ^ ((blocks // offset) % 2) ^ ((place // offset) % 2)
+    return core
+
+
+def swap(array, cells, vector_of):
+    return lax.ppermute(array, "cell", [(i, i ^ vector_of(i)) for i in range(cells)])
+
+
+def gather_cells(shard, cells, beside):
+    place = lax.axis_index("cell")
+    offsets = halvings(cells)[:-1]
+    far, (a, b) = offsets[:-2], offsets[-2:]
+
+    def late(i):
+        return ((i // a) ^ (i // b) ^ i) % 2
+
+    steps = [(offset, offset) for offset in far] + [(a, b), (b, a)]
+    held = shard
+    done = ()
+    for early, other in steps:
+        vectors = (crossing(early, offsets), crossing(other, offsets))
+        arrived = swap(held, cells, lambda i, vectors=vectors: vectors[late(i)])
+        if beside:
+            done = beside.pop(0)(*done)
+            arrived, done = lax.optimization_barrier((arrived, done))
+        bit = jnp.where(late(place) == 0, place // early, place // other) % 2
+        held = jnp.where(bit == 0, jnp.stack([held, arrived]), jnp.stack([arrived, held]))
+    held = jnp.where(late(place) == 0, held, jnp.swapaxes(held, 0, 1))
+    arrived = swap(held, cells, lambda i: 1)
+    count = len(offsets)
+    order = tuple(reversed(range(count))) + tuple(range(count, held.ndim))
+    held, arrived = held.transpose(order), arrived.transpose(order)
+    core = own_core(cells, offsets).reshape((2,) * count + (1,) * shard.ndim)
+    pair = [jnp.where(core == 0, held, arrived), jnp.where(core == 0, arrived, held)]
+    blocks = jnp.stack(pair, axis=count).reshape((cells,) + shard.shape)
+    return blocks.transpose(1, 0, 2, 3).reshape(shard.shape[0], -1, shard.shape[2]), done
+
+
+def reduce_all(parts, cells, bricks):
     place = lax.axis_index("cell")
     tail = parts.shape[1:]
-    for offset in reversed(halvings(cells)):
-        bit = (place // offset) % 2
-        pairs = parts.reshape((-1, 2) + tail)
-        keep = lax.dynamic_index_in_dim(pairs, bit, 1, False)
-        send = lax.dynamic_index_in_dim(pairs, 1 - bit, 1, False)
-        parts = keep + lax.ppermute(send.astype(BF16), "cell", flips(cells, offset)).astype(F32)
-    return parts[0]
-
-
-def reduce_bricks(total, bricks):
-    for offset in halvings(bricks):
-        mine = total.astype(BF16)
-        total = mine.astype(F32) + lax.ppermute(mine, "brick", flips(bricks, offset)).astype(F32)
+    left = halvings(cells)[:-1]
+    near, middle, farthest = left[-2:], left[1:-2], left[0]
+    crossed = [near[0], *middle, farthest]
+    parts = parts.reshape((cells // 2, 2) + tail)
+    core = own_core(cells, crossed).reshape((cells // 2,) + (1,) * len(tail))
+    keep = jnp.where(core == 0, parts[:, 0], parts[:, 1])
+    send = jnp.where(core == 0, parts[:, 1], parts[:, 0])
+    total = keep + swap(send.astype(BF16), cells, lambda i: 1).astype(F32)
+    total = total.reshape((2,) * len(left) + tail)
+
+    def portion(array, flipped):
+        for offset, flip in reversed(flipped):
+            bit = (place // offset) % 2
+            array = lax.dynamic_index_in_dim(array, 1 - bit if flip else bit, left.index(offset), False)
+        return array
+
+    def exchange(group):
+        nonlocal total, left
+        mine = portion(total, [(offset, 0) for offset in group])
+        for step in range(1, 1 << len(group)):
+            flipped = [(offset, step >> k & 1) for k, offset in enumerate(group)]
+            vector = 0
+            for offset, flip in flipped:
+                vector ^= crossing(offset, crossed) * flip
+            sent = portion(total, flipped).astype(BF16)
+            mine = mine + swap(sent, cells, lambda i, vector=vector: vector).astype(F32)
+        total = mine
+        left = [offset for offset in left if offset not in group]
+
+    exchange(near)
+    for offset in reversed(middle):
+        exchange([offset])
+
+    def meet(array, vector, step):
+        pairs = [
+            (cell * bricks + brick, (cell ^ vector) * bricks + (brick ^ step))
+            for cell in range(cells)
+            for brick in range(bricks)
+        ]
+        return lax.ppermute(array, ("cell", "brick"), pairs).astype(F32)
+
+    vector = crossing(farthest, crossed)
+    keep = portion(total, [(farthest, 0)]).astype(BF16)
+    send = portion(total, [(farthest, 1)]).astype(BF16)
+    total = keep.astype(F32) + meet(send, vector, 0)
+    if bricks > 1:
+        total = total + (meet(keep, 0, 1) + meet(send, vector, 1))
+    for step in list(reversed(halvings(bricks)))[1:]:
+        keep = total.astype(BF16)
+        total = keep.astype(F32) + meet(keep, 0, step)
     return total
 
 
@@ -263,38 +351,43 @@
     heads = head_decay.shape[0]
     table_rows = atoms + bricks * ghost_slots
 
-    weights = gather_cells(master.astype(BF16), cells)
-
-    embedded, normed, normed_t, parcel = pl.pallas_call(
-        embed_kernel,
-        out_shape=(
-            struct((atoms, width), F32),
-            struct((atoms, width), BF16),
-            struct((width, atoms), BF16),
-            struct((bricks, ghost_slots, width), BF16),
-        ),
-        in_specs=vmem(5),
-        out_specs=tuple(vmem(4)),
-        name="embed",
-    )(features[0, 0], species[0], species_table, norm_gain[None], send_lists[0, 0])
-
-    brick = lax.axis_index("brick")
-    ghosts = parcel
-    for offset in range(1, bricks):
-        peer = brick ^ offset
-        sent = lax.dynamic_index_in_dim(parcel, peer, 0, True)
-        arrived = lax.ppermute(sent, "brick", flips(bricks, offset))
-        ghosts = lax.dynamic_update_slice_in_dim(ghosts, arrived, peer, 0)
-    ghosts = ghosts.reshape(bricks * ghost_slots, width)
-
-    weight, absent = pl.pallas_call(
-        index_kernel,
-        out_shape=(struct((heads, table_rows, atoms), F32), struct((table_rows, atoms), F32)),
-        in_specs=[SMEM] + vmem(3),
-        out_specs=tuple(vmem(2)),
-        scratch_shapes=[pltpu.VMEM((slots, atoms), jnp.int32)],
-        name="index",
-    )(head_decay, neighbours[0, 0], counts[0], distances[0, 0])
+    def embed():
+        return pl.pallas_call(
+            embed_kernel,
+            out_shape=(
+                pinned((atoms, width), F32),
+                pinned((atoms, width), BF16),
+                pinned((width, atoms), BF16),
+                pinned((bricks, ghost_slots, width), BF16),
+            ),
+            in_specs=vmem(5),
+            out_specs=tuple(vmem(4)),
+            name="embed",
+        )(features[0, 0], species[0], species_table, norm_gain[None], send_lists[0, 0])
+
+    def exchange(embedded, normed, normed_t, parcel):
+        brick = lax.axis_index("brick")
+        ghosts = parcel
+        for offset in range(1, bricks):
+            peer = brick ^ offset
+            sent = lax.dynamic_index_in_dim(parcel, peer, 0, True)
+            arrived = lax.ppermute(sent, "brick", [(i, i ^ offset) for i in range(bricks)])
+            ghosts = lax.dynamic_update_slice_in_dim(ghosts, arrived, peer, 0)
+        return embedded, normed, normed_t, ghosts.reshape(bricks * ghost_slots, width)
+
+    def index(*done):
+        where = lax.optimization_barrier((done, neighbours))[1]
+        return done + pl.pallas_call(
+            index_kernel,
+            out_shape=(pinned((heads, table_rows, atoms), F32), pinned((table_rows, atoms), F32)),
+            in_specs=[SMEM] + vmem(3),
+            out_specs=tuple(vmem(2)),
+            scratch_shapes=[pltpu.VMEM((slots, atoms), jnp.int32)],
+            name="index",
+        )(head_decay, where[0, 0], counts[0], distances[0, 0])
+
+    weights, done = gather_cells(master.astype(BF16), cells, [embed, exchange, index])
+    embedded, normed, normed_t, ghosts, weight, absent = done
 
     columns = heads * atoms
     energies, grads = pl.pallas_call(
@@ -313,7 +406,7 @@
     )(weights, normed, normed_t, ghosts, embedded, weight, absent, readout[None], targets[0])
 
     parts = grads.reshape(4, cells, width // cells, width).transpose(1, 0, 2, 3)
-    owned = reduce_bricks(reduce_cells(parts, cells), bricks)
+    owned = reduce_all(parts, cells, bricks)
     moment_new = 0.9 * moment + 0.1 * owned
     second_new = 0.999 * second + 0.001 * owned * owned
     adam_step = moment_new / (jnp.sqrt(second_new) + 1e-08)

time: 52 us -> 42.5 us (0.82)
  waiting for transfers between devices: 21.7 us -> 14 us
  Pallas kernels: 9.11 us -> 7.17 us
  local copies, waits for them, and re-layouts: 2.07 us -> 0.87 us
    ppermute x10 -> x12, waiting for transfers between devices: 21.7 us -> 14 us  [the longest x8 9.06 us: swap(): lax.ppermute(array, 'cell', [(i, i ^ vector_of(i)) for i in range(cells)])]
    pallas_call x2, Pallas kernels: 6.41 us -> 4.47 us  [the longest x1 3.26 us: index(): pl.pallas_call(index_kernel, out_shape=(pinned((heads, table_rows, atoms)...]
    convert_element_type x1 -> x2, other arithmetic: 0.01 us -> 1.02 us  [the longest x1 0.91 us: body(): master.astype(BF16)]
    broadcast_in_dim x1 -> x0, other arithmetic: 0.85 us -> none  [gather_cells(): held = shard[None]]
    dynamic_slice x1, local copies, waits for them, and re-layouts: 0.72 us -> 0.01 us  [exchange(): sent = lax.dynamic_index_in_dim(parcel, peer, 0, True)]
    ppermute x10 -> x12, starting transfers between devices: 16.2 us -> 16.6 us  [the longest x8 9.85 us: swap(): lax.ppermute(array, 'cell', [(i, i ^ vector_of(i)) for i in range(cells)])]
    unnamed x20 -> x10, local copies, waits for them, and re-layouts: 1.1 us -> 0.69 us
  transfers between devices with their start and end apart: 10 -> 12, of which waited for: 8 -> 11; matrix products, arithmetic and copies ran while one was open for 1% -> 0% of each run, Pallas kernels for 12% -> 11%
where the time goes in v3:
time: 42.5 us; the launch traced here: 41.8 us
  starting transfers between devices  16.6 us (39%)
  waiting for transfers between devices  14 us (33%)
  Pallas kernels  7.17 us (17%)
  other arithmetic  2.26 us (5%)
  between operations  0.95 us (2%)
  local copies, waits for them, and re-layouts  0.87 us (2%)
    ppermute x8, starting transfers between devices, swap(): lax.ppermute(array, 'cell', [(i, i ^ vector_of(i)) for i in range(cells)])  9.85 us
    ppermute x8, waiting for transfers between devices, swap(): lax.ppermute(array, 'cell', [(i, i ^ vector_of(i)) for i in range(cells)])  9.06 us
    ppermute x3, starting transfers between devices, meet(): return lax.ppermute(array, ('cell', 'brick'), pairs).astype(F32)  4.68 us
    ppermute x3, waiting for transfers between devices, meet(): return lax.ppermute(array, ('cell', 'brick'), pairs).astype(F32)  4.28 us
    pallas_call x1, Pallas kernels, index(): pl.pallas_call(index_kernel, out_shape=(pinned((heads, table_rows, atoms)...  3.26 us
    pallas_call x1, Pallas kernels, body(): pl.pallas_call(sweep_kernel, out_shape=(struct((1, atoms), F32), struct((...  2.69 us
    ppermute x1, starting transfers between devices, exchange(): lax.ppermute(sent, 'brick', [(i, i ^ offset) for i in range(bricks)])  2.09 us
    pallas_call x1, Pallas kernels, embed(): pl.pallas_call(embed_kernel, out_shape=(pinned((atoms, width), F32), pinn...  1.21 us
  transfers between devices with their start and end apart: 12, of which 11 were waited for; matrix products, arithmetic and copies ran while one was open for 0% of the time, Pallas kernels for 11%

profile of v3, /device:TPU:0, one launch (start us, length us, event | category | flops | bytes accessed | tf_op | source)
XLA Modules:
  0.0 41.8 jit_solution(1118267735686580204)
XLA Ops:
  0.6 0.0 copy-start.2
  0.6 0.9 %convert_element_type.60 = bf16[4,16,256]{2,1,0:T(8,128)(2,1)S(1)} convert(f32[4,16,256]{2,1,0:T(8,128)} %param.25) | non-fusion elementwise | flops 16384 | bytes 98304 | tf_op jit(solution)/shard_map/convert_element_type | solution.py:389
  1.6 3.5 %collective-permute-start = (bf16[4,16,256]{2,1,0:T(8,128)(2,1)S(1)}, bf16[4,16,256]{2,1,0:T(8,128)(2,1)S(1)}, u32[]{:S(2)}, u32[]{:S(2)}) collective-permute-start(bf16[4,16,256]{2,1,0:T(8,128)(2,1)S(1)} %convert_element_type.60), channel_id=1, source_target_pairs={{0,18},{2,16},{4,22},{6,20},{8,26},{10,24},{12,30},{14,28},{16,2},... | collective-permute-start | bytes 98312 | tf_op jit(solution)/shard_map/ppermute | solution.py:241
  5.0 0.0 copy-done.2
  5.2 1.2 %embed.1 = (f32[128,256]{1,0:T(8,128)S(1)}, bf16[128,256]{1,0:T(8,128)(2,1)S(1)}, bf16[256,128]{1,0:T(8,128)(2,1)S(1)}, bf16[2,32,256]{2,1,0:T(8,128)(2,1)S(1)}) custom-call(bf16[128,256]{1,0:T(8,128)(2,1)} %bitcast.119, s32[1,128]{1,0:T(1,128)} %bitcast.124, bf16[4,256]{1,0:T(4,128)(2,1)} %species_table.1, f32[1,256]{1,0:T(1,128)} %bitcast.122, ...), custom_call_target="tpu_custom_call" | custom-call | tf_op jit(solution)/shard_map/embed/pallas_call | solution.py:355
  6.4 0.4 collective-permute-done
  6.9 2.1 %collective-permute-start.2 = (bf16[1,32,256]{2,1,0:T(8,128)(2,1)S(1)}, bf16[1,32,256]{2,1,0:T(8,128)(2,1)S(1)}, u32[]{:S(2)}, u32[]{:S(2)}) collective-permute-start(bf16[1,32,256]{2,1,0:T(8,128)(2,1)S(1)} %constant_dynamic-slice_fusion), channel_id=1, source_target_pairs={{0,1},{1,0},{2,3},{3,2},{4,5},{5,4},{6,7},{7,6},{8,9},{9,8},{10,11... | collective-permute-start | bytes 49160 | tf_op jit(solution)/shard_map/ppermute | solution.py:374
  9.0 1.1 %collective-permute-start.1 = (bf16[2,4,16,256]{3,2,1,0:T(8,128)(2,1)S(1)}, bf16[2,4,16,256]{3,2,1,0:T(8,128)(2,1)S(1)}, u32[]{:S(2)}, u32[]{:S(2)}) collective-permute-start(bf16[2,4,16,256]{3,2,1,0:T(8,128)(2,1)S(1)} %maximum_select_fusion.2), channel_id=1, source_target_pairs={{0,10},{2,4},{4,2},{6,12},{8,14},{10,0},{12,6},{14,8},{16,26},{18,... | collective-permute-start | bytes 196616 | tf_op jit(solution)/shard_map/ppermute | solution.py:241
  10.0 0.6 %collective-permute-done.2 = bf16[1,32,256]{2,1,0:T(8,128)(2,1)S(1)} collective-permute-done((bf16[1,32,256]{2,1,0:T(8,128)(2,1)S(1)}, bf16[1,32,256]{2,1,0:T(8,128)(2,1)S(1)}, u32[]{:S(2)}, u32[]{:S(2)}) %collective-permute-start.2) | collective-permute-done | bytes 16416 | tf_op jit(solution)/shard_map/ppermute | solution.py:374
  10.7 2.0 %collective-permute-done.1 = bf16[2,4,16,256]{3,2,1,0:T(8,128)(2,1)S(1)} collective-permute-done((bf16[2,4,16,256]{3,2,1,0:T(8,128)(2,1)S(1)}, bf16[2,4,16,256]{3,2,1,0:T(8,128)(2,1)S(1)}, u32[]{:S(2)}, u32[]{:S(2)}) %collective-permute-start.1) | collective-permute-done | bytes 65568 | tf_op jit(solution)/shard_map/ppermute | solution.py:241
  12.7 1.3 %collective-permute-start.3 = (bf16[2,2,4,16,256]{4,3,2,0,1:T(8,128)(2,1)S(1)}, bf16[2,2,4,16,256]{4,3,2,0,1:T(8,128)(2,1)S(1)}, u32[]{:S(2)}, u32[]{:S(2)}) collective-permute-start(bf16[2,2,4,16,256]{4,3,2,0,1:T(8,128)(2,1)S(1)} %maximum_select_fusion.1), channel_id=1, source_target_pairs={{0,6},{2,8},{4,14},{6,0},{8,2},{10,12},{12,10},{14,4},{16,22},{18,... | collective-permute-start | bytes 393224 | tf_op jit(solution)/shard_map/ppermute | solution.py:241
  14.1 3.3 %index.1 = (f32[8,192,128]{2,1,0:T(8,128)S(1)}, f32[192,128]{1,0:T(8,128)S(1)}) custom-call(f32[8]{0:T(128)} %decay.1, s32[64,128]{1,0:T(8,128)} %bitcast.120, s32[1,128]{1,0:T(1,128)} %bitcast.125, f32[64,128]{1,0:T(8,128)} %bitcast.121), custom_call_target="tpu_custom_call" | custom-call | tf_op jit(solution)/shard_map/index/pallas_call | solution.py:380
  17.4 0.0 collective-permute-done.3
  17.4 0.5 %collective-permute-start.4 = (bf16[2,2,2,4,16,256]{5,4,3,0,1,2:T(8,128)(2,1)S(1)}, bf16[2,2,2,4,16,256]{5,4,3,0,1,2:T(8,128)(2,1)S(1)}, u32[]{:S(2)}, u32[]{:S(2)}) collective-permute-start(bf16[2,2,2,4,16,256]{5,4,3,0,1,2:T(8,128)(2,1)S(1)} %bitcast_select_fusion.2), channel_id=1, source_target_pairs={{0,2},{2,0},{4,6},{6,4},{8,10},{10,8},{12,14},{14,12},{16,18},{18,... | collective-permute-start | bytes 786440 | tf_op jit(solution)/shard_map/ppermute | solution.py:241
  18.0 1.1 %collective-permute-done.4 = bf16[2,2,2,4,16,256]{5,4,3,0,1,2:T(8,128)(2,1)S(1)} collective-permute-done((bf16[2,2,2,4,16,256]{5,4,3,0,1,2:T(8,128)(2,1)S(1)}, bf16[2,2,2,4,16,256]{5,4,3,0,1,2:T(8,128)(2,1)S(1)}, u32[]{:S(2)}, u32[]{:S(2)}) %collective-permute-start.4) | collective-permute-done | bytes 262176 | tf_op jit(solution)/shard_map/ppermute | solution.py:241
  19.1 0.1 fusion
  19.2 0.1 pad_maximum_fusion
  19.3 0.0 copy-start
  19.3 0.0 copy-start.1
  19.4 0.7 %copy-done = f32[256]{0:T(256)S(1)} copy-done((f32[256]{0:T(256)S(1)}, f32[256]{0:T(256)}, u32[]{:S(2)}) %copy-start) | copy-done | bytes 1048
  20.0 0.0 copy-done.1
  20.0 2.7 %sweep.1 = (f32[1,128]{1,0:T(1,128)}, f32[4,256,256]{2,1,0:T(8,128)S(1)}) custom-call(bf16[4,256,256]{2,1,0:T(8,128)(2,1)S(1)} %bitcast.104, bf16[128,256]{1,0:T(8,128)(2,1)S(1)} %get-tuple-element.48.normed, bf16[256,128]{1,0:T(8,128)(2,1)S(1)} %get-tuple-element.49.normed_t, bf16[64,256]{1,0:T(8,128)(2,1)S(1)} %bitcast.105, ...), custom_call_target="tpu_custom_call" | custom-call | tf_op jit(solution)/shard_map/sweep/pallas_call | solution.py:393
  22.7 0.1 copy.36
  22.8 0.1 select_convert_fusion
  22.9 0.4 %collective-permute-start.5 = (bf16[8,4,16,256]{3,2,1,0:T(8,128)(2,1)S(1)}, bf16[8,4,16,256]{3,2,1,0:T(8,128)(2,1)S(1)}, u32[]{:S(2)}, u32[]{:S(2)}) collective-permute-start(bf16[8,4,16,256]{3,2,1,0:T(8,128)(2,1)S(1)} %select_convert_fusion), channel_id=1, source_target_pairs={{0,2},{2,0},{4,6},{6,4},{8,10},{10,8},{12,14},{14,12},{16,18},{18,... | collective-permute-start | bytes 786440 | tf_op jit(solution)/shard_map/ppermute | solution.py:241
  23.4 1.2 %collective-permute-done.5 = bf16[8,4,16,256]{3,2,1,0:T(8,128)(2,1)S(1)} collective-permute-done((bf16[8,4,16,256]{3,2,1,0:T(8,128)(2,1)S(1)}, bf16[8,4,16,256]{3,2,1,0:T(8,128)(2,1)S(1)}, u32[]{:S(2)}, u32[]{:S(2)}) %collective-permute-start.5) | collective-permute-done | bytes 262176 | tf_op jit(solution)/shard_map/ppermute | solution.py:241
  24.5 0.1 convert_add_fusion
  24.7 2.1 %collective-permute-start.8 = (bf16[2,4,16,256]{3,2,1,0:T(8,128)(2,1)S(1)}, bf16[2,4,16,256]{3,2,1,0:T(8,128)(2,1)S(1)}, u32[]{:S(2)}, u32[]{:S(2)}) collective-permute-start(bf16[2,4,16,256]{3,2,1,0:T(8,128)(2,1)S(1)} %get-tuple-element.62), channel_id=1, source_target_pairs={{0,14},{2,12},{4,10},{6,8},{8,6},{10,4},{12,2},{14,0},{16,30},{18,... | collective-permute-start | bytes 196616 | tf_op jit(solution)/shard_map/ppermute | solution.py:241
  26.8 0.9 %collective-permute-start.7 = (bf16[2,4,16,256]{3,2,1,0:T(8,128)(2,1)S(1)}, bf16[2,4,16,256]{3,2,1,0:T(8,128)(2,1)S(1)}, u32[]{:S(2)}, u32[]{:S(2)}) collective-permute-start(bf16[2,4,16,256]{3,2,1,0:T(8,128)(2,1)S(1)} %get-tuple-element.63), channel_id=1, source_target_pairs={{0,4},{2,6},{4,0},{6,2},{8,12},{10,14},{12,8},{14,10},{16,20},{18,... | collective-permute-start | bytes 196616 | tf_op jit(solution)/shard_map/ppermute | solution.py:241
  27.7 0.0 collective-permute-start.6
  27.7 1.9 %collective-permute-done.8 = bf16[2,4,16,256]{3,2,1,0:T(8,128)(2,1)S(1)} collective-permute-done((bf16[2,4,16,256]{3,2,1,0:T(8,128)(2,1)S(1)}, bf16[2,4,16,256]{3,2,1,0:T(8,128)(2,1)S(1)}, u32[]{:S(2)}, u32[]{:S(2)}) %collective-permute-start.8) | collective-permute-done | bytes 65568 | tf_op jit(solution)/shard_map/ppermute | solution.py:241
  29.6 1.9 %collective-permute-done.7 = bf16[2,4,16,256]{3,2,1,0:T(8,128)(2,1)S(1)} collective-permute-done((bf16[2,4,16,256]{3,2,1,0:T(8,128)(2,1)S(1)}, bf16[2,4,16,256]{3,2,1,0:T(8,128)(2,1)S(1)}, u32[]{:S(2)}, u32[]{:S(2)}) %collective-permute-start.7) | collective-permute-done | bytes 65568 | tf_op jit(solution)/shard_map/ppermute | solution.py:241
  31.5 0.6 %collective-permute-done.6 = bf16[2,4,16,256]{3,2,1,0:T(8,128)(2,1)S(1)} collective-permute-done((bf16[2,4,16,256]{3,2,1,0:T(8,128)(2,1)S(1)}, bf16[2,4,16,256]{3,2,1,0:T(8,128)(2,1)S(1)}, u32[]{:S(2)}, u32[]{:S(2)}) %collective-permute-start.6) | collective-permute-done | bytes 65568 | tf_op jit(solution)/shard_map/ppermute | solution.py:241
  32.1 0.0 copy-start.3
  32.1 0.0 copy-start.4
  32.2 3.5 %collective-permute-start.11 = (bf16[4,16,256]{2,1,0:T(8,128)(2,1)S(1)}, bf16[4,16,256]{2,1,0:T(8,128)(2,1)S(1)}, u32[]{:S(2)}, u32[]{:S(2)}) collective-permute-start(bf16[4,16,256]{2,1,0:T(8,128)(2,1)S(1)} %get-tuple-element.67), channel_id=1, source_target_pairs={{0,19},{1,18},{2,17},{3,16},{4,23},{5,22},{6,21},{7,20},{8,27},{9,... | collective-permute-start | bytes 98312 | tf_op jit(solution)/shard_map/ppermute | solution.py:316
  35.7 1.2 %collective-permute-start.10 = (bf16[4,16,256]{2,1,0:T(8,128)(2,1)S(1)}, bf16[4,16,256]{2,1,0:T(8,128)(2,1)S(1)}, u32[]{:S(2)}, u32[]{:S(2)}) collective-permute-start(bf16[4,16,256]{2,1,0:T(8,128)(2,1)S(1)} %get-tuple-element.66), channel_id=1, source_target_pairs={{0,1},{1,0},{2,3},{3,2},{4,5},{5,4},{6,7},{7,6},{8,9},{9,8},{10,11... | collective-permute-start | bytes 98312 | tf_op jit(solution)/shard_map/ppermute | solution.py:316
  36.8 0.0 collective-permute-start.9
  36.8 0.5 %collective-permute-done.11 = bf16[4,16,256]{2,1,0:T(8,128)(2,1)S(1)} collective-permute-done((bf16[4,16,256]{2,1,0:T(8,128)(2,1)S(1)}, bf16[4,16,256]{2,1,0:T(8,128)(2,1)S(1)}, u32[]{:S(2)}, u32[]{:S(2)}) %collective-permute-start.11) | collective-permute-done | bytes 32800 | tf_op jit(solution)/shard_map/ppermute | solution.py:316
  37.4 2.2 %collective-permute-done.10 = bf16[4,16,256]{2,1,0:T(8,128)(2,1)S(1)} collective-permute-done((bf16[4,16,256]{2,1,0:T(8,128)(2,1)S(1)}, bf16[4,16,256]{2,1,0:T(8,128)(2,1)S(1)}, u32[]{:S(2)}, u32[]{:S(2)}) %collective-permute-start.10) | collective-permute-done | bytes 32800 | tf_op jit(solution)/shard_map/ppermute | solution.py:316
  39.6 1.5 %collective-permute-done.9 = bf16[4,16,256]{2,1,0:T(8,128)(2,1)S(1)} collective-permute-done((bf16[4,16,256]{2,1,0:T(8,128)(2,1)S(1)}, bf16[4,16,256]{2,1,0:T(8,128)(2,1)S(1)}, u32[]{:S(2)}, u32[]{:S(2)}) %collective-permute-start.9) | collective-permute-done | bytes 32800 | tf_op jit(solution)/shard_map/ppermute | solution.py:316
  41.1 0.0 copy-done.3
  41.1 0.0 copy-done.4
  41.1 0.7 %add_divide_fusion = (f32[4,16,256]{2,1,0:T(8,128)}, f32[4,16,256]{2,1,0:T(8,128)}, f32[4,16,256]{2,1,0:T(8,128)}) fusion(bf16[4,16,256]{2,1,0:T(8,128)(2,1)S(1)} %collective-permute-done.11, bf16[4,16,256]{2,1,0:T(8,128)(2,1)S(1)} %collective-permute-done.10, bf16[4,16,256]{2,1,0:T(8,128)(2,1)S(1)} %collective-permute-done.9, ...), kind=kLoop, calls=%fused_computation.30 | loop fusion | flops 262144 | bytes 458752 | tf_op jit(solution)/shard_map/div | solution.py:412
  (18 shorter events, 0.3 us)
Async XLA Ops:
  0.6 4.4 %copy-start.2 = (f32[4,16,256]{2,1,0:T(8,128)S(1)}, f32[4,16,256]{2,1,0:T(8,128)}, u32[]{:S(2)}) copy-start(f32[4,16,256]{2,1,0:T(8,128)} %param.25) | copy-start | bytes 196612
  1.6 5.3 %collective-permute-start = (bf16[4,16,256]{2,1,0:T(8,128)(2,1)S(1)}, bf16[4,16,256]{2,1,0:T(8,128)(2,1)S(1)}, u32[]{:S(2)}, u32[]{:S(2)}) collective-permute-start(bf16[4,16,256]{2,1,0:T(8,128)(2,1)S(1)} %convert_element_type.60), channel_id=1, source_target_pairs={{0,18},{2,16},{4,22},{6,20},{8,26},{10,24},{12,30},{14,28},{16,2},... | collective-permute-start | bytes 98312 | tf_op jit(solution)/shard_map/ppermute | solution.py:241
  6.9 3.8 %collective-permute-start.2 = (bf16[1,32,256]{2,1,0:T(8,128)(2,1)S(1)}, bf16[1,32,256]{2,1,0:T(8,128)(2,1)S(1)}, u32[]{:S(2)}, u32[]{:S(2)}) collective-permute-start(bf16[1,32,256]{2,1,0:T(8,128)(2,1)S(1)} %constant_dynamic-slice_fusion), channel_id=1, source_target_pairs={{0,1},{1,0},{2,3},{3,2},{4,5},{5,4},{6,7},{7,6},{8,9},{9,8},{10,11... | collective-permute-start | bytes 49160 | tf_op jit(solution)/shard_map/ppermute | solution.py:374
  9.0 3.8 %collective-permute-start.1 = (bf16[2,4,16,256]{3,2,1,0:T(8,128)(2,1)S(1)}, bf16[2,4,16,256]{3,2,1,0:T(8,128)(2,1)S(1)}, u32[]{:S(2)}, u32[]{:S(2)}) collective-permute-start(bf16[2,4,16,256]{3,2,1,0:T(8,128)(2,1)S(1)} %maximum_select_fusion.2), channel_id=1, source_target_pairs={{0,10},{2,4},{4,2},{6,12},{8,14},{10,0},{12,6},{14,8},{16,26},{18,... | collective-permute-start | bytes 196616 | tf_op jit(solution)/shard_map/ppermute | solution.py:241
  12.7 4.6 %collective-permute-start.3 = (bf16[2,2,4,16,256]{4,3,2,0,1:T(8,128)(2,1)S(1)}, bf16[2,2,4,16,256]{4,3,2,0,1:T(8,128)(2,1)S(1)}, u32[]{:S(2)}, u32[]{:S(2)}) collective-permute-start(bf16[2,2,4,16,256]{4,3,2,0,1:T(8,128)(2,1)S(1)} %maximum_select_fusion.1), channel_id=1, source_target_pairs={{0,6},{2,8},{4,14},{6,0},{8,2},{10,12},{12,10},{14,4},{16,22},{18,... | collective-permute-start | bytes 393224 | tf_op jit(solution)/shard_map/ppermute | solution.py:241
  17.4 1.7 %collective-permute-start.4 = (bf16[2,2,2,4,16,256]{5,4,3,0,1,2:T(8,128)(2,1)S(1)}, bf16[2,2,2,4,16,256]{5,4,3,0,1,2:T(8,128)(2,1)S(1)}, u32[]{:S(2)}, u32[]{:S(2)}) collective-permute-start(bf16[2,2,2,4,16,256]{5,4,3,0,1,2:T(8,128)(2,1)S(1)} %bitcast_select_fusion.2), channel_id=1, source_target_pairs={{0,2},{2,0},{4,6},{6,4},{8,10},{10,8},{12,14},{14,12},{16,18},{18,... | collective-permute-start | bytes 786440 | tf_op jit(solution)/shard_map/ppermute | solution.py:241
  19.3 0.7 %copy-start = (f32[256]{0:T(256)S(1)}, f32[256]{0:T(256)}, u32[]{:S(2)}) copy-start(f32[256]{0:T(256)} %param.23) | copy-start | bytes 3076
  19.3 0.7 %copy-start.1 = (f32[1,1,128]{2,1,0:T(1,128)S(1)}, f32[1,1,128]{2,1,0:T(1,128)}, u32[]{:S(2)}) copy-start(f32[1,1,128]{2,1,0:T(1,128)} %param.24) | copy-start | bytes 1540
  22.9 1.6 %collective-permute-start.5 = (bf16[8,4,16,256]{3,2,1,0:T(8,128)(2,1)S(1)}, bf16[8,4,16,256]{3,2,1,0:T(8,128)(2,1)S(1)}, u32[]{:S(2)}, u32[]{:S(2)}) collective-permute-start(bf16[8,4,16,256]{3,2,1,0:T(8,128)(2,1)S(1)} %select_convert_fusion), channel_id=1, source_target_pairs={{0,2},{2,0},{4,6},{6,4},{8,10},{10,8},{12,14},{14,12},{16,18},{18,... | collective-permute-start | bytes 786440 | tf_op jit(solution)/shard_map/ppermute | solution.py:241
  24.7 4.9 %collective-permute-start.8 = (bf16[2,4,16,256]{3,2,1,0:T(8,128)(2,1)S(1)}, bf16[2,4,16,256]{3,2,1,0:T(8,128)(2,1)S(1)}, u32[]{:S(2)}, u32[]{:S(2)}) collective-permute-start(bf16[2,4,16,256]{3,2,1,0:T(8,128)(2,1)S(1)} %get-tuple-element.62), channel_id=1, source_target_pairs={{0,14},{2,12},{4,10},{6,8},{8,6},{10,4},{12,2},{14,0},{16,30},{18,... | collective-permute-start | bytes 196616 | tf_op jit(solution)/shard_map/ppermute | solution.py:241
  26.8 4.7 %collective-permute-start.7 = (bf16[2,4,16,256]{3,2,1,0:T(8,128)(2,1)S(1)}, bf16[2,4,16,256]{3,2,1,0:T(8,128)(2,1)S(1)}, u32[]{:S(2)}, u32[]{:S(2)}) collective-permute-start(bf16[2,4,16,256]{3,2,1,0:T(8,128)(2,1)S(1)} %get-tuple-element.63), channel_id=1, source_target_pairs={{0,4},{2,6},{4,0},{6,2},{8,12},{10,14},{12,8},{14,10},{16,20},{18,... | collective-permute-start | bytes 196616 | tf_op jit(solution)/shard_map/ppermute | solution.py:241
  27.7 4.3 %collective-permute-start.6 = (bf16[2,4,16,256]{3,2,1,0:T(8,128)(2,1)S(1)}, bf16[2,4,16,256]{3,2,1,0:T(8,128)(2,1)S(1)}, u32[]{:S(2)}, u32[]{:S(2)}) collective-permute-start(bf16[2,4,16,256]{3,2,1,0:T(8,128)(2,1)S(1)} %get-tuple-element.61), channel_id=1, source_target_pairs={{0,10},{2,8},{4,14},{6,12},{8,2},{10,0},{12,6},{14,4},{16,26},{18,... | collective-permute-start | bytes 196616 | tf_op jit(solution)/shard_map/ppermute | solution.py:241
  32.1 9.0 %copy-start.3 = (f32[4,16,256]{2,1,0:T(8,128)S(1)}, f32[4,16,256]{2,1,0:T(8,128)}, u32[]{:S(2)}) copy-start(f32[4,16,256]{2,1,0:T(8,128)} %param.27) | copy-start | bytes 196612
  32.1 9.0 %copy-start.4 = (f32[4,16,256]{2,1,0:T(8,128)S(1)}, f32[4,16,256]{2,1,0:T(8,128)}, u32[]{:S(2)}) copy-start(f32[4,16,256]{2,1,0:T(8,128)} %param.26) | copy-start | bytes 196612
  32.2 5.2 %collective-permute-start.11 = (bf16[4,16,256]{2,1,0:T(8,128)(2,1)S(1)}, bf16[4,16,256]{2,1,0:T(8,128)(2,1)S(1)}, u32[]{:S(2)}, u32[]{:S(2)}) collective-permute-start(bf16[4,16,256]{2,1,0:T(8,128)(2,1)S(1)} %get-tuple-element.67), channel_id=1, source_target_pairs={{0,19},{1,18},{2,17},{3,16},{4,23},{5,22},{6,21},{7,20},{8,27},{9,... | collective-permute-start | bytes 98312 | tf_op jit(solution)/shard_map/ppermute | solution.py:316
  35.7 3.9 %collective-permute-start.10 = (bf16[4,16,256]{2,1,0:T(8,128)(2,1)S(1)}, bf16[4,16,256]{2,1,0:T(8,128)(2,1)S(1)}, u32[]{:S(2)}, u32[]{:S(2)}) collective-permute-start(bf16[4,16,256]{2,1,0:T(8,128)(2,1)S(1)} %get-tuple-element.66), channel_id=1, source_target_pairs={{0,1},{1,0},{2,3},{3,2},{4,5},{5,4},{6,7},{7,6},{8,9},{9,8},{10,11... | collective-permute-start | bytes 98312 | tf_op jit(solution)/shard_map/ppermute | solution.py:316
  36.8 4.3 %collective-permute-start.9 = (bf16[4,16,256]{2,1,0:T(8,128)(2,1)S(1)}, bf16[4,16,256]{2,1,0:T(8,128)(2,1)S(1)}, u32[]{:S(2)}, u32[]{:S(2)}) collective-permute-start(bf16[4,16,256]{2,1,0:T(8,128)(2,1)S(1)} %get-tuple-element.67), channel_id=1, source_target_pairs={{0,18},{1,19},{2,16},{3,17},{4,22},{5,23},{6,20},{7,21},{8,26},{9,... | collective-permute-start | bytes 98312 | tf_op jit(solution)/shard_map/ppermute | solution.py:316

commit v4 on v3

--- a/solution.py
+++ b/solution.py
@@ -11,6 +11,7 @@
 CHUNK = 32
 DEPTH = 5
 FAR = 1e30
+FAR_ROW = 1 << 20
 
 loss_weight = 0.0625
 epsilon_norm = 1e-06
@@ -45,7 +46,11 @@
     return jnp.sum(jnp.where(eye, column, jnp.zeros_like(column)), axis=0, keepdims=True)
 
 
-def embed_kernel(features, species, species_table, norm_gain, send_rows, embedded, normed, normed_t, parcel):
+def embed_kernel(features, species, species_table, norm_gain, send_rows, *refs):
+    count = (len(refs) - 4) // 2
+    embedded, normed, normed_t, parcel = refs[count : count + 4]
+    for source, target in zip(refs[:count], refs[count + 4 :]):
+        target[...] = source[...]
     atoms = features.shape[0]
     kinds = species_table.shape[0]
     column = to_column(species[...])
@@ -68,13 +73,14 @@
         parcel[brick] = dot_tn(picks, half).astype(BF16)
 
 
-def index_kernel(decay, neighbours, counts, distances, weight, absent, key_ref):
+def index_kernel(first, neighbours, counts, distances, decay, weight, absent, key_ref):
     slots, atoms = neighbours.shape
     heads, table_rows = weight.shape[:2]
     slot = lax.broadcasted_iota(jnp.int32, (slots, atoms), 0)
     valid = slot < counts[...]
-    held = jnp.where(valid, neighbours[...], -1 - slot)
+    held = jnp.where(valid, neighbours[...] - first, -FAR_ROW - slot)
     key_ref[...] = held
+    slope = [-decay[:, h : h + 1] for h in range(heads)]
 
     def chunk(step, nearest):
         start = pl.multiple_of(step * CHUNK, CHUNK)
@@ -88,7 +94,7 @@
                 entering, layers[k] = layers[k], jnp.where(hit, entering, layers[k])
         absent[at, :] = jnp.where(layers[0] < FAR, 0.0, -FAR)
         for h in range(heads):
-            weight[h, at, :] = sum(jnp.exp(-decay[h] * layer) for layer in layers)
+            weight[h, at, :] = sum(jnp.exp(slope[h] * layer) for layer in layers)
         return jnp.minimum(nearest, jnp.min(layers[-1], axis=0, keepdims=True))
 
     nearest = lax.fori_loop(0, table_rows // CHUNK, chunk, jnp.full((1, atoms), FAR, F32))
@@ -98,7 +104,8 @@
         rank = jnp.zeros((slots, atoms), jnp.int32)
         for j in range(slots):
             rank += ((held == key_ref[j : j + 1, :]) & (slot < j)).astype(jnp.int32)
-        key_ref[...] = jnp.where(valid, held + table_rows * rank, -1)
+        inside = valid & (held >= 0) & (held < table_rows)
+        key_ref[...] = jnp.where(inside, held + table_rows * rank, -1)
 
         def layer(level, carry):
             for start in range(0, table_rows, CHUNK):
@@ -108,7 +115,7 @@
                 for j in range(slots):
                     distance = jnp.where(row == key_ref[j : j + 1, :], distances[j : j + 1, :], distance)
                 for h in range(heads):
-                    weight[h, at, :] += jnp.exp(-decay[h] * distance)
+                    weight[h, at, :] += jnp.exp(slope[h] * distance)
             return carry
 
         lax.fori_loop(DEPTH, jnp.max(rank) + 1, layer, 0)
@@ -122,6 +129,8 @@
     embedded,
     weight,
     absent,
+    weight_rest,
+    absent_rest,
     readout,
     targets,
     energies,
@@ -163,11 +172,12 @@
     keys = dot(table, weights[1]).astype(BF16)
     values = dot(table, weights[2]).astype(BF16)
     score_ref[...] = dot(keys, stacked_t(query.T.astype(BF16)))
-    gone = absent[...]
+    gone = jnp.concatenate([absent[...], absent_rest[...]], axis=0)
     for h in range(heads):
         at = pl.ds(h * atoms, atoms)
         score = score_ref[:, at] * scale + gone
-        terms = jnp.exp(score - jnp.max(score, axis=0, keepdims=True)) * weight[h]
+        weights_h = jnp.concatenate([weight[h], weight_rest[h]], axis=0)
+        terms = jnp.exp(score - jnp.max(score, axis=0, keepdims=True)) * weights_h
         attention = terms * (1.0 / jnp.sum(terms, axis=0, keepdims=True))
         att_ref[:, at] = attention
         att_half[:, at] = attention.astype(BF16)
@@ -254,10 +264,9 @@
     done = ()
     for early, other in steps:
         vectors = (crossing(early, offsets), crossing(other, offsets))
+        work = beside.pop(0)(*done) if beside else done
         arrived = swap(held, cells, lambda i, vectors=vectors: vectors[late(i)])
-        if beside:
-            done = beside.pop(0)(*done)
-            arrived, done = lax.optimization_barrier((arrived, done))
+        done, arrived = lax.optimization_barrier((work, arrived))
         bit = jnp.where(late(place) == 0, place // early, place // other) % 2
         held = jnp.where(bit == 0, jnp.stack([held, arrived]), jnp.stack([arrived, held]))
     held = jnp.where(late(place) == 0, held, jnp.swapaxes(held, 0, 1))
@@ -320,7 +329,8 @@
     send = portion(total, [(farthest, 1)]).astype(BF16)
     total = keep.astype(F32) + meet(send, vector, 0)
     if bricks > 1:
-        total = total + (meet(keep, 0, 1) + meet(send, vector, 1))
+        far = meet(send, vector, 1)
+        total = total + (far + meet(keep, 0, 1))
     for step in list(reversed(halvings(bricks)))[1:]:
         keep = total.astype(BF16)
         total = keep.astype(F32) + meet(keep, 0, step)
@@ -351,6 +361,8 @@
     heads = head_decay.shape[0]
     table_rows = atoms + bricks * ghost_slots
 
+    kept = (neighbours[0, 0], counts[0], distances[0, 0], head_decay[None], readout[None], targets[0])
+
     def embed():
         return pl.pallas_call(
             embed_kernel,
@@ -359,11 +371,13 @@
                 pinned((atoms, width), BF16),
                 pinned((width, atoms), BF16),
                 pinned((bricks, ghost_slots, width), BF16),
+                *(pinned(array.shape, array.dtype) for array in kept),
             ),
-            in_specs=vmem(5),
-            out_specs=tuple(vmem(4)),
+            in_specs=vmem(5 + len(kept)),
+            out_specs=tuple(vmem(4 + len(kept))),
+            compiler_params=pltpu.CompilerParams(vmem_limit_bytes=4 * 1024 * 1024),
             name="embed",
-        )(features[0, 0], species[0], species_table, norm_gain[None], send_lists[0, 0])
+        )(features[0, 0], species[0], species_table, norm_gain[None], send_lists[0, 0], *kept)
 
     def exchange(embedded, normed, normed_t, parcel):
         brick = lax.axis_index("brick")
@@ -375,25 +389,40 @@
             ghosts = lax.dynamic_update_slice_in_dim(ghosts, arrived, peer, 0)
         return embedded, normed, normed_t, ghosts.reshape(bricks * ghost_slots, width)
 
-    def index(*done):
-        where = lax.optimization_barrier((done, neighbours))[1]
-        return done + pl.pallas_call(
-            index_kernel,
-            out_shape=(pinned((heads, table_rows, atoms), F32), pinned((table_rows, atoms), F32)),
-            in_specs=[SMEM] + vmem(3),
+    part = table_rows // 2
+
+    def index(first, rows, valid, away, decay):
+        return pl.pallas_call(
+            functools.partial(index_kernel, first),
+            out_shape=(pinned((heads, part, atoms), F32), pinned((part, atoms), F32)),
+            in_specs=vmem(4),
             out_specs=tuple(vmem(2)),
             scratch_shapes=[pltpu.VMEM((slots, atoms), jnp.int32)],
+            compiler_params=pltpu.CompilerParams(vmem_limit_bytes=8 * 1024 * 1024),
             name="index",
-        )(head_decay, where[0, 0], counts[0], distances[0, 0])
-
-    weights, done = gather_cells(master.astype(BF16), cells, [embed, exchange, index])
-    embedded, normed, normed_t, ghosts, weight, absent = done
+        )(rows, valid, away, decay)
+
+    def prepare():
+        done = embed()
+        return done[:4], done[4:8], done[8:], index(0, *done[4:8])
+
+    ghosts = []
+
+    def send(state, slot_arrays, held, half):
+        ghosts.append(exchange(*state))
+        return state, slot_arrays, held, half
+
+    def finish(state, slot_arrays, held, half):
+        return ghosts[0], held, half, index(part, *slot_arrays)
+
+    weights, done = gather_cells(master.astype(BF16), cells, [prepare, send, finish])
+    (embedded, normed, normed_t, ghosts), held, *halves = done
 
     columns = heads * atoms
     energies, grads = pl.pallas_call(
         sweep_kernel,
         out_shape=(struct((1, atoms), F32), struct((4, width, width), F32)),
-        in_specs=vmem(9),
+        in_specs=vmem(11),
         out_specs=tuple(vmem(2)),
         scratch_shapes=[
             pltpu.VMEM((table_rows, columns), F32),
@@ -403,7 +432,7 @@
         ],
         compiler_params=pltpu.CompilerParams(vmem_limit_bytes=32 * 1024 * 1024),
         name="sweep",
-    )(weights, normed, normed_t, ghosts, embedded, weight, absent, readout[None], targets[0])
+    )(weights, normed, normed_t, ghosts, embedded, *halves[0], *halves[1], *held)
 
     parts = grads.reshape(4, cells, width // cells, width).transpose(1, 0, 2, 3)
     owned = reduce_all(parts, cells, bricks)

time: 42.5 us -> 39.2 us (0.922)
  Pallas kernels: 7.17 us -> 5.01 us
  waiting for transfers between devices: 14 us -> 12.3 us
    ppermute x8, starting transfers between devices: 9.85 us -> 11.3 us  [swap(): lax.ppermute(array, 'cell', [(i, i ^ vector_of(i)) for i in range(cells)])]
    pallas_call x1 -> x2, Pallas kernels: 3.26 us -> 1.98 us  [index(): pl.pallas_call(functools.partial(index_kernel, first), out_shape=(pinned(...]
    pallas_call x1, Pallas kernels: 1.21 us -> 0.33 us  [embed(): pl.pallas_call(embed_kernel, out_shape=(pinned((atoms, width), F32), pinn...]
    ppermute x1, waiting for transfers between devices: 0.62 us -> 0.01 us  [exchange(): lax.ppermute(sent, 'brick', [(i, i ^ offset) for i in range(bricks)])]
    ppermute x3, waiting for transfers between devices: 4.28 us -> 3.67 us  [meet(): return lax.ppermute(array, ('cell', 'brick'), pairs).astype(F32)]
    ppermute x1, starting transfers between devices: 2.09 us -> 1.49 us  [exchange(): lax.ppermute(sent, 'brick', [(i, i ^ offset) for i in range(bricks)])]
    ppermute x3, starting transfers between devices: 4.68 us -> 4.17 us  [meet(): return lax.ppermute(array, ('cell', 'brick'), pairs).astype(F32)]
  transfers between devices with their start and end apart: 12 -> 12, of which waited for: 11 -> 9; matrix products, arithmetic and copies ran while one was open for 0% -> 0% of each run, Pallas kernels for 11% -> 6%
where the time goes in v4:
time: 39.2 us; the launch traced here: 38.6 us
  starting transfers between devices  17 us (43%)
  waiting for transfers between devices  12.3 us (31%)
  Pallas kernels  5.01 us (13%)
  other arithmetic  2.26 us (6%)
  between operations  1.04 us (3%)
  local copies, waits for them, and re-layouts  0.98 us (2%)
    ppermute x8, starting transfers between devices, swap(): lax.ppermute(array, 'cell', [(i, i ^ vector_of(i)) for i in range(cells)])  11.3 us
    ppermute x8, waiting for transfers between devices, swap(): lax.ppermute(array, 'cell', [(i, i ^ vector_of(i)) for i in range(cells)])  8.64 us
    ppermute x3, starting transfers between devices, meet(): return lax.ppermute(array, ('cell', 'brick'), pairs).astype(F32)  4.17 us
    ppermute x3, waiting for transfers between devices, meet(): return lax.ppermute(array, ('cell', 'brick'), pairs).astype(F32)  3.67 us
    pallas_call x1, Pallas kernels, body(): pl.pallas_call(sweep_kernel, out_shape=(struct((1, atoms), F32), struct((...  2.7 us
    pallas_call x2, Pallas kernels, index(): pl.pallas_call(functools.partial(index_kernel, first), out_shape=(pinned(...  1.98 us
    ppermute x1, starting transfers between devices, exchange(): lax.ppermute(sent, 'brick', [(i, i ^ offset) for i in range(bricks)])  1.49 us
    convert_element_type x1, other arithmetic, body(): master.astype(BF16)  0.91 us
  transfers between devices with their start and end apart: 12, of which 9 were waited for; matrix products, arithmetic and copies ran while one was open for 0% of the time, Pallas kernels for 6%

profile of v4, /device:TPU:0, one launch (start us, length us, event | category | flops | bytes accessed | tf_op | source)
XLA Modules:
  0.0 38.6 jit_solution(9272343760240121479)
XLA Ops:
  0.6 0.0 copy-start.11
  0.6 0.9 %convert_element_type.60 = bf16[4,16,256]{2,1,0:T(8,128)(2,1)S(1)} convert(f32[4,16,256]{2,1,0:T(8,128)} %param.25) | non-fusion elementwise | flops 16384 | bytes 98304 | tf_op jit(solution)/shard_map/convert_element_type | solution.py:418
  1.6 3.5 %collective-permute-start = (bf16[4,16,256]{2,1,0:T(8,128)(2,1)S(1)}, bf16[4,16,256]{2,1,0:T(8,128)(2,1)S(1)}, u32[]{:S(2)}, u32[]{:S(2)}) collective-permute-start(bf16[4,16,256]{2,1,0:T(8,128)(2,1)S(1)} %convert_element_type.60), channel_id=1, source_target_pairs={{0,18},{2,16},{4,22},{6,20},{8,26},{10,24},{12,30},{14,28},{16,2},... | collective-permute-start | bytes 98312 | tf_op jit(solution)/shard_map/ppermute | solution.py:251
  5.0 0.0 copy-done.11
  5.1 0.0 copy-start.9
  5.1 0.0 copy-start.10
  5.1 0.0 copy-start.4
  5.1 0.0 copy-start.5
  5.1 0.0 copy-start.6
  5.1 0.0 copy-start.8
  5.2 0.0 copy-start.3
  5.2 0.0 copy-start
  5.2 0.0 copy-start.2
  5.2 0.0 copy-start.1
  5.3 0.0 copy-start.7
  5.3 0.4 %copy-done.9 = f32[8]{0:T(128)S(1)} copy-done((f32[8]{0:T(128)S(1)}, f32[8]{0:T(128)}, u32[]{:S(2)}) %copy-start.9) | copy-done | bytes 56
  5.7 0.0 copy-done.10
  5.8 0.0 copy-done.4
  5.8 0.0 copy-done.5
  5.8 0.0 copy-done.6
  5.8 0.0 copy-done.8
  5.8 0.0 copy-done.3
  5.9 0.2 copy-done
  6.0 0.0 copy-done.2
  6.0 0.0 copy-done.1
  6.0 0.0 copy-done.7
  6.0 0.3 embed.1
  6.4 1.0 %index.2 = (f32[8,96,128]{2,1,0:T(8,128)S(1)}, f32[96,128]{1,0:T(8,128)S(1)}) custom-call(s32[64,128]{1,0:T(8,128)S(1)} %get-tuple-element.83.neighbours, s32[1,128]{1,0:T(1,128)S(1)} %get-tuple-element.84.counts, f32[64,128]{1,0:T(8,128)S(1)} %get-tuple-element.85.distances, f32[1,8]{1,0:T(1,128)S(1)} %get-tuple-element.86.decay), custom_call_target="tpu_custom_call" | custom-call | tf_op jit(solution)/shard_map/index/pallas_call | solution.py:395
  7.4 0.0 collective-permute-done
  7.4 1.9 %collective-permute-start.1 = (bf16[2,4,16,256]{3,2,1,0:T(8,128)(2,1)S(1)}, bf16[2,4,16,256]{3,2,1,0:T(8,128)(2,1)S(1)}, u32[]{:S(2)}, u32[]{:S(2)}) collective-permute-start(bf16[2,4,16,256]{3,2,1,0:T(8,128)(2,1)S(1)} %maximum_select_fusion.2), channel_id=1, source_target_pairs={{0,10},{2,4},{4,2},{6,12},{8,14},{10,0},{12,6},{14,8},{16,26},{18,... | collective-permute-start | bytes 196616 | tf_op jit(solution)/shard_map/ppermute | solution.py:251
  9.3 1.5 %collective-permute-start.2 = (bf16[1,32,256]{2,1,0:T(8,128)(2,1)S(1)}, bf16[1,32,256]{2,1,0:T(8,128)(2,1)S(1)}, u32[]{:S(2)}, u32[]{:S(2)}) collective-permute-start(bf16[1,32,256]{2,1,0:T(8,128)(2,1)S(1)} %constant_dynamic-slice_fusion), channel_id=1, source_target_pairs={{0,1},{1,0},{2,3},{3,2},{4,5},{5,4},{6,7},{7,6},{8,9},{9,8},{10,11... | collective-permute-start | bytes 49160 | tf_op jit(solution)/shard_map/ppermute | solution.py:388
  10.9 0.4 %collective-permute-done.1 = bf16[2,4,16,256]{3,2,1,0:T(8,128)(2,1)S(1)} collective-permute-done((bf16[2,4,16,256]{3,2,1,0:T(8,128)(2,1)S(1)}, bf16[2,4,16,256]{3,2,1,0:T(8,128)(2,1)S(1)}, u32[]{:S(2)}, u32[]{:S(2)}) %collective-permute-start.1) | collective-permute-done | bytes 65568 | tf_op jit(solution)/shard_map/ppermute | solution.py:251
  11.3 2.0 %collective-permute-start.3 = (bf16[2,2,4,16,256]{4,3,2,0,1:T(8,128)(2,1)S(1)}, bf16[2,2,4,16,256]{4,3,2,0,1:T(8,128)(2,1)S(1)}, u32[]{:S(2)}, u32[]{:S(2)}) collective-permute-start(bf16[2,2,4,16,256]{4,3,2,0,1:T(8,128)(2,1)S(1)} %maximum_select_fusion.1), channel_id=1, source_target_pairs={{0,6},{2,8},{4,14},{6,0},{8,2},{10,12},{12,10},{14,4},{16,22},{18,... | collective-permute-start | bytes 393224 | tf_op jit(solution)/shard_map/ppermute | solution.py:251
  13.4 1.0 %index.3 = (f32[8,96,128]{2,1,0:T(8,128)S(1)}, f32[96,128]{1,0:T(8,128)S(1)}) custom-call(s32[64,128]{1,0:T(8,128)S(1)} %get-tuple-element.83.neighbours, s32[1,128]{1,0:T(1,128)S(1)} %get-tuple-element.84.counts, f32[64,128]{1,0:T(8,128)S(1)} %get-tuple-element.85.distances, f32[1,8]{1,0:T(1,128)S(1)} %get-tuple-element.86.decay), custom_call_target="tpu_custom_call" | custom-call | tf_op jit(solution)/shard_map/index/pallas_call | solution.py:395
  14.4 0.0 collective-permute-done.2
  14.4 1.6 %collective-permute-done.3 = bf16[2,2,4,16,256]{4,3,2,0,1:T(8,128)(2,1)S(1)} collective-permute-done((bf16[2,2,4,16,256]{4,3,2,0,1:T(8,128)(2,1)S(1)}, bf16[2,2,4,16,256]{4,3,2,0,1:T(8,128)(2,1)S(1)}, u32[]{:S(2)}, u32[]{:S(2)}) %collective-permute-start.3) | collective-permute-done | bytes 131104 | tf_op jit(solution)/shard_map/ppermute | solution.py:251
  16.1 0.4 %collective-permute-start.4 = (bf16[2,2,2,4,16,256]{5,4,3,0,1,2:T(8,128)(2,1)S(1)}, bf16[2,2,2,4,16,256]{5,4,3,0,1,2:T(8,128)(2,1)S(1)}, u32[]{:S(2)}, u32[]{:S(2)}) collective-permute-start(bf16[2,2,2,4,16,256]{5,4,3,0,1,2:T(8,128)(2,1)S(1)} %bitcast_select_fusion.2), channel_id=1, source_target_pairs={{0,2},{2,0},{4,6},{6,4},{8,10},{10,8},{12,14},{14,12},{16,18},{18,... | collective-permute-start | bytes 786440 | tf_op jit(solution)/shard_map/ppermute | solution.py:251
  16.5 1.1 %collective-permute-done.4 = bf16[2,2,2,4,16,256]{5,4,3,0,1,2:T(8,128)(2,1)S(1)} collective-permute-done((bf16[2,2,2,4,16,256]{5,4,3,0,1,2:T(8,128)(2,1)S(1)}, bf16[2,2,2,4,16,256]{5,4,3,0,1,2:T(8,128)(2,1)S(1)}, u32[]{:S(2)}, u32[]{:S(2)}) %collective-permute-start.4) | collective-permute-done | bytes 262176 | tf_op jit(solution)/shard_map/ppermute | solution.py:251
  17.7 0.1 fusion
  17.8 0.1 pad_maximum_fusion
  17.9 2.7 %sweep.1 = (f32[1,128]{1,0:T(1,128)}, f32[4,256,256]{2,1,0:T(8,128)S(1)}) custom-call(bf16[4,256,256]{2,1,0:T(8,128)(2,1)S(1)} %bitcast.105, bf16[128,256]{1,0:T(8,128)(2,1)S(1)} %get-tuple-element.90.normed, bf16[256,128]{1,0:T(8,128)(2,1)S(1)} %get-tuple-element.91.normed_t, bf16[64,256]{1,0:T(8,128)(2,1)S(1)} %bitcast.106, ...), custom_call_target="tpu_custom_call" | custom-call | tf_op jit(solution)/shard_map/sweep/pallas_call | solution.py:422
  20.6 0.1 copy.36
  20.7 0.1 select_convert_fusion
  20.8 0.4 collective-permute-start.5
  21.2 1.2 %collective-permute-done.5 = bf16[8,4,16,256]{3,2,1,0:T(8,128)(2,1)S(1)} collective-permute-done((bf16[8,4,16,256]{3,2,1,0:T(8,128)(2,1)S(1)}, bf16[8,4,16,256]{3,2,1,0:T(8,128)(2,1)S(1)}, u32[]{:S(2)}, u32[]{:S(2)}) %collective-permute-start.5) | collective-permute-done | bytes 262176 | tf_op jit(solution)/shard_map/ppermute | solution.py:251
  22.4 0.1 convert_add_fusion
  22.6 2.7 %collective-permute-start.8 = (bf16[2,4,16,256]{3,2,1,0:T(8,128)(2,1)S(1)}, bf16[2,4,16,256]{3,2,1,0:T(8,128)(2,1)S(1)}, u32[]{:S(2)}, u32[]{:S(2)}) collective-permute-start(bf16[2,4,16,256]{3,2,1,0:T(8,128)(2,1)S(1)} %get-tuple-element.108), channel_id=1, source_target_pairs={{0,14},{2,12},{4,10},{6,8},{8,6},{10,4},{12,2},{14,0},{16,30},{18,... | collective-permute-start | bytes 196616 | tf_op jit(solution)/shard_map/ppermute | solution.py:251
  25.3 0.3 collective-permute-start.7
  25.6 0.1 collective-permute-start.6
  25.7 2.1 %collective-permute-done.8 = bf16[2,4,16,256]{3,2,1,0:T(8,128)(2,1)S(1)} collective-permute-done((bf16[2,4,16,256]{3,2,1,0:T(8,128)(2,1)S(1)}, bf16[2,4,16,256]{3,2,1,0:T(8,128)(2,1)S(1)}, u32[]{:S(2)}, u32[]{:S(2)}) %collective-permute-start.8) | collective-permute-done | bytes 65568 | tf_op jit(solution)/shard_map/ppermute | solution.py:251
  27.7 1.8 %collective-permute-done.7 = bf16[2,4,16,256]{3,2,1,0:T(8,128)(2,1)S(1)} collective-permute-done((bf16[2,4,16,256]{3,2,1,0:T(8,128)(2,1)S(1)}, bf16[2,4,16,256]{3,2,1,0:T(8,128)(2,1)S(1)}, u32[]{:S(2)}, u32[]{:S(2)}) %collective-permute-start.7) | collective-permute-done | bytes 65568 | tf_op jit(solution)/shard_map/ppermute | solution.py:251
  29.6 0.4 collective-permute-done.6
  30.0 0.0 copy-start.12
  30.0 0.0 copy-start.13
  30.0 1.6 %collective-permute-start.11 = (bf16[4,16,256]{2,1,0:T(8,128)(2,1)S(1)}, bf16[4,16,256]{2,1,0:T(8,128)(2,1)S(1)}, u32[]{:S(2)}, u32[]{:S(2)}) collective-permute-start(bf16[4,16,256]{2,1,0:T(8,128)(2,1)S(1)} %get-tuple-element.113), channel_id=1, source_target_pairs={{0,1},{1,0},{2,3},{3,2},{4,5},{5,4},{6,7},{7,6},{8,9},{9,8},{10,11... | collective-permute-start | bytes 98312 | tf_op jit(solution)/shard_map/ppermute | solution.py:325
  31.6 2.0 %collective-permute-start.10 = (bf16[4,16,256]{2,1,0:T(8,128)(2,1)S(1)}, bf16[4,16,256]{2,1,0:T(8,128)(2,1)S(1)}, u32[]{:S(2)}, u32[]{:S(2)}) collective-permute-start(bf16[4,16,256]{2,1,0:T(8,128)(2,1)S(1)} %get-tuple-element.112), channel_id=1, source_target_pairs={{0,19},{1,18},{2,17},{3,16},{4,23},{5,22},{6,21},{7,20},{8,27},{9,... | collective-permute-start | bytes 98312 | tf_op jit(solution)/shard_map/ppermute | solution.py:325
  33.6 0.6 %collective-permute-start.9 = (bf16[4,16,256]{2,1,0:T(8,128)(2,1)S(1)}, bf16[4,16,256]{2,1,0:T(8,128)(2,1)S(1)}, u32[]{:S(2)}, u32[]{:S(2)}) collective-permute-start(bf16[4,16,256]{2,1,0:T(8,128)(2,1)S(1)} %get-tuple-element.112), channel_id=1, source_target_pairs={{0,18},{1,19},{2,16},{3,17},{4,22},{5,23},{6,20},{7,21},{8,26},{9,... | collective-permute-start | bytes 98312 | tf_op jit(solution)/shard_map/ppermute | solution.py:325
  34.2 0.0 collective-permute-done.11
  34.2 3.6 %collective-permute-done.10 = bf16[4,16,256]{2,1,0:T(8,128)(2,1)S(1)} collective-permute-done((bf16[4,16,256]{2,1,0:T(8,128)(2,1)S(1)}, bf16[4,16,256]{2,1,0:T(8,128)(2,1)S(1)}, u32[]{:S(2)}, u32[]{:S(2)}) %collective-permute-start.10) | collective-permute-done | bytes 32800 | tf_op jit(solution)/shard_map/ppermute | solution.py:325
  37.8 0.1 collective-permute-done.9
  37.9 0.0 copy-done.12
  37.9 0.0 copy-done.13
  37.9 0.7 %add_divide_fusion = (f32[4,16,256]{2,1,0:T(8,128)}, f32[4,16,256]{2,1,0:T(8,128)}, f32[4,16,256]{2,1,0:T(8,128)}) fusion(bf16[4,16,256]{2,1,0:T(8,128)(2,1)S(1)} %collective-permute-done.11, bf16[4,16,256]{2,1,0:T(8,128)(2,1)S(1)} %collective-permute-done.10, bf16[4,16,256]{2,1,0:T(8,128)(2,1)S(1)} %collective-permute-done.9, ...), kind=kLoop, calls=%fused_computation.30 | loop fusion | flops 262144 | bytes 458752 | tf_op jit(solution)/shard_map/div | solution.py:441
  (18 shorter events, 0.3 us)
Async XLA Ops:
  0.6 4.4 %copy-start.11 = (f32[4,16,256]{2,1,0:T(8,128)S(1)}, f32[4,16,256]{2,1,0:T(8,128)}, u32[]{:S(2)}) copy-start(f32[4,16,256]{2,1,0:T(8,128)} %param.25) | copy-start | bytes 196612
  1.6 5.8 %collective-permute-start = (bf16[4,16,256]{2,1,0:T(8,128)(2,1)S(1)}, bf16[4,16,256]{2,1,0:T(8,128)(2,1)S(1)}, u32[]{:S(2)}, u32[]{:S(2)}) collective-permute-start(bf16[4,16,256]{2,1,0:T(8,128)(2,1)S(1)} %convert_element_type.60), channel_id=1, source_target_pairs={{0,18},{2,16},{4,22},{6,20},{8,26},{10,24},{12,30},{14,28},{16,2},... | collective-permute-start | bytes 98312 | tf_op jit(solution)/shard_map/ppermute | solution.py:251
  5.1 0.7 %copy-start.9 = (f32[8]{0:T(128)S(1)}, f32[8]{0:T(128)}, u32[]{:S(2)}) copy-start(f32[8]{0:T(128)} %param.21) | copy-start | bytes 100
  5.1 0.7 %copy-start.10 = (f32[1,1,128]{2,1,0:T(1,128)S(1)}, f32[1,1,128]{2,1,0:T(1,128)}, u32[]{:S(2)}) copy-start(f32[1,1,128]{2,1,0:T(1,128)} %param.24) | copy-start | bytes 1540
  5.1 0.7 %copy-start.4 = (f32[256]{0:T(256)S(1)}, f32[256]{0:T(256)}, u32[]{:S(2)}) copy-start(f32[256]{0:T(256)} %param.22) | copy-start | bytes 3076
  5.1 0.7 %copy-start.5 = (s32[1,1,2,32]{3,2,1,0:T(2,128)S(1)}, s32[1,1,2,32]{3,2,1,0:T(2,128)}, u32[]{:S(2)}) copy-start(s32[1,1,2,32]{3,2,1,0:T(2,128)} %param.19) | copy-start | bytes 772
  5.1 0.7 %copy-start.6 = (f32[256]{0:T(256)S(1)}, f32[256]{0:T(256)}, u32[]{:S(2)}) copy-start(f32[256]{0:T(256)} %param.23) | copy-start | bytes 3076
  5.1 0.7 %copy-start.8 = (s32[1,1,128]{2,1,0:T(1,128)S(1)}, s32[1,1,128]{2,1,0:T(1,128)}, u32[]{:S(2)}) copy-start(s32[1,1,128]{2,1,0:T(1,128)} %param.18) | copy-start | bytes 1540
  5.2 0.7 %copy-start.3 = (bf16[4,256]{1,0:T(4,128)(2,1)S(1)}, bf16[4,256]{1,0:T(4,128)(2,1)}, u32[]{:S(2)}) copy-start(bf16[4,256]{1,0:T(4,128)(2,1)} %species_table.1) | copy-start | bytes 6148
  5.2 0.9 %copy-start = (bf16[1,1,128,256]{3,2,1,0:T(8,128)(2,1)S(1)}, bf16[1,1,128,256]{3,2,1,0:T(8,128)(2,1)}, u32[]{:S(2)}) copy-start(bf16[1,1,128,256]{3,2,1,0:T(8,128)(2,1)} %param.14) | copy-start | bytes 196612
  5.2 0.8 %copy-start.2 = (f32[1,1,64,128]{3,2,1,0:T(8,128)S(1)}, f32[1,1,64,128]{3,2,1,0:T(8,128)}, u32[]{:S(2)}) copy-start(f32[1,1,64,128]{3,2,1,0:T(8,128)} %param.20) | copy-start | bytes 98308
  5.2 0.8 %copy-start.1 = (s32[1,1,64,128]{3,2,1,0:T(8,128)S(1)}, s32[1,1,64,128]{3,2,1,0:T(8,128)}, u32[]{:S(2)}) copy-start(s32[1,1,64,128]{3,2,1,0:T(8,128)} %param.17) | copy-start | bytes 98308
  5.3 0.8 %copy-start.7 = (s32[1,1,128]{2,1,0:T(1,128)S(1)}, s32[1,1,128]{2,1,0:T(1,128)}, u32[]{:S(2)}) copy-start(s32[1,1,128]{2,1,0:T(1,128)} %param.15) | copy-start | bytes 1540
  7.4 3.9 %collective-permute-start.1 = (bf16[2,4,16,256]{3,2,1,0:T(8,128)(2,1)S(1)}, bf16[2,4,16,256]{3,2,1,0:T(8,128)(2,1)S(1)}, u32[]{:S(2)}, u32[]{:S(2)}) collective-permute-start(bf16[2,4,16,256]{3,2,1,0:T(8,128)(2,1)S(1)} %maximum_select_fusion.2), channel_id=1, source_target_pairs={{0,10},{2,4},{4,2},{6,12},{8,14},{10,0},{12,6},{14,8},{16,26},{18,... | collective-permute-start | bytes 196616 | tf_op jit(solution)/shard_map/ppermute | solution.py:251
  9.3 5.1 %collective-permute-start.2 = (bf16[1,32,256]{2,1,0:T(8,128)(2,1)S(1)}, bf16[1,32,256]{2,1,0:T(8,128)(2,1)S(1)}, u32[]{:S(2)}, u32[]{:S(2)}) collective-permute-start(bf16[1,32,256]{2,1,0:T(8,128)(2,1)S(1)} %constant_dynamic-slice_fusion), channel_id=1, source_target_pairs={{0,1},{1,0},{2,3},{3,2},{4,5},{5,4},{6,7},{7,6},{8,9},{9,8},{10,11... | collective-permute-start | bytes 49160 | tf_op jit(solution)/shard_map/ppermute | solution.py:388
  11.3 4.7 %collective-permute-start.3 = (bf16[2,2,4,16,256]{4,3,2,0,1:T(8,128)(2,1)S(1)}, bf16[2,2,4,16,256]{4,3,2,0,1:T(8,128)(2,1)S(1)}, u32[]{:S(2)}, u32[]{:S(2)}) collective-permute-start(bf16[2,2,4,16,256]{4,3,2,0,1:T(8,128)(2,1)S(1)} %maximum_select_fusion.1), channel_id=1, source_target_pairs={{0,6},{2,8},{4,14},{6,0},{8,2},{10,12},{12,10},{14,4},{16,22},{18,... | collective-permute-start | bytes 393224 | tf_op jit(solution)/shard_map/ppermute | solution.py:251
  16.1 1.6 %collective-permute-start.4 = (bf16[2,2,2,4,16,256]{5,4,3,0,1,2:T(8,128)(2,1)S(1)}, bf16[2,2,2,4,16,256]{5,4,3,0,1,2:T(8,128)(2,1)S(1)}, u32[]{:S(2)}, u32[]{:S(2)}) collective-permute-start(bf16[2,2,2,4,16,256]{5,4,3,0,1,2:T(8,128)(2,1)S(1)} %bitcast_select_fusion.2), channel_id=1, source_target_pairs={{0,2},{2,0},{4,6},{6,4},{8,10},{10,8},{12,14},{14,12},{16,18},{18,... | collective-permute-start | bytes 786440 | tf_op jit(solution)/shard_map/ppermute | solution.py:251
  20.8 1.6 %collective-permute-start.5 = (bf16[8,4,16,256]{3,2,1,0:T(8,128)(2,1)S(1)}, bf16[8,4,16,256]{3,2,1,0:T(8,128)(2,1)S(1)}, u32[]{:S(2)}, u32[]{:S(2)}) collective-permute-start(bf16[8,4,16,256]{3,2,1,0:T(8,128)(2,1)S(1)} %select_convert_fusion), channel_id=1, source_target_pairs={{0,2},{2,0},{4,6},{6,4},{8,10},{10,8},{12,14},{14,12},{16,18},{18,... | collective-permute-start | bytes 786440 | tf_op jit(solution)/shard_map/ppermute | solution.py:251
  22.6 5.2 %collective-permute-start.8 = (bf16[2,4,16,256]{3,2,1,0:T(8,128)(2,1)S(1)}, bf16[2,4,16,256]{3,2,1,0:T(8,128)(2,1)S(1)}, u32[]{:S(2)}, u32[]{:S(2)}) collective-permute-start(bf16[2,4,16,256]{3,2,1,0:T(8,128)(2,1)S(1)} %get-tuple-element.108), channel_id=1, source_target_pairs={{0,14},{2,12},{4,10},{6,8},{8,6},{10,4},{12,2},{14,0},{16,30},{18,... | collective-permute-start | bytes 196616 | tf_op jit(solution)/shard_map/ppermute | solution.py:251
  25.3 4.3 %collective-permute-start.7 = (bf16[2,4,16,256]{3,2,1,0:T(8,128)(2,1)S(1)}, bf16[2,4,16,256]{3,2,1,0:T(8,128)(2,1)S(1)}, u32[]{:S(2)}, u32[]{:S(2)}) collective-permute-start(bf16[2,4,16,256]{3,2,1,0:T(8,128)(2,1)S(1)} %get-tuple-element.109), channel_id=1, source_target_pairs={{0,4},{2,6},{4,0},{6,2},{8,12},{10,14},{12,8},{14,10},{16,20},{18,... | collective-permute-start | bytes 196616 | tf_op jit(solution)/shard_map/ppermute | solution.py:251
  25.6 4.3 %collective-permute-start.6 = (bf16[2,4,16,256]{3,2,1,0:T(8,128)(2,1)S(1)}, bf16[2,4,16,256]{3,2,1,0:T(8,128)(2,1)S(1)}, u32[]{:S(2)}, u32[]{:S(2)}) collective-permute-start(bf16[2,4,16,256]{3,2,1,0:T(8,128)(2,1)S(1)} %get-tuple-element.107), channel_id=1, source_target_pairs={{0,10},{2,8},{4,14},{6,12},{8,2},{10,0},{12,6},{14,4},{16,26},{18,... | collective-permute-start | bytes 196616 | tf_op jit(solution)/shard_map/ppermute | solution.py:251
  30.0 7.9 %copy-start.12 = (f32[4,16,256]{2,1,0:T(8,128)S(1)}, f32[4,16,256]{2,1,0:T(8,128)}, u32[]{:S(2)}) copy-start(f32[4,16,256]{2,1,0:T(8,128)} %param.27) | copy-start | bytes 196612
  30.0 7.9 %copy-start.13 = (f32[4,16,256]{2,1,0:T(8,128)S(1)}, f32[4,16,256]{2,1,0:T(8,128)}, u32[]{:S(2)}) copy-start(f32[4,16,256]{2,1,0:T(8,128)} %param.26) | copy-start | bytes 196612
  30.0 4.2 %collective-permute-start.11 = (bf16[4,16,256]{2,1,0:T(8,128)(2,1)S(1)}, bf16[4,16,256]{2,1,0:T(8,128)(2,1)S(1)}, u32[]{:S(2)}, u32[]{:S(2)}) collective-permute-start(bf16[4,16,256]{2,1,0:T(8,128)(2,1)S(1)} %get-tuple-element.113), channel_id=1, source_target_pairs={{0,1},{1,0},{2,3},{3,2},{4,5},{5,4},{6,7},{7,6},{8,9},{9,8},{10,11... | collective-permute-start | bytes 98312 | tf_op jit(solution)/shard_map/ppermute | solution.py:325
  31.6 6.2 %collective-permute-start.10 = (bf16[4,16,256]{2,1,0:T(8,128)(2,1)S(1)}, bf16[4,16,256]{2,1,0:T(8,128)(2,1)S(1)}, u32[]{:S(2)}, u32[]{:S(2)}) collective-permute-start(bf16[4,16,256]{2,1,0:T(8,128)(2,1)S(1)} %get-tuple-element.112), channel_id=1, source_target_pairs={{0,19},{1,18},{2,17},{3,16},{4,23},{5,22},{6,21},{7,20},{8,27},{9,... | collective-permute-start | bytes 98312 | tf_op jit(solution)/shard_map/ppermute | solution.py:325
  33.6 4.2 %collective-permute-start.9 = (bf16[4,16,256]{2,1,0:T(8,128)(2,1)S(1)}, bf16[4,16,256]{2,1,0:T(8,128)(2,1)S(1)}, u32[]{:S(2)}, u32[]{:S(2)}) collective-permute-start(bf16[4,16,256]{2,1,0:T(8,128)(2,1)S(1)} %get-tuple-element.112), channel_id=1, source_target_pairs={{0,18},{1,19},{2,16},{3,17},{4,22},{5,23},{6,20},{7,21},{8,26},{9,... | collective-permute-start | bytes 98312 | tf_op jit(solution)/shard_map/ppermute | solution.py:325

commit v5 on v4

--- a/solution.py
+++ b/solution.py
@@ -251,30 +251,38 @@
     return lax.ppermute(array, "cell", [(i, i ^ vector_of(i)) for i in range(cells)])
 
 
-def gather_cells(shard, cells, beside):
+def gather_cells(shard, cells, beside, first):
     place = lax.axis_index("cell")
     offsets = halvings(cells)[:-1]
     far, (a, b) = offsets[:-2], offsets[-2:]
-
-    def late(i):
-        return ((i // a) ^ (i // b) ^ i) % 2
-
-    steps = [(offset, offset) for offset in far] + [(a, b), (b, a)]
+    crossed = [*far, b]
     held = shard
     done = ()
-    for early, other in steps:
-        vectors = (crossing(early, offsets), crossing(other, offsets))
+
+    def step(vectors, after=None):
+        nonlocal done
         work = beside.pop(0)(*done) if beside else done
-        arrived = swap(held, cells, lambda i, vectors=vectors: vectors[late(i)])
+        arrived = [swap(held, cells, lambda i, vector=vector: vector) for vector in vectors]
+        if after is not None:
+            arrived[0], early = after(arrived[0])
+            work = (*work, early)
         done, arrived = lax.optimization_barrier((work, arrived))
-        bit = jnp.where(late(place) == 0, place // early, place // other) % 2
-        held = jnp.where(bit == 0, jnp.stack([held, arrived]), jnp.stack([arrived, held]))
-    held = jnp.where(late(place) == 0, held, jnp.swapaxes(held, 0, 1))
-    arrived = swap(held, cells, lambda i: 1)
+        return arrived
+
+    def placed(first, second, offset):
+        own = (place // offset) % 2 == 0
+        return jnp.where(own, jnp.stack([first, second]), jnp.stack([second, first]))
+
+    for offset in far:
+        held = placed(held, step([crossing(offset, crossed)])[0], offset)
+    vectors = [crossing(offset, crossed) for offset in (a, b)]
+    over_both, over_a, over_b = step([vectors[0] ^ vectors[1], *vectors], first)
+    held = placed(placed(held, over_b, b), placed(over_a, over_both, b), a)
+    (arrived,) = step([1])
     count = len(offsets)
-    order = tuple(reversed(range(count))) + tuple(range(count, held.ndim))
+    order = (*reversed(range(2, count)), 0, 1, *range(count, held.ndim))
     held, arrived = held.transpose(order), arrived.transpose(order)
-    core = own_core(cells, offsets).reshape((2,) * count + (1,) * shard.ndim)
+    core = own_core(cells, crossed).reshape((2,) * count + (1,) * shard.ndim)
     pair = [jnp.where(core == 0, held, arrived), jnp.where(core == 0, arrived, held)]
     blocks = jnp.stack(pair, axis=count).reshape((cells,) + shard.shape)
     return blocks.transpose(1, 0, 2, 3).reshape(shard.shape[0], -1, shard.shape[2]), done
@@ -409,13 +417,17 @@
     ghosts = []
 
     def send(state, slot_arrays, held, half):
-        ghosts.append(exchange(*state))
-        return state, slot_arrays, held, half
-
-    def finish(state, slot_arrays, held, half):
-        return ghosts[0], held, half, index(part, *slot_arrays)
-
-    weights, done = gather_cells(master.astype(BF16), cells, [prepare, send, finish])
+        ghosts.append(state)
+        return held, half, index(part, *slot_arrays)
+
+    def start(arrived):
+        return arrived, exchange(*ghosts.pop())
+
+    def receive(held, half, rest, state):
+        return state, held, half, rest
+
+    steps = [prepare, *[lambda *done: done] * (len(halvings(cells)) - 4), send, receive]
+    weights, done = gather_cells(master.astype(BF16), cells, steps, start)
     (embedded, normed, normed_t, ghosts), held, *halves = done
 
     columns = heads * atoms

time: 39.2 us -> 37.9 us (0.967)
  starting transfers between devices: 17 us -> 15.4 us
    ppermute x8 -> x9, starting transfers between devices: 11.3 us -> 9.75 us  [swap(): lax.ppermute(array, 'cell', [(i, i ^ vector_of(i)) for i in range(cells)])]
    ppermute x1, waiting for transfers between devices: 0.01 us -> 1.24 us  [exchange(): lax.ppermute(sent, 'brick', [(i, i ^ offset) for i in range(bricks)])]
    ppermute x8 -> x9, waiting for transfers between devices: 8.64 us -> 7.42 us  [swap(): lax.ppermute(array, 'cell', [(i, i ^ vector_of(i)) for i in range(cells)])]
  transfers between devices with their start and end apart: 12 -> 13, of which waited for: 9 -> 10; matrix products, arithmetic and copies ran while one was open for 0% -> 0% of each run, Pallas kernels for 6% -> 7%
where the time goes in v5:
time: 37.9 us; the launch traced here: 37.2 us
  starting transfers between devices  15.4 us (41%)
  waiting for transfers between devices  12.3 us (32%)
  Pallas kernels  5.34 us (14%)
  other arithmetic  2.22 us (6%)
  local copies, waits for them, and re-layouts  1 us (3%)
  between operations  0.99 us (3%)
    ppermute x9, starting transfers between devices, swap(): lax.ppermute(array, 'cell', [(i, i ^ vector_of(i)) for i in range(cells)])  9.75 us
    ppermute x9, waiting for transfers between devices, swap(): lax.ppermute(array, 'cell', [(i, i ^ vector_of(i)) for i in range(cells)])  7.42 us
    ppermute x3, starting transfers between devices, meet(): return lax.ppermute(array, ('cell', 'brick'), pairs).astype(F32)  4.17 us
    ppermute x3, waiting for transfers between devices, meet(): return lax.ppermute(array, ('cell', 'brick'), pairs).astype(F32)  3.6 us
    pallas_call x1, Pallas kernels, body(): pl.pallas_call(sweep_kernel, out_shape=(struct((1, atoms), F32), struct((...  2.7 us
    pallas_call x2, Pallas kernels, index(): pl.pallas_call(functools.partial(index_kernel, first), out_shape=(pinned(...  2.31 us
    ppermute x1, starting transfers between devices, exchange(): lax.ppermute(sent, 'brick', [(i, i ^ offset) for i in range(bricks)])  1.49 us
    ppermute x1, waiting for transfers between devices, exchange(): lax.ppermute(sent, 'brick', [(i, i ^ offset) for i in range(bricks)])  1.24 us
  transfers between devices with their start and end apart: 13, of which 10 were waited for; matrix products, arithmetic and copies ran while one was open for 0% of the time, Pallas kernels for 7%

profile of v5, /device:TPU:0, one launch (start us, length us, event | category | flops | bytes accessed | tf_op | source)
XLA Modules:
  0.0 37.2 jit_solution(12099085982037634785)
XLA Ops:
  0.6 0.0 copy-start.11
  0.6 0.9 %convert_element_type.60 = bf16[4,16,256]{2,1,0:T(8,128)(2,1)S(1)} convert(f32[4,16,256]{2,1,0:T(8,128)} %param.25) | non-fusion elementwise | flops 16384 | bytes 98304 | tf_op jit(solution)/shard_map/convert_element_type | solution.py:430
  1.6 3.5 %collective-permute-start = (bf16[4,16,256]{2,1,0:T(8,128)(2,1)S(1)}, bf16[4,16,256]{2,1,0:T(8,128)(2,1)S(1)}, u32[]{:S(2)}, u32[]{:S(2)}) collective-permute-start(bf16[4,16,256]{2,1,0:T(8,128)(2,1)S(1)} %convert_element_type.60), channel_id=1, source_target_pairs={{0,18},{2,16},{4,22},{6,20},{8,26},{10,24},{12,30},{14,28},{16,2},... | collective-permute-start | bytes 98312 | tf_op jit(solution)/shard_map/ppermute | solution.py:251
  5.0 0.0 copy-done.11
  5.1 0.0 copy-start.9
  5.1 0.0 copy-start.10
  5.1 0.0 copy-start.4
  5.1 0.0 copy-start.5
  5.1 0.0 copy-start.6
  5.1 0.0 copy-start.7
  5.1 0.0 copy-start.8
  5.2 0.0 copy-start.3
  5.2 0.0 copy-start
  5.2 0.0 copy-start.2
  5.2 0.0 copy-start.1
  5.3 0.5 %copy-done.9 = f32[8]{0:T(128)S(1)} copy-done((f32[8]{0:T(128)S(1)}, f32[8]{0:T(128)}, u32[]{:S(2)}) %copy-start.9) | copy-done | bytes 56
  5.7 0.0 copy-done.10
  5.7 0.0 copy-done.4
  5.8 0.0 copy-done.5
  5.8 0.0 copy-done.6
  5.8 0.0 copy-done.7
  5.8 0.0 copy-done.8
  5.8 0.0 copy-done.3
  5.9 0.2 copy-done
  6.0 0.0 copy-done.2
  6.0 0.0 copy-done.1
  6.0 0.3 embed.1
  6.4 1.3 %index.2 = (f32[8,96,128]{2,1,0:T(8,128)S(1)}, f32[96,128]{1,0:T(8,128)S(1)}) custom-call(s32[64,128]{1,0:T(8,128)S(1)} %get-tuple-element.74.neighbours, s32[1,128]{1,0:T(1,128)S(1)} %get-tuple-element.75.counts, f32[64,128]{1,0:T(8,128)S(1)} %get-tuple-element.76.distances, f32[1,8]{1,0:T(1,128)S(1)} %get-tuple-element.77.decay), custom_call_target="tpu_custom_call" | custom-call | tf_op jit(solution)/shard_map/index/pallas_call | solution.py:403
  7.7 0.0 collective-permute-done
  7.7 2.5 %collective-permute-start.2 = (bf16[2,4,16,256]{3,2,1,0:T(8,128)(2,1)S(1)}, bf16[2,4,16,256]{3,2,1,0:T(8,128)(2,1)S(1)}, u32[]{:S(2)}, u32[]{:S(2)}) collective-permute-start(bf16[2,4,16,256]{3,2,1,0:T(8,128)(2,1)S(1)} %maximum_select_fusion.3), channel_id=1, source_target_pairs={{0,14},{2,12},{4,10},{6,8},{8,6},{10,4},{12,2},{14,0},{16,30},{18,... | collective-permute-start | bytes 196616 | tf_op jit(solution)/shard_map/ppermute | solution.py:251
  10.3 0.4 %collective-permute-start.3 = (bf16[2,4,16,256]{3,2,1,0:T(8,128)(2,1)S(1)}, bf16[2,4,16,256]{3,2,1,0:T(8,128)(2,1)S(1)}, u32[]{:S(2)}, u32[]{:S(2)}) collective-permute-start(bf16[2,4,16,256]{3,2,1,0:T(8,128)(2,1)S(1)} %maximum_select_fusion.3), channel_id=1, source_target_pairs={{0,8},{2,10},{4,12},{6,14},{8,0},{10,2},{12,4},{14,6},{16,24},{18,... | collective-permute-start | bytes 196616 | tf_op jit(solution)/shard_map/ppermute | solution.py:251
  10.7 0.0 collective-permute-start.4
  10.7 1.5 %collective-permute-start.1 = (bf16[1,32,256]{2,1,0:T(8,128)(2,1)S(1)}, bf16[1,32,256]{2,1,0:T(8,128)(2,1)S(1)}, u32[]{:S(2)}, u32[]{:S(2)}) collective-permute-start(bf16[1,32,256]{2,1,0:T(8,128)(2,1)S(1)} %constant_dynamic-slice_fusion), channel_id=1, source_target_pairs={{0,1},{1,0},{2,3},{3,2},{4,5},{5,4},{6,7},{7,6},{8,9},{9,8},{10,11... | collective-permute-start | bytes 49160 | tf_op jit(solution)/shard_map/ppermute | solution.py:396
  12.2 1.0 %index.3 = (f32[8,96,128]{2,1,0:T(8,128)S(1)}, f32[96,128]{1,0:T(8,128)S(1)}) custom-call(s32[64,128]{1,0:T(8,128)S(1)} %get-tuple-element.74.neighbours, s32[1,128]{1,0:T(1,128)S(1)} %get-tuple-element.75.counts, f32[64,128]{1,0:T(8,128)S(1)} %get-tuple-element.76.distances, f32[1,8]{1,0:T(1,128)S(1)} %get-tuple-element.77.decay), custom_call_target="tpu_custom_call" | custom-call | tf_op jit(solution)/shard_map/index/pallas_call | solution.py:403
  13.2 1.2 %collective-permute-done.1 = bf16[1,32,256]{2,1,0:T(8,128)(2,1)S(1)} collective-permute-done((bf16[1,32,256]{2,1,0:T(8,128)(2,1)S(1)}, bf16[1,32,256]{2,1,0:T(8,128)(2,1)S(1)}, u32[]{:S(2)}, u32[]{:S(2)}) %collective-permute-start.1) | collective-permute-done | bytes 16416 | tf_op jit(solution)/shard_map/ppermute | solution.py:396
  14.5 0.0 collective-permute-done.2
  14.5 0.1 collective-permute-done.3
  14.6 0.5 %collective-permute-done.4 = bf16[2,4,16,256]{3,2,1,0:T(8,128)(2,1)S(1)} collective-permute-done((bf16[2,4,16,256]{3,2,1,0:T(8,128)(2,1)S(1)}, bf16[2,4,16,256]{3,2,1,0:T(8,128)(2,1)S(1)}, u32[]{:S(2)}, u32[]{:S(2)}) %collective-permute-start.4) | collective-permute-done | bytes 65568 | tf_op jit(solution)/shard_map/ppermute | solution.py:251
  15.1 0.1 collective-permute-start.5
  15.3 1.4 %collective-permute-done.5 = bf16[2,2,2,4,16,256]{5,4,3,1,0,2:T(8,128)(2,1)S(1)} collective-permute-done((bf16[2,2,2,4,16,256]{5,4,3,1,0,2:T(8,128)(2,1)S(1)}, bf16[2,2,2,4,16,256]{5,4,3,1,0,2:T(8,128)(2,1)S(1)}, u32[]{:S(2)}, u32[]{:S(2)}) %collective-permute-start.5) | collective-permute-done | bytes 262176 | tf_op jit(solution)/shard_map/ppermute | solution.py:251
  16.7 0.1 fusion
  16.8 0.1 pad_maximum_fusion
  16.9 2.7 %sweep.1 = (f32[1,128]{1,0:T(1,128)}, f32[4,256,256]{2,1,0:T(8,128)S(1)}) custom-call(bf16[4,256,256]{2,1,0:T(8,128)(2,1)S(1)} %bitcast.89, bf16[128,256]{1,0:T(8,128)(2,1)S(1)} %get-tuple-element.98.normed, bf16[256,128]{1,0:T(8,128)(2,1)S(1)} %get-tuple-element.99.normed_t, bf16[64,256]{1,0:T(8,128)(2,1)S(1)} %bitcast.90, ...), custom_call_target="tpu_custom_call" | custom-call | tf_op jit(solution)/shard_map/sweep/pallas_call | solution.py:434
  19.6 0.1 copy.29
  19.7 0.1 select_convert_fusion
  19.9 0.2 collective-permute-start.6
  20.1 1.4 %collective-permute-done.6 = bf16[8,4,16,256]{3,2,1,0:T(8,128)(2,1)S(1)} collective-permute-done((bf16[8,4,16,256]{3,2,1,0:T(8,128)(2,1)S(1)}, bf16[8,4,16,256]{3,2,1,0:T(8,128)(2,1)S(1)}, u32[]{:S(2)}, u32[]{:S(2)}) %collective-permute-start.6) | collective-permute-done | bytes 262176 | tf_op jit(solution)/shard_map/ppermute | solution.py:251
  21.5 0.1 convert_add_fusion
  21.6 1.8 %collective-permute-start.9 = (bf16[2,4,16,256]{3,2,1,0:T(8,128)(2,1)S(1)}, bf16[2,4,16,256]{3,2,1,0:T(8,128)(2,1)S(1)}, u32[]{:S(2)}, u32[]{:S(2)}) collective-permute-start(bf16[2,4,16,256]{3,2,1,0:T(8,128)(2,1)S(1)} %get-tuple-element.116), channel_id=1, source_target_pairs={{0,14},{2,12},{4,10},{6,8},{8,6},{10,4},{12,2},{14,0},{16,30},{18,... | collective-permute-start | bytes 196616 | tf_op jit(solution)/shard_map/ppermute | solution.py:251
  23.4 1.1 %collective-permute-start.8 = (bf16[2,4,16,256]{3,2,1,0:T(8,128)(2,1)S(1)}, bf16[2,4,16,256]{3,2,1,0:T(8,128)(2,1)S(1)}, u32[]{:S(2)}, u32[]{:S(2)}) collective-permute-start(bf16[2,4,16,256]{3,2,1,0:T(8,128)(2,1)S(1)} %get-tuple-element.117), channel_id=1, source_target_pairs={{0,4},{2,6},{4,0},{6,2},{8,12},{10,14},{12,8},{14,10},{16,20},{18,... | collective-permute-start | bytes 196616 | tf_op jit(solution)/shard_map/ppermute | solution.py:251
  24.5 0.1 collective-permute-start.7
  24.6 2.1 %collective-permute-done.9 = bf16[2,4,16,256]{3,2,1,0:T(8,128)(2,1)S(1)} collective-permute-done((bf16[2,4,16,256]{3,2,1,0:T(8,128)(2,1)S(1)}, bf16[2,4,16,256]{3,2,1,0:T(8,128)(2,1)S(1)}, u32[]{:S(2)}, u32[]{:S(2)}) %collective-permute-start.9) | collective-permute-done | bytes 65568 | tf_op jit(solution)/shard_map/ppermute | solution.py:251
  26.7 1.7 %collective-permute-done.8 = bf16[2,4,16,256]{3,2,1,0:T(8,128)(2,1)S(1)} collective-permute-done((bf16[2,4,16,256]{3,2,1,0:T(8,128)(2,1)S(1)}, bf16[2,4,16,256]{3,2,1,0:T(8,128)(2,1)S(1)}, u32[]{:S(2)}, u32[]{:S(2)}) %collective-permute-start.8) | collective-permute-done | bytes 65568 | tf_op jit(solution)/shard_map/ppermute | solution.py:251
  28.4 0.3 collective-permute-done.7
  28.7 0.0 copy-start.12
  28.7 0.0 copy-start.13
  28.8 1.4 %collective-permute-start.12 = (bf16[4,16,256]{2,1,0:T(8,128)(2,1)S(1)}, bf16[4,16,256]{2,1,0:T(8,128)(2,1)S(1)}, u32[]{:S(2)}, u32[]{:S(2)}) collective-permute-start(bf16[4,16,256]{2,1,0:T(8,128)(2,1)S(1)} %get-tuple-element.121), channel_id=1, source_target_pairs={{0,1},{1,0},{2,3},{3,2},{4,5},{5,4},{6,7},{7,6},{8,9},{9,8},{10,11... | collective-permute-start | bytes 98312 | tf_op jit(solution)/shard_map/ppermute | solution.py:333
  30.1 2.2 %collective-permute-start.11 = (bf16[4,16,256]{2,1,0:T(8,128)(2,1)S(1)}, bf16[4,16,256]{2,1,0:T(8,128)(2,1)S(1)}, u32[]{:S(2)}, u32[]{:S(2)}) collective-permute-start(bf16[4,16,256]{2,1,0:T(8,128)(2,1)S(1)} %get-tuple-element.120), channel_id=1, source_target_pairs={{0,19},{1,18},{2,17},{3,16},{4,23},{5,22},{6,21},{7,20},{8,27},{9,... | collective-permute-start | bytes 98312 | tf_op jit(solution)/shard_map/ppermute | solution.py:333
  32.3 0.6 %collective-permute-start.10 = (bf16[4,16,256]{2,1,0:T(8,128)(2,1)S(1)}, bf16[4,16,256]{2,1,0:T(8,128)(2,1)S(1)}, u32[]{:S(2)}, u32[]{:S(2)}) collective-permute-start(bf16[4,16,256]{2,1,0:T(8,128)(2,1)S(1)} %get-tuple-element.120), channel_id=1, source_target_pairs={{0,18},{1,19},{2,16},{3,17},{4,22},{5,23},{6,20},{7,21},{8,26},{9,... | collective-permute-start | bytes 98312 | tf_op jit(solution)/shard_map/ppermute | solution.py:333
  32.9 0.0 collective-permute-done.12
  32.9 3.4 %collective-permute-done.11 = bf16[4,16,256]{2,1,0:T(8,128)(2,1)S(1)} collective-permute-done((bf16[4,16,256]{2,1,0:T(8,128)(2,1)S(1)}, bf16[4,16,256]{2,1,0:T(8,128)(2,1)S(1)}, u32[]{:S(2)}, u32[]{:S(2)}) %collective-permute-start.11) | collective-permute-done | bytes 32800 | tf_op jit(solution)/shard_map/ppermute | solution.py:333
  36.3 0.2 collective-permute-done.10
  36.5 0.0 copy-done.12
  36.5 0.7 %add_divide_fusion = (f32[4,16,256]{2,1,0:T(8,128)}, f32[4,16,256]{2,1,0:T(8,128)}, f32[4,16,256]{2,1,0:T(8,128)}) fusion(bf16[4,16,256]{2,1,0:T(8,128)(2,1)S(1)} %collective-permute-done.12, bf16[4,16,256]{2,1,0:T(8,128)(2,1)S(1)} %collective-permute-done.11, bf16[4,16,256]{2,1,0:T(8,128)(2,1)S(1)} %collective-permute-done.10, ...), kind=kLoop, calls=%fused_computation.28 | loop fusion | flops 262144 | bytes 458752 | tf_op jit(solution)/shard_map/div | solution.py:453
  (16 shorter events, 0.3 us)
Async XLA Ops:
  0.6 4.4 %copy-start.11 = (f32[4,16,256]{2,1,0:T(8,128)S(1)}, f32[4,16,256]{2,1,0:T(8,128)}, u32[]{:S(2)}) copy-start(f32[4,16,256]{2,1,0:T(8,128)} %param.25) | copy-start | bytes 196612
  1.6 6.2 %collective-permute-start = (bf16[4,16,256]{2,1,0:T(8,128)(2,1)S(1)}, bf16[4,16,256]{2,1,0:T(8,128)(2,1)S(1)}, u32[]{:S(2)}, u32[]{:S(2)}) collective-permute-start(bf16[4,16,256]{2,1,0:T(8,128)(2,1)S(1)} %convert_element_type.60), channel_id=1, source_target_pairs={{0,18},{2,16},{4,22},{6,20},{8,26},{10,24},{12,30},{14,28},{16,2},... | collective-permute-start | bytes 98312 | tf_op jit(solution)/shard_map/ppermute | solution.py:251
  5.1 0.7 %copy-start.9 = (f32[8]{0:T(128)S(1)}, f32[8]{0:T(128)}, u32[]{:S(2)}) copy-start(f32[8]{0:T(128)} %param.21) | copy-start | bytes 100
  5.1 0.7 %copy-start.10 = (f32[1,1,128]{2,1,0:T(1,128)S(1)}, f32[1,1,128]{2,1,0:T(1,128)}, u32[]{:S(2)}) copy-start(f32[1,1,128]{2,1,0:T(1,128)} %param.24) | copy-start | bytes 1540
  5.1 0.7 %copy-start.4 = (f32[256]{0:T(256)S(1)}, f32[256]{0:T(256)}, u32[]{:S(2)}) copy-start(f32[256]{0:T(256)} %param.22) | copy-start | bytes 3076
  5.1 0.7 %copy-start.5 = (s32[1,1,2,32]{3,2,1,0:T(2,128)S(1)}, s32[1,1,2,32]{3,2,1,0:T(2,128)}, u32[]{:S(2)}) copy-start(s32[1,1,2,32]{3,2,1,0:T(2,128)} %param.19) | copy-start | bytes 772
  5.1 0.7 %copy-start.6 = (f32[256]{0:T(256)S(1)}, f32[256]{0:T(256)}, u32[]{:S(2)}) copy-start(f32[256]{0:T(256)} %param.23) | copy-start | bytes 3076
  5.1 0.7 %copy-start.7 = (s32[1,1,128]{2,1,0:T(1,128)S(1)}, s32[1,1,128]{2,1,0:T(1,128)}, u32[]{:S(2)}) copy-start(s32[1,1,128]{2,1,0:T(1,128)} %param.15) | copy-start | bytes 1540
  5.1 0.7 %copy-start.8 = (s32[1,1,128]{2,1,0:T(1,128)S(1)}, s32[1,1,128]{2,1,0:T(1,128)}, u32[]{:S(2)}) copy-start(s32[1,1,128]{2,1,0:T(1,128)} %param.18) | copy-start | bytes 1540
  5.2 0.7 %copy-start.3 = (bf16[4,256]{1,0:T(4,128)(2,1)S(1)}, bf16[4,256]{1,0:T(4,128)(2,1)}, u32[]{:S(2)}) copy-start(bf16[4,256]{1,0:T(4,128)(2,1)} %species_table.1) | copy-start | bytes 6148
  5.2 0.9 %copy-start = (bf16[1,1,128,256]{3,2,1,0:T(8,128)(2,1)S(1)}, bf16[1,1,128,256]{3,2,1,0:T(8,128)(2,1)}, u32[]{:S(2)}) copy-start(bf16[1,1,128,256]{3,2,1,0:T(8,128)(2,1)} %param.14) | copy-start | bytes 196612
  5.2 0.8 %copy-start.2 = (f32[1,1,64,128]{3,2,1,0:T(8,128)S(1)}, f32[1,1,64,128]{3,2,1,0:T(8,128)}, u32[]{:S(2)}) copy-start(f32[1,1,64,128]{3,2,1,0:T(8,128)} %param.20) | copy-start | bytes 98308
  5.2 0.8 %copy-start.1 = (s32[1,1,64,128]{3,2,1,0:T(8,128)S(1)}, s32[1,1,64,128]{3,2,1,0:T(8,128)}, u32[]{:S(2)}) copy-start(s32[1,1,64,128]{3,2,1,0:T(8,128)} %param.17) | copy-start | bytes 98308
  7.7 6.7 %collective-permute-start.2 = (bf16[2,4,16,256]{3,2,1,0:T(8,128)(2,1)S(1)}, bf16[2,4,16,256]{3,2,1,0:T(8,128)(2,1)S(1)}, u32[]{:S(2)}, u32[]{:S(2)}) collective-permute-start(bf16[2,4,16,256]{3,2,1,0:T(8,128)(2,1)S(1)} %maximum_select_fusion.3), channel_id=1, source_target_pairs={{0,14},{2,12},{4,10},{6,8},{8,6},{10,4},{12,2},{14,0},{16,30},{18,... | collective-permute-start | bytes 196616 | tf_op jit(solution)/shard_map/ppermute | solution.py:251
  10.3 4.3 %collective-permute-start.3 = (bf16[2,4,16,256]{3,2,1,0:T(8,128)(2,1)S(1)}, bf16[2,4,16,256]{3,2,1,0:T(8,128)(2,1)S(1)}, u32[]{:S(2)}, u32[]{:S(2)}) collective-permute-start(bf16[2,4,16,256]{3,2,1,0:T(8,128)(2,1)S(1)} %maximum_select_fusion.3), channel_id=1, source_target_pairs={{0,8},{2,10},{4,12},{6,14},{8,0},{10,2},{12,4},{14,6},{16,24},{18,... | collective-permute-start | bytes 196616 | tf_op jit(solution)/shard_map/ppermute | solution.py:251
  10.7 4.3 %collective-permute-start.4 = (bf16[2,4,16,256]{3,2,1,0:T(8,128)(2,1)S(1)}, bf16[2,4,16,256]{3,2,1,0:T(8,128)(2,1)S(1)}, u32[]{:S(2)}, u32[]{:S(2)}) collective-permute-start(bf16[2,4,16,256]{3,2,1,0:T(8,128)(2,1)S(1)} %maximum_select_fusion.3), channel_id=1, source_target_pairs={{0,6},{2,4},{4,2},{6,0},{8,14},{10,12},{12,10},{14,8},{16,22},{18,... | collective-permute-start | bytes 196616 | tf_op jit(solution)/shard_map/ppermute | solution.py:251
  10.7 3.7 %collective-permute-start.1 = (bf16[1,32,256]{2,1,0:T(8,128)(2,1)S(1)}, bf16[1,32,256]{2,1,0:T(8,128)(2,1)S(1)}, u32[]{:S(2)}, u32[]{:S(2)}) collective-permute-start(bf16[1,32,256]{2,1,0:T(8,128)(2,1)S(1)} %constant_dynamic-slice_fusion), channel_id=1, source_target_pairs={{0,1},{1,0},{2,3},{3,2},{4,5},{5,4},{6,7},{7,6},{8,9},{9,8},{10,11... | collective-permute-start | bytes 49160 | tf_op jit(solution)/shard_map/ppermute | solution.py:396
  15.1 1.6 %collective-permute-start.5 = (bf16[2,2,2,4,16,256]{5,4,3,1,0,2:T(8,128)(2,1)S(1)}, bf16[2,2,2,4,16,256]{5,4,3,1,0,2:T(8,128)(2,1)S(1)}, u32[]{:S(2)}, u32[]{:S(2)}) collective-permute-start(bf16[2,2,2,4,16,256]{5,4,3,1,0,2:T(8,128)(2,1)S(1)} %maximum_select_fusion), channel_id=1, source_target_pairs={{0,2},{2,0},{4,6},{6,4},{8,10},{10,8},{12,14},{14,12},{16,18},{18,... | collective-permute-start | bytes 786440 | tf_op jit(solution)/shard_map/ppermute | solution.py:251
  19.9 1.6 %collective-permute-start.6 = (bf16[8,4,16,256]{3,2,1,0:T(8,128)(2,1)S(1)}, bf16[8,4,16,256]{3,2,1,0:T(8,128)(2,1)S(1)}, u32[]{:S(2)}, u32[]{:S(2)}) collective-permute-start(bf16[8,4,16,256]{3,2,1,0:T(8,128)(2,1)S(1)} %select_convert_fusion), channel_id=1, source_target_pairs={{0,2},{2,0},{4,6},{6,4},{8,10},{10,8},{12,14},{14,12},{16,18},{18,... | collective-permute-start | bytes 786440 | tf_op jit(solution)/shard_map/ppermute | solution.py:251
  21.6 5.1 %collective-permute-start.9 = (bf16[2,4,16,256]{3,2,1,0:T(8,128)(2,1)S(1)}, bf16[2,4,16,256]{3,2,1,0:T(8,128)(2,1)S(1)}, u32[]{:S(2)}, u32[]{:S(2)}) collective-permute-start(bf16[2,4,16,256]{3,2,1,0:T(8,128)(2,1)S(1)} %get-tuple-element.116), channel_id=1, source_target_pairs={{0,14},{2,12},{4,10},{6,8},{8,6},{10,4},{12,2},{14,0},{16,30},{18,... | collective-permute-start | bytes 196616 | tf_op jit(solution)/shard_map/ppermute | solution.py:251
  23.4 5.0 %collective-permute-start.8 = (bf16[2,4,16,256]{3,2,1,0:T(8,128)(2,1)S(1)}, bf16[2,4,16,256]{3,2,1,0:T(8,128)(2,1)S(1)}, u32[]{:S(2)}, u32[]{:S(2)}) collective-permute-start(bf16[2,4,16,256]{3,2,1,0:T(8,128)(2,1)S(1)} %get-tuple-element.117), channel_id=1, source_target_pairs={{0,4},{2,6},{4,0},{6,2},{8,12},{10,14},{12,8},{14,10},{16,20},{18,... | collective-permute-start | bytes 196616 | tf_op jit(solution)/shard_map/ppermute | solution.py:251
  24.5 4.1 %collective-permute-start.7 = (bf16[2,4,16,256]{3,2,1,0:T(8,128)(2,1)S(1)}, bf16[2,4,16,256]{3,2,1,0:T(8,128)(2,1)S(1)}, u32[]{:S(2)}, u32[]{:S(2)}) collective-permute-start(bf16[2,4,16,256]{3,2,1,0:T(8,128)(2,1)S(1)} %get-tuple-element.115), channel_id=1, source_target_pairs={{0,10},{2,8},{4,14},{6,12},{8,2},{10,0},{12,6},{14,4},{16,26},{18,... | collective-permute-start | bytes 196616 | tf_op jit(solution)/shard_map/ppermute | solution.py:251
  28.7 7.8 %copy-start.12 = (f32[4,16,256]{2,1,0:T(8,128)S(1)}, f32[4,16,256]{2,1,0:T(8,128)}, u32[]{:S(2)}) copy-start(f32[4,16,256]{2,1,0:T(8,128)} %param.27) | copy-start | bytes 196612
  28.7 7.8 %copy-start.13 = (f32[4,16,256]{2,1,0:T(8,128)S(1)}, f32[4,16,256]{2,1,0:T(8,128)}, u32[]{:S(2)}) copy-start(f32[4,16,256]{2,1,0:T(8,128)} %param.26) | copy-start | bytes 196612
  28.8 4.2 %collective-permute-start.12 = (bf16[4,16,256]{2,1,0:T(8,128)(2,1)S(1)}, bf16[4,16,256]{2,1,0:T(8,128)(2,1)S(1)}, u32[]{:S(2)}, u32[]{:S(2)}) collective-permute-start(bf16[4,16,256]{2,1,0:T(8,128)(2,1)S(1)} %get-tuple-element.121), channel_id=1, source_target_pairs={{0,1},{1,0},{2,3},{3,2},{4,5},{5,4},{6,7},{7,6},{8,9},{9,8},{10,11... | collective-permute-start | bytes 98312 | tf_op jit(solution)/shard_map/ppermute | solution.py:333
  30.1 6.2 %collective-permute-start.11 = (bf16[4,16,256]{2,1,0:T(8,128)(2,1)S(1)}, bf16[4,16,256]{2,1,0:T(8,128)(2,1)S(1)}, u32[]{:S(2)}, u32[]{:S(2)}) collective-permute-start(bf16[4,16,256]{2,1,0:T(8,128)(2,1)S(1)} %get-tuple-element.120), channel_id=1, source_target_pairs={{0,19},{1,18},{2,17},{3,16},{4,23},{5,22},{6,21},{7,20},{8,27},{9,... | collective-permute-start | bytes 98312 | tf_op jit(solution)/shard_map/ppermute | solution.py:333
  32.3 4.2 %collective-permute-start.10 = (bf16[4,16,256]{2,1,0:T(8,128)(2,1)S(1)}, bf16[4,16,256]{2,1,0:T(8,128)(2,1)S(1)}, u32[]{:S(2)}, u32[]{:S(2)}) collective-permute-start(bf16[4,16,256]{2,1,0:T(8,128)(2,1)S(1)} %get-tuple-element.120), channel_id=1, source_target_pairs={{0,18},{1,19},{2,16},{3,17},{4,22},{5,23},{6,20},{7,21},{8,26},{9,... | collective-permute-start | bytes 98312 | tf_op jit(solution)/shard_map/ppermute | solution.py:333

commit v6 on v5

--- a/solution.py
+++ b/solution.py
@@ -12,6 +12,7 @@
 DEPTH = 5
 FAR = 1e30
 FAR_ROW = 1 << 20
+PACK_ROWS = 16
 
 loss_weight = 0.0625
 epsilon_norm = 1e-06
@@ -46,20 +47,14 @@
     return jnp.sum(jnp.where(eye, column, jnp.zeros_like(column)), axis=0, keepdims=True)
 
 
-def embed_kernel(features, species, species_table, norm_gain, send_rows, *refs):
-    count = (len(refs) - 4) // 2
-    embedded, normed, normed_t, parcel = refs[count : count + 4]
-    for source, target in zip(refs[:count], refs[count + 4 :]):
-        target[...] = source[...]
+def embed(features, species, species_table, norm_gain, send_rows, embedded, normed, normed_t, parcel):
     atoms = features.shape[0]
-    kinds = species_table.shape[0]
-    column = to_column(species[...])
-    total = features[...].astype(F32)
-    picked = jnp.zeros_like(total)
-    for kind in range(kinds):
+    column = to_column(species)
+    picked = jnp.zeros_like(features)
+    for kind in range(species_table.shape[0]):
         row = species_table[kind : kind + 1, :].astype(F32)
         picked = jnp.where(column == kind, row, picked)
-    total = total + picked
+    total = features + picked
     embedded[...] = total
     scale = lax.rsqrt(jnp.mean(total * total, axis=-1, keepdims=True) + epsilon_norm)
     norm = total * scale * norm_gain[...]
@@ -71,6 +66,60 @@
         chosen = send_rows[brick : brick + 1, :]
         picks = (lax.broadcasted_iota(jnp.int32, (atoms, slots), 0) == chosen).astype(F32).astype(BF16)
         parcel[brick] = dot_tn(picks, half).astype(BF16)
+
+
+def terms_of(value):
+    high = value.astype(BF16).astype(F32)
+    rest = value - high
+    middle = rest.astype(BF16).astype(F32)
+    return [high, middle, rest - middle]
+
+
+def embed_kernel(pack, master, features, species, send_rows, species_table, norm_gain, *refs):
+    count = (len(refs) - 5 - pack) // 2
+    sources, (shard, embedded, normed, normed_t, parcel) = refs[:count], refs[count : count + 5]
+    kept = refs[count + 5 :]
+    shard[...] = master[...].astype(BF16)
+    for source, target in zip(sources, kept):
+        target[...] = source[...]
+    if pack:
+        neighbours, counts, distances, targets = sources[:4]
+        packed = kept[-1]
+        slots, atoms = neighbours.shape
+        width = features.shape[1]
+        arrays = [features[:, at : at + atoms].astype(F32) for at in range(0, width, atoms)]
+        arrays += [neighbours[...].astype(F32), *terms_of(distances[...])]
+        bricks, sent = send_rows.shape
+        rows = [species[...].astype(F32), counts[...].astype(F32), *terms_of(targets[...])]
+        lists = jnp.concatenate([send_rows[...].astype(F32), jnp.zeros((bricks, atoms - sent), F32)], axis=1)
+        rows += [lists, jnp.zeros((PACK_ROWS - len(rows) - bricks, atoms), F32)]
+        start = 0
+        for array in [*arrays, jnp.concatenate(rows, axis=0)]:
+            packed[start : start + array.shape[0], :] = array.astype(BF16)
+            start += array.shape[0]
+    embed(features[...].astype(F32), species[...], species_table, norm_gain, send_rows, embedded, normed, normed_t, parcel)
+
+
+def unpack_kernel(packed, species_table, norm_gain, embedded, normed, normed_t, parcel, neighbours, counts, distances, targets):
+    slots, atoms = neighbours.shape
+    width = embedded.shape[1]
+    bricks, sent = parcel.shape[:2]
+    start = 0
+
+    def take(rows):
+        nonlocal start
+        start += rows
+        return packed[start - rows : start, :].astype(F32)
+
+    features = jnp.concatenate([take(atoms) for _ in range(width // atoms)], axis=1)
+    neighbours[...] = take(slots).astype(jnp.int32)
+    distances[...] = take(slots) + take(slots) + take(slots)
+    rows = take(PACK_ROWS)
+    counts[...] = rows[1:2].astype(jnp.int32)
+    targets[...] = rows[2:3] + rows[3:4] + rows[4:5]
+    send_rows = rows[5 : 5 + bricks, :sent].astype(jnp.int32)
+    species = rows[0:1].astype(jnp.int32)
+    embed(features, species, species_table, norm_gain, send_rows, embedded, normed, normed_t, parcel)
 
 
 def index_kernel(first, neighbours, counts, distances, decay, weight, absent, key_ref):
@@ -121,93 +170,93 @@
         lax.fori_loop(DEPTH, jnp.max(rank) + 1, layer, 0)
 
 
-def sweep_kernel(
-    weights,
-    normed,
-    normed_t,
-    ghosts,
-    embedded,
-    weight,
-    absent,
-    weight_rest,
-    absent_rest,
-    readout,
-    targets,
-    energies,
-    grads,
-    score_ref,
-    att_ref,
-    att_half,
-    grad_score,
-):
-    atoms, width = normed.shape
-    heads = weight.shape[0]
+def sweep_kernel(count, weights, readout, *refs):
+    operands, scratch = 9, 4
+    energies, grads = refs[operands * count : operands * count + 2]
+    bricks = [refs[operands * i : operands * (i + 1)] for i in range(count)]
+    start = operands * count + 2
+    memory = [refs[start + scratch * i : start + scratch * (i + 1)] for i in range(count)]
+    atoms, width = bricks[0][0].shape
+    heads = bricks[0][4].shape[0]
     head_size = width // heads
     scale = 1.0 / math.sqrt(head_size)
     head_of = lax.broadcasted_iota(jnp.int32, (atoms, width), 1) // head_size
+    group = math.gcd(heads, 4)
+    out_proj = weights[3]
 
     def stacked(array):
         zero = jnp.zeros_like(array)
         return jnp.concatenate([jnp.where(head_of == h, array, zero) for h in range(heads)], axis=0)
 
-    def stacked_t(array):
-        columns = []
+    def own_channels(turned, blocks):
+        parts = []
+        for h in range(0, heads, group):
+            channels = turned[h * head_size : (h + group) * head_size]
+            wide = dot(channels, blocks[:, h * atoms : (h + group) * atoms])
+            for i in range(group):
+                parts.append(wide[i * head_size : (i + 1) * head_size, i * atoms : (i + 1) * atoms])
+        return jnp.concatenate(parts, axis=0)
+
+    def forward(i):
+        normed, normed_t, ghosts, embedded, weight, absent, weight_rest, absent_rest, targets = bricks[i]
+        score_ref, att_ref, att_half, _ = memory[i]
+        norm = normed[...]
+        table = jnp.concatenate([norm, ghosts[...]], axis=0)
+        table_t = jnp.concatenate([normed_t[...], ghosts[...].astype(F32).T.astype(BF16)], axis=1)
+        query = stacked(dot(norm, weights[0]).astype(BF16))
+        keys = dot(table, weights[1])
+        values = dot(table, weights[2])
+        keys_t, values_t = keys.T.astype(BF16), values.T.astype(BF16)
+        keys, values = keys.astype(BF16), values.astype(BF16)
+        score_ref[...] = dot_nt(keys, query)
+        gone = jnp.concatenate([absent[...], absent_rest[...]], axis=0)
         for h in range(heads):
-            pieces = [array[h * head_size : (h + 1) * head_size]]
-            if h > 0:
-                pieces.insert(0, jnp.zeros((h * head_size, atoms), array.dtype))
-            if h + 1 < heads:
-                pieces.append(jnp.zeros((width - (h + 1) * head_size, atoms), array.dtype))
-            columns.append(jnp.concatenate(pieces, axis=0))
-        return jnp.concatenate(columns, axis=1)
-
-    def own_channels(wide):
-        return jnp.concatenate(
-            [wide[h * head_size : (h + 1) * head_size, h * atoms : (h + 1) * atoms] for h in range(heads)], axis=0
-        )
-
-    norm = normed[...]
-    table = jnp.concatenate([norm, ghosts[...]], axis=0)
-    query = dot(norm, weights[0])
-    keys = dot(table, weights[1]).astype(BF16)
-    values = dot(table, weights[2]).astype(BF16)
-    score_ref[...] = dot(keys, stacked_t(query.T.astype(BF16)))
-    gone = jnp.concatenate([absent[...], absent_rest[...]], axis=0)
-    for h in range(heads):
-        at = pl.ds(h * atoms, atoms)
-        score = score_ref[:, at] * scale + gone
-        weights_h = jnp.concatenate([weight[h], weight_rest[h]], axis=0)
-        terms = jnp.exp(score - jnp.max(score, axis=0, keepdims=True)) * weights_h
-        attention = terms * (1.0 / jnp.sum(terms, axis=0, keepdims=True))
-        att_ref[:, at] = attention
-        att_half[:, at] = attention.astype(BF16)
-    attended_t = own_channels(dot_tn(values, att_half[...]))
-    attended = attended_t.T.astype(BF16)
-
-    out_proj = weights[3]
-    updated = embedded[...] + dot(attended, out_proj)
-    sigmoid = 1.0 / (1.0 + jnp.exp(-updated))
-    energy = jnp.sum(readout[...] * (updated * sigmoid), axis=1, keepdims=True)
-    energies[...] = to_row(energy)
-    grad_energy = loss_weight * (energy - to_column(targets[...]))
-    slope = sigmoid * (1.0 + updated * (1.0 - sigmoid))
-    grad_updated = (grad_energy * readout[...] * slope).astype(BF16)
-    grads[3] = dot(attended_t.astype(BF16), grad_updated)
-    grad_attended = dot_nt(grad_updated, out_proj)
-
-    score_ref[...] = dot(values, stacked_t(grad_attended.T.astype(BF16)))
-    value_grads = dot(att_half[...], stacked(grad_attended.astype(BF16)))
-    grads[2] = dot_tn(table, value_grads.astype(BF16))
-    for h in range(heads):
-        at = pl.ds(h * atoms, atoms)
-        attention = att_ref[:, at]
-        grad_weights = score_ref[:, at]
-        mean = jnp.sum(attention * grad_weights, axis=0, keepdims=True)
-        grad_score[:, at] = (attention * (grad_weights - mean)).astype(BF16)
-    grad_query_t = own_channels(dot_tn(keys, grad_score[...])) * scale
-    grads[0] = dot_nt(normed_t[...], grad_query_t.astype(BF16))
-    key_grads = dot(grad_score[...], stacked(query.astype(BF16))) * scale
-    grads[1] = dot_tn(table, key_grads.astype(BF16))
+            at = pl.ds(h * atoms, atoms)
+            score = score_ref[:, at] + gone
+            weights_h = jnp.concatenate([weight[h], weight_rest[h]], axis=0)
+            score = (score - jnp.max(score, axis=0, keepdims=True)) * (scale * math.log2(math.e))
+            terms = jnp.exp2(score) * weights_h
+            attention = terms * (1.0 / jnp.sum(terms, axis=0, keepdims=True))
+            att_ref[:, at] = attention
+            att_half[:, at] = attention.astype(BF16)
+        return table_t, query, keys_t, values, own_channels(values_t, att_half[...])
+
+    def middle(i, attended_t):
+        embedded, targets = bricks[i][3], bricks[i][8]
+        updated = embedded[...] + dot(attended_t.T.astype(BF16), out_proj)
+        sigmoid = 1.0 / (1.0 + jnp.exp(-updated))
+        energy = jnp.sum(readout[...] * (updated * sigmoid), axis=1, keepdims=True)
+        if i == 0:
+            energies[...] = to_row(energy)
+        grad_energy = loss_weight * (energy - to_column(targets[...]))
+        slope = sigmoid * (1.0 + updated * (1.0 - sigmoid))
+        grad_updated = (grad_energy * readout[...] * slope).astype(BF16)
+        grad_out = dot(attended_t.astype(BF16), grad_updated)
+        return grad_out, stacked(dot_nt(grad_updated, out_proj).astype(BF16))
+
+    def backward(i, table_t, query, keys_t, values, grad_attended):
+        normed_t = bricks[i][1]
+        score_ref, att_ref, att_half, grad_score = memory[i]
+        score_ref[...] = dot_nt(values, grad_attended)
+        for h in range(heads):
+            at = pl.ds(h * atoms, atoms)
+            attention = att_ref[:, at]
+            grad_weights = score_ref[:, at]
+            mean = jnp.sum(attention * grad_weights, axis=0, keepdims=True)
+            grad_score[:, at] = (attention * (grad_weights - mean)).astype(BF16)
+        value_grads = dot(att_half[...], grad_attended)
+        grad_value = dot(table_t, value_grads.astype(BF16))
+        grad_query_t = own_channels(keys_t, grad_score[...]) * scale
+        grad_query = dot_nt(normed_t[...], grad_query_t.astype(BF16))
+        key_grads = dot(grad_score[...], query) * scale
+        return grad_query, dot(table_t, key_grads.astype(BF16)), grad_value
+
+    first = [forward(i) for i in range(count)]
+    second = [middle(i, first[i][4]) for i in range(count)]
+    third = [backward(i, *first[i][:4], second[i][1]) for i in range(count)]
+    for place in range(3):
+        grads[place] = sum(third[i][place] for i in range(1, count)) + third[0][place]
+    grads[3] = sum(second[i][0] for i in range(1, count)) + second[0][0]
 
 
 def vmem(count):
@@ -251,7 +300,7 @@
     return lax.ppermute(array, "cell", [(i, i ^ vector_of(i)) for i in range(cells)])
 
 
-def gather_cells(shard, cells, beside, first):
+def gather_cells(shard, cells, beside):
     place = lax.axis_index("cell")
     offsets = halvings(cells)[:-1]
     far, (a, b) = offsets[:-2], offsets[-2:]
@@ -259,13 +308,10 @@
     held = shard
     done = ()
 
-    def step(vectors, after=None):
+    def step(vectors):
         nonlocal done
         work = beside.pop(0)(*done) if beside else done
         arrived = [swap(held, cells, lambda i, vector=vector: vector) for vector in vectors]
-        if after is not None:
-            arrived[0], early = after(arrived[0])
-            work = (*work, early)
         done, arrived = lax.optimization_barrier((work, arrived))
         return arrived
 
@@ -276,7 +322,7 @@
     for offset in far:
         held = placed(held, step([crossing(offset, crossed)])[0], offset)
     vectors = [crossing(offset, crossed) for offset in (a, b)]
-    over_both, over_a, over_b = step([vectors[0] ^ vectors[1], *vectors], first)
+    over_both, over_a, over_b = step([vectors[0] ^ vectors[1], *vectors])
     held = placed(placed(held, over_b, b), placed(over_a, over_both, b), a)
     (arrived,) = step([1])
     count = len(offsets)
@@ -288,7 +334,7 @@
     return blocks.transpose(1, 0, 2, 3).reshape(shard.shape[0], -1, shard.shape[2]), done
 
 
-def reduce_all(parts, cells, bricks):
+def reduce_all(parts, cells, bricks, across):
     place = lax.axis_index("cell")
     tail = parts.shape[1:]
     left = halvings(cells)[:-1]
@@ -333,13 +379,15 @@
         return lax.ppermute(array, ("cell", "brick"), pairs).astype(F32)
 
     vector = crossing(farthest, crossed)
-    keep = portion(total, [(farthest, 0)]).astype(BF16)
+    keep = portion(total, [(farthest, 0)])
     send = portion(total, [(farthest, 1)]).astype(BF16)
+    if across:
+        keep = keep.astype(BF16)
     total = keep.astype(F32) + meet(send, vector, 0)
-    if bricks > 1:
-        far = meet(send, vector, 1)
-        total = total + (far + meet(keep, 0, 1))
-    for step in list(reversed(halvings(bricks)))[1:]:
+    if across:
+        far = meet(send, vector, across[0])
+        total = total + (far + meet(keep, 0, across[0]))
+    for step in across[1:]:
         keep = total.astype(BF16)
         total = keep.astype(F32) + meet(keep, 0, step)
     return total
@@ -369,85 +417,130 @@
     heads = head_decay.shape[0]
     table_rows = atoms + bricks * ghost_slots
 
-    kept = (neighbours[0, 0], counts[0], distances[0, 0], head_decay[None], readout[None], targets[0])
-
-    def embed():
-        return pl.pallas_call(
-            embed_kernel,
-            out_shape=(
-                pinned((atoms, width), F32),
-                pinned((atoms, width), BF16),
-                pinned((width, atoms), BF16),
-                pinned((bricks, ghost_slots, width), BF16),
-                *(pinned(array.shape, array.dtype) for array in kept),
-            ),
-            in_specs=vmem(5 + len(kept)),
-            out_specs=tuple(vmem(4 + len(kept))),
-            compiler_params=pltpu.CompilerParams(vmem_limit_bytes=4 * 1024 * 1024),
+    paired = bricks == 2 and table_rows <= 256
+    count = 2 if paired else 1
+    brick = lax.axis_index("brick")
+    part = table_rows // 2
+    own = (features[0, 0], species[0], send_lists[0, 0])
+    slot_arrays = (neighbours[0, 0], counts[0], distances[0, 0], targets[0])
+    common = (species_table, norm_gain[None])
+    embed_shapes = (
+        pinned((atoms, width), F32),
+        pinned((atoms, width), BF16),
+        pinned((width, atoms), BF16),
+        pinned((bricks, ghost_slots, width), BF16),
+    )
+    slot_shapes = tuple(pinned(array.shape, array.dtype) for array in slot_arrays)
+    small = pltpu.CompilerParams(vmem_limit_bytes=8 * 1024 * 1024)
+
+    def embed_own():
+        rest = (head_decay[None], readout[None], *common)
+        shapes = (pinned(master.shape, BF16),) + embed_shapes + slot_shapes
+        shapes += tuple(pinned(array.shape, array.dtype) for array in rest)
+        if paired:
+            shapes += (pinned((width + 4 * slots + PACK_ROWS, atoms), BF16),)
+        outs = pl.pallas_call(
+            functools.partial(embed_kernel, int(paired)),
+            out_shape=shapes,
+            in_specs=vmem(6 + len(slot_arrays) + len(rest)),
+            out_specs=tuple(vmem(len(shapes))),
             name="embed",
-        )(features[0, 0], species[0], species_table, norm_gain[None], send_lists[0, 0], *kept)
-
-    def exchange(embedded, normed, normed_t, parcel):
-        brick = lax.axis_index("brick")
-        ghosts = parcel
-        for offset in range(1, bricks):
-            peer = brick ^ offset
-            sent = lax.dynamic_index_in_dim(parcel, peer, 0, True)
-            arrived = lax.ppermute(sent, "brick", [(i, i ^ offset) for i in range(bricks)])
-            ghosts = lax.dynamic_update_slice_in_dim(ghosts, arrived, peer, 0)
-        return embedded, normed, normed_t, ghosts.reshape(bricks * ghost_slots, width)
-
-    part = table_rows // 2
-
-    def index(first, rows, valid, away, decay):
+        )(master, *own, *common, *slot_arrays, *rest)
+        return outs[0], outs[1:5], outs[5:9], outs[9:13], outs[13:]
+
+    def embed_partner(packed, *common):
+        outs = pl.pallas_call(
+            unpack_kernel,
+            out_shape=embed_shapes + slot_shapes,
+            in_specs=vmem(3),
+            out_specs=tuple(vmem(8)),
+            compiler_params=small,
+            name="unpack",
+        )(packed, *common)
+        return outs[:4], outs[4:]
+
+    def index(first, arrays, decay):
         return pl.pallas_call(
             functools.partial(index_kernel, first),
             out_shape=(pinned((heads, part, atoms), F32), pinned((part, atoms), F32)),
             in_specs=vmem(4),
             out_specs=tuple(vmem(2)),
             scratch_shapes=[pltpu.VMEM((slots, atoms), jnp.int32)],
-            compiler_params=pltpu.CompilerParams(vmem_limit_bytes=8 * 1024 * 1024),
+            compiler_params=small,
             name="index",
-        )(rows, valid, away, decay)
+        )(*arrays[:3], decay)
+
+    def over_bricks(array, offset):
+        return lax.ppermute(array, "brick", [(i, i ^ offset) for i in range(bricks)])
+
+    def ghosts_from(parcel):
+        ghosts = parcel
+        for offset in range(1, bricks):
+            peer = brick ^ offset
+            arrived = over_bricks(lax.dynamic_index_in_dim(parcel, peer, 0, True), offset)
+            ghosts = lax.dynamic_update_slice_in_dim(ghosts, arrived, peer, 0)
+        return ghosts.reshape(bricks * ghost_slots, width)
+
+    def ghosts_of(parcels, place):
+        chosen = [lax.dynamic_index_in_dim(parcel, place, 0, False) for parcel in parcels]
+        ordered = jnp.where(brick == 0, jnp.stack(chosen), jnp.stack(chosen[::-1]))
+        return ordered.reshape(bricks * ghost_slots, width)
+
+    late = []
+
+    shard, state, arrays, (decay, gain, *kept), packed = embed_own()
 
     def prepare():
-        done = embed()
-        return done[:4], done[4:8], done[8:], index(0, *done[4:8])
-
-    ghosts = []
-
-    def send(state, slot_arrays, held, half):
-        ghosts.append(state)
-        return held, half, index(part, *slot_arrays)
-
-    def start(arrived):
-        return arrived, exchange(*ghosts.pop())
-
-    def receive(held, half, rest, state):
-        return state, held, half, rest
-
-    steps = [prepare, *[lambda *done: done] * (len(halvings(cells)) - 4), send, receive]
-    weights, done = gather_cells(master.astype(BF16), cells, steps, start)
-    (embedded, normed, normed_t, ghosts), held, *halves = done
+        if paired:
+            late.extend([over_bricks(packed[0], 1), *kept])
+        return state, arrays, decay, gain, index(0, arrays, decay)
+
+    def gather_ghosts(state, arrays, decay, gain, half):
+        rows = ghosts_from(state[3])
+        return [(state, rows, arrays[3], half, index(part, arrays, decay))], gain
+
+    def visit_partner(state, arrays, decay, gain, half):
+        rest = index(part, arrays, decay)
+        partner, partner_arrays = embed_partner(*late)
+        partner_half = index(0, partner_arrays, decay)
+        return (state, arrays[3], half, rest), (partner, partner_arrays, partner_half), decay, gain
+
+    def finish_partner(mine, other, decay, gain):
+        state, wanted, half, rest = mine
+        partner, arrays, partner_half = other
+        parcels = (state[3], partner[3])
+        return [
+            (state, ghosts_of(parcels, brick), wanted, half, rest),
+            (partner, ghosts_of(parcels, 1 - brick), arrays[3], partner_half, index(part, arrays, decay)),
+        ], gain
+
+    steps = [prepare, *[lambda *done: done] * (len(halvings(cells)) - 4)]
+    steps += [visit_partner, finish_partner] if paired else [gather_ghosts]
+    weights, (worked, gain) = gather_cells(shard, cells, steps)
+    operands = []
+    for (embedded, normed, normed_t, _), ghosts, wanted, half, rest in worked:
+        operands += [normed, normed_t, ghosts, embedded, *half, *rest, wanted]
 
     columns = heads * atoms
     energies, grads = pl.pallas_call(
-        sweep_kernel,
+        functools.partial(sweep_kernel, count),
         out_shape=(struct((1, atoms), F32), struct((4, width, width), F32)),
-        in_specs=vmem(11),
+        in_specs=vmem(2 + len(operands)),
         out_specs=tuple(vmem(2)),
         scratch_shapes=[
             pltpu.VMEM((table_rows, columns), F32),
             pltpu.VMEM((table_rows, columns), F32),
             pltpu.VMEM((table_rows, columns), BF16),
             pltpu.VMEM((table_rows, columns), BF16),
-        ],
+        ]
+        * count,
         compiler_params=pltpu.CompilerParams(vmem_limit_bytes=32 * 1024 * 1024),
         name="sweep",
-    )(weights, normed, normed_t, ghosts, embedded, *halves[0], *halves[1], *held)
+    )(weights, gain, *operands)
 
     parts = grads.reshape(4, cells, width // cells, width).transpose(1, 0, 2, 3)
-    owned = reduce_all(parts, cells, bricks)
+    across = [] if paired else list(reversed(halvings(bricks)))
+    owned = reduce_all(parts, cells, bricks, across)
     moment_new = 0.9 * moment + 0.1 * owned
     second_new = 0.999 * second + 0.001 * owned * owned
     adam_step = moment_new / (jnp.sqrt(second_new) + 1e-08)

time: 37.9 us -> 37 us (0.976); the launches traced: 37.2 us -> 36.9 us
  Pallas kernels: 5.34 us -> 9.64 us
  waiting for transfers between devices: 12.3 us -> 10.6 us
  starting transfers between devices: 15.4 us -> 14.3 us
  other arithmetic: 2.22 us -> 1.27 us
  local copies, waits for them, and re-layouts: 1 us -> 0.23 us
    pallas_call x2 -> x3, Pallas kernels: 3.03 us -> 5.69 us  [the longest x1 4.01 us: body(): pl.pallas_call(functools.partial(sweep_kernel, count), out_shape=(struct(...]
    pallas_call x2 -> x4, Pallas kernels: 2.31 us -> 3.95 us  [index(): pl.pallas_call(functools.partial(index_kernel, first), out_shape=(pinned(...]
    ppermute x3 -> x1, starting transfers between devices: 4.17 us -> 2.82 us  [meet(): return lax.ppermute(array, ('cell', 'brick'), pairs).astype(F32)]
    ppermute x1, waiting for transfers between devices: 1.24 us -> 0.01 us  [over_bricks(): lax.ppermute(array, 'brick', [(i, i ^ offset) for i in range(bricks)])]
    ppermute x3 -> x1, waiting for transfers between devices: 3.6 us -> 2.4 us  [meet(): return lax.ppermute(array, ('cell', 'brick'), pairs).astype(F32)]
    convert_element_type x1 -> x0, other arithmetic: 0.91 us -> none  [body(): weights, done = gather_cells(master.astype(BF16), cells, steps, start)]
    unnamed x28 -> x4, local copies, waits for them, and re-layouts: 0.82 us -> 0.01 us
    ppermute x9, waiting for transfers between devices: 7.42 us -> 8.15 us  [swap(): lax.ppermute(array, 'cell', [(i, i ^ vector_of(i)) for i in range(cells)])]
  transfers between devices with their start and end apart: 13 -> 11, of which waited for: 10 -> 8; matrix products, arithmetic and copies ran while one was open for 0% -> 0% of each run, Pallas kernels for 7% -> 12%
where the time goes in v6:
time: 37 us; the launch traced here: 36.9 us
  starting transfers between devices  14.3 us (39%)
  waiting for transfers between devices  10.6 us (29%)
  Pallas kernels  9.64 us (26%)
  other arithmetic  1.27 us (3%)
  between operations  0.86 us (2%)
    ppermute x9, starting transfers between devices, swap(): lax.ppermute(array, 'cell', [(i, i ^ vector_of(i)) for i in range(cells)])  9.98 us
    ppermute x9, waiting for transfers between devices, swap(): lax.ppermute(array, 'cell', [(i, i ^ vector_of(i)) for i in range(cells)])  8.15 us
    pallas_call x1, Pallas kernels, body(): pl.pallas_call(functools.partial(sweep_kernel, count), out_shape=(struct(...  4.01 us
    pallas_call x4, Pallas kernels, index(): pl.pallas_call(functools.partial(index_kernel, first), out_shape=(pinned(...  3.95 us
    ppermute x1, starting transfers between devices, meet(): return lax.ppermute(array, ('cell', 'brick'), pairs).astype(F32)  2.82 us
    ppermute x1, waiting for transfers between devices, meet(): return lax.ppermute(array, ('cell', 'brick'), pairs).astype(F32)  2.4 us
    ppermute x1, starting transfers between devices, over_bricks(): lax.ppermute(array, 'brick', [(i, i ^ offset) for i in range(bricks)])  1.49 us
    pallas_call x1, Pallas kernels, embed_own(): pl.pallas_call(functools.partial(embed_kernel, int(paired)), out_shape=sh...  1.34 us
  transfers between devices with their start and end apart: 11, of which 8 were waited for; matrix products, arithmetic and copies ran while one was open for 0% of the time, Pallas kernels for 12%

profile of v6, /device:TPU:0, one launch (start us, length us, event | category | flops | bytes accessed | tf_op | source)
XLA Modules:
  0.0 36.9 jit_solution(14777928443300600666)
XLA Ops:
  0.6 1.3 %embed.1 = (bf16[4,16,256]{2,1,0:T(8,128)(2,1)S(1)}, f32[128,256]{1,0:T(8,128)S(1)}, bf16[128,256]{1,0:T(8,128)(2,1)S(1)}, bf16[256,128]{1,0:T(8,128)(2,1)S(1)},...) custom-call(f32[4,16,256]{2,1,0:T(8,128)} %master.1, ...), custom_call_target="tpu_custom_call" | custom-call | tf_op jit(solution)/shard_map/embed/pallas_call | solution.py:442
  2.0 3.5 %collective-permute-start = (bf16[4,16,256]{2,1,0:T(8,128)(2,1)S(1)}, bf16[4,16,256]{2,1,0:T(8,128)(2,1)S(1)}, u32[]{:S(2)}, u32[]{:S(2)}) collective-permute-start(bf16[4,16,256]{2,1,0:T(8,128)(2,1)S(1)} %get-tuple-element.93), channel_id=1, source_target_pairs={{0,18},{2,16},{4,22},{6,20},{8,26},{10,24},{12,30},{14,28},{16,2},... | collective-permute-start | bytes 98312 | tf_op jit(solution)/shard_map/ppermute | solution.py:300
  5.5 1.5 %collective-permute-start.1 = (bf16[528,128]{1,0:T(8,128)(2,1)S(1)}, bf16[528,128]{1,0:T(8,128)(2,1)S(1)}, u32[]{:S(2)}, u32[]{:S(2)}) collective-permute-start(bf16[528,128]{1,0:T(8,128)(2,1)S(1)} %get-tuple-element.120), channel_id=1, source_target_pairs={{0,1},{1,0},{2,3},{3,2},{4,5},{5,4},{6,7},{7,6},{8,9},{9,8},{10,11... | collective-permute-start | bytes 405512 | tf_op jit(solution)/shard_map/ppermute | solution.py:474
  7.1 1.0 %index.4 = (f32[8,96,128]{2,1,0:T(8,128)S(1)}, f32[96,128]{1,0:T(8,128)S(1)}) custom-call(s32[64,128]{1,0:T(8,128)S(1)} %get-tuple-element.114.neighbours, s32[1,128]{1,0:T(1,128)S(1)} %get-tuple-element.115.counts, f32[64,128]{1,0:T(8,128)S(1)} %get-tuple-element.116.distances, f32[1,8]{1,0:T(1,128)S(1)} %get-tuple-element.156.decay), custom_call_target="tpu_custom_call" | custom-call | tf_op jit(solution)/shard_map/index/pallas_call | solution.py:463
  8.1 0.0 collective-permute-done
  8.1 2.6 %collective-permute-start.2 = (bf16[2,4,16,256]{3,2,1,0:T(8,128)(2,1)S(1)}, bf16[2,4,16,256]{3,2,1,0:T(8,128)(2,1)S(1)}, u32[]{:S(2)}, u32[]{:S(2)}) collective-permute-start(bf16[2,4,16,256]{3,2,1,0:T(8,128)(2,1)S(1)} %maximum_select_fusion.4), channel_id=1, source_target_pairs={{0,14},{2,12},{4,10},{6,8},{8,6},{10,4},{12,2},{14,0},{16,30},{18,... | collective-permute-start | bytes 196616 | tf_op jit(solution)/shard_map/ppermute | solution.py:300
  10.8 0.4 %collective-permute-start.3 = (bf16[2,4,16,256]{3,2,1,0:T(8,128)(2,1)S(1)}, bf16[2,4,16,256]{3,2,1,0:T(8,128)(2,1)S(1)}, u32[]{:S(2)}, u32[]{:S(2)}) collective-permute-start(bf16[2,4,16,256]{3,2,1,0:T(8,128)(2,1)S(1)} %maximum_select_fusion.4), channel_id=1, source_target_pairs={{0,8},{2,10},{4,12},{6,14},{8,0},{10,2},{12,4},{14,6},{16,24},{18,... | collective-permute-start | bytes 196616 | tf_op jit(solution)/shard_map/ppermute | solution.py:300
  11.2 0.0 collective-permute-start.4
  11.2 1.0 %index.5 = (f32[8,96,128]{2,1,0:T(8,128)S(1)}, f32[96,128]{1,0:T(8,128)S(1)}) custom-call(s32[64,128]{1,0:T(8,128)S(1)} %get-tuple-element.114.neighbours, s32[1,128]{1,0:T(1,128)S(1)} %get-tuple-element.115.counts, f32[64,128]{1,0:T(8,128)S(1)} %get-tuple-element.116.distances, f32[1,8]{1,0:T(1,128)S(1)} %get-tuple-element.156.decay), custom_call_target="tpu_custom_call" | custom-call | tf_op jit(solution)/shard_map/index/pallas_call | solution.py:463
  12.2 0.0 collective-permute-done.1.packed
  12.2 0.3 unpack.1
  12.6 1.0 %index.6 = (f32[8,96,128]{2,1,0:T(8,128)S(1)}, f32[96,128]{1,0:T(8,128)S(1)}) custom-call(s32[64,128]{1,0:T(8,128)S(1)} %get-tuple-element.153.neighbours, s32[1,128]{1,0:T(1,128)S(1)} %get-tuple-element.154.counts, f32[64,128]{1,0:T(8,128)S(1)} %get-tuple-element.155.distances, f32[1,8]{1,0:T(1,128)S(1)} %get-tuple-element.156.decay), custom_call_target="tpu_custom_call" | custom-call | tf_op jit(solution)/shard_map/index/pallas_call | solution.py:463
  13.6 0.0 collective-permute-done.2
  13.6 1.4 %collective-permute-done.3 = bf16[2,4,16,256]{3,2,1,0:T(8,128)(2,1)S(1)} collective-permute-done((bf16[2,4,16,256]{3,2,1,0:T(8,128)(2,1)S(1)}, bf16[2,4,16,256]{3,2,1,0:T(8,128)(2,1)S(1)}, u32[]{:S(2)}, u32[]{:S(2)}) %collective-permute-start.3) | collective-permute-done | bytes 65568 | tf_op jit(solution)/shard_map/ppermute | solution.py:300
  15.0 0.6 %collective-permute-done.4 = bf16[2,4,16,256]{3,2,1,0:T(8,128)(2,1)S(1)} collective-permute-done((bf16[2,4,16,256]{3,2,1,0:T(8,128)(2,1)S(1)}, bf16[2,4,16,256]{3,2,1,0:T(8,128)(2,1)S(1)}, u32[]{:S(2)}, u32[]{:S(2)}) %collective-permute-start.4) | collective-permute-done | bytes 65568 | tf_op jit(solution)/shard_map/ppermute | solution.py:300
  15.6 0.2 collective-permute-start.5
  15.8 1.0 %index.7 = (f32[8,96,128]{2,1,0:T(8,128)S(1)}, f32[96,128]{1,0:T(8,128)S(1)}) custom-call(s32[64,128]{1,0:T(8,128)S(1)} %get-tuple-element.153.neighbours, s32[1,128]{1,0:T(1,128)S(1)} %get-tuple-element.154.counts, f32[64,128]{1,0:T(8,128)S(1)} %get-tuple-element.155.distances, f32[1,8]{1,0:T(1,128)S(1)} %get-tuple-element.156.decay), custom_call_target="tpu_custom_call" | custom-call | tf_op jit(solution)/shard_map/index/pallas_call | solution.py:463
  16.8 0.4 %collective-permute-done.5 = bf16[2,2,2,4,16,256]{5,4,3,2,1,0:T(8,128)(2,1)S(1)} collective-permute-done((bf16[2,2,2,4,16,256]{5,4,3,2,1,0:T(8,128)(2,1)S(1)}, bf16[2,2,2,4,16,256]{5,4,3,2,1,0:T(8,128)(2,1)S(1)}, u32[]{:S(2)}, u32[]{:S(2)}) %collective-permute-start.5) | collective-permute-done | bytes 262176 | tf_op jit(solution)/shard_map/ppermute | solution.py:300
  17.2 0.1 fusion
  17.4 0.1 pad_maximum_fusion
  17.5 4.0 %sweep.1 = (f32[1,128]{1,0:T(1,128)}, f32[4,256,256]{2,1,0:T(8,128)S(1)}) custom-call(bf16[4,256,256]{2,1,0:T(8,128)(2,1)S(1)} %bitcast.92, f32[1,256]{1,0:T(1,128)S(1)} %get-tuple-element.161.readout, bf16[128,256]{1,0:T(8,128)(2,1)S(1)} %get-tuple-element.162.refs_0_, bf16[256,128]{1,0:T(8,128)(2,1)S(1)} %get-tuple-element.163.refs_1_, ...), custom_call_target="tpu_custom_call" | custom-call | tf_op jit(solution)/shard_map/sweep/pallas_call | solution.py:525
  21.5 0.1 copy.25
  21.6 0.1 select_convert_fusion
  21.7 0.2 collective-permute-start.6
  21.9 1.4 %collective-permute-done.6 = bf16[8,4,16,256]{3,2,1,0:T(8,128)(2,1)S(1)} collective-permute-done((bf16[8,4,16,256]{3,2,1,0:T(8,128)(2,1)S(1)}, bf16[8,4,16,256]{3,2,1,0:T(8,128)(2,1)S(1)}, u32[]{:S(2)}, u32[]{:S(2)}) %collective-permute-start.6) | collective-permute-done | bytes 262176 | tf_op jit(solution)/shard_map/ppermute | solution.py:300
  23.3 0.1 convert_add_fusion
  23.5 1.4 %collective-permute-start.7 = (bf16[2,4,16,256]{3,2,1,0:T(8,128)(2,1)S(1)}, bf16[2,4,16,256]{3,2,1,0:T(8,128)(2,1)S(1)}, u32[]{:S(2)}, u32[]{:S(2)}) collective-permute-start(bf16[2,4,16,256]{3,2,1,0:T(8,128)(2,1)S(1)} %get-tuple-element.187), channel_id=1, source_target_pairs={{0,10},{2,8},{4,14},{6,12},{8,2},{10,0},{12,6},{14,4},{16,26},{18,... | collective-permute-start | bytes 196616 | tf_op jit(solution)/shard_map/ppermute | solution.py:300
  24.9 0.9 %collective-permute-start.8 = (bf16[2,4,16,256]{3,2,1,0:T(8,128)(2,1)S(1)}, bf16[2,4,16,256]{3,2,1,0:T(8,128)(2,1)S(1)}, u32[]{:S(2)}, u32[]{:S(2)}) collective-permute-start(bf16[2,4,16,256]{3,2,1,0:T(8,128)(2,1)S(1)} %get-tuple-element.189), channel_id=1, source_target_pairs={{0,4},{2,6},{4,0},{6,2},{8,12},{10,14},{12,8},{14,10},{16,20},{18,... | collective-permute-start | bytes 196616 | tf_op jit(solution)/shard_map/ppermute | solution.py:300
  25.8 0.7 %collective-permute-start.9 = (bf16[2,4,16,256]{3,2,1,0:T(8,128)(2,1)S(1)}, bf16[2,4,16,256]{3,2,1,0:T(8,128)(2,1)S(1)}, u32[]{:S(2)}, u32[]{:S(2)}) collective-permute-start(bf16[2,4,16,256]{3,2,1,0:T(8,128)(2,1)S(1)} %get-tuple-element.188), channel_id=1, source_target_pairs={{0,14},{2,12},{4,10},{6,8},{8,6},{10,4},{12,2},{14,0},{16,30},{18,... | collective-permute-start | bytes 196616 | tf_op jit(solution)/shard_map/ppermute | solution.py:300
  26.5 1.1 %collective-permute-done.7 = bf16[2,4,16,256]{3,2,1,0:T(8,128)(2,1)S(1)} collective-permute-done((bf16[2,4,16,256]{3,2,1,0:T(8,128)(2,1)S(1)}, bf16[2,4,16,256]{3,2,1,0:T(8,128)(2,1)S(1)}, u32[]{:S(2)}, u32[]{:S(2)}) %collective-permute-start.7) | collective-permute-done | bytes 65568 | tf_op jit(solution)/shard_map/ppermute | solution.py:300
  27.7 1.6 %collective-permute-done.8 = bf16[2,4,16,256]{3,2,1,0:T(8,128)(2,1)S(1)} collective-permute-done((bf16[2,4,16,256]{3,2,1,0:T(8,128)(2,1)S(1)}, bf16[2,4,16,256]{3,2,1,0:T(8,128)(2,1)S(1)}, u32[]{:S(2)}, u32[]{:S(2)}) %collective-permute-start.8) | collective-permute-done | bytes 65568 | tf_op jit(solution)/shard_map/ppermute | solution.py:300
  29.3 1.6 %collective-permute-done.9 = bf16[2,4,16,256]{3,2,1,0:T(8,128)(2,1)S(1)} collective-permute-done((bf16[2,4,16,256]{3,2,1,0:T(8,128)(2,1)S(1)}, bf16[2,4,16,256]{3,2,1,0:T(8,128)(2,1)S(1)}, u32[]{:S(2)}, u32[]{:S(2)}) %collective-permute-start.9) | collective-permute-done | bytes 65568 | tf_op jit(solution)/shard_map/ppermute | solution.py:300
  30.9 0.0 copy-start.1
  30.9 0.0 copy-start
  30.9 2.8 %collective-permute-start.10 = (bf16[4,16,256]{2,1,0:T(8,128)(2,1)S(1)}, bf16[4,16,256]{2,1,0:T(8,128)(2,1)S(1)}, u32[]{:S(2)}, u32[]{:S(2)}) collective-permute-start(bf16[4,16,256]{2,1,0:T(8,128)(2,1)S(1)} %fusion.9), channel_id=1, source_target_pairs={{0,18},{1,19},{2,16},{3,17},{4,22},{5,23},{6,20},{7,21},{8,26},{9,... | collective-permute-start | bytes 98312 | tf_op jit(solution)/shard_map/ppermute | solution.py:379
  33.8 2.4 %collective-permute-done.10 = bf16[4,16,256]{2,1,0:T(8,128)(2,1)S(1)} collective-permute-done((bf16[4,16,256]{2,1,0:T(8,128)(2,1)S(1)}, bf16[4,16,256]{2,1,0:T(8,128)(2,1)S(1)}, u32[]{:S(2)}, u32[]{:S(2)}) %collective-permute-start.10) | collective-permute-done | bytes 32800 | tf_op jit(solution)/shard_map/ppermute | solution.py:379
  36.2 0.0 copy-done.1
  36.2 0.0 copy-done
  36.2 0.7 %add_divide_fusion = (f32[4,16,256]{2,1,0:T(8,128)}, f32[4,16,256]{2,1,0:T(8,128)}, f32[4,16,256]{2,1,0:T(8,128)}) fusion(bf16[4,16,256]{2,1,0:T(8,128)(2,1)S(1)} %collective-permute-done.10, f32[2,4,16,256]{3,2,1,0:T(8,128)S(1)} %fusion.3, s32[]{:T(128)S(6)} %select_n.325, f32[4,16,256]{2,1,0:T(8,128)S(1)} %copy-done, f32[4,16,256]{2,1,0:T(8,128)S(1)} %copy-done.1), kind=kLoop, calls=%fused_computation.27 | loop fusion | flops 180224 | bytes 425988 | tf_op jit(solution)/shard_map/div | solution.py:546
  (14 shorter events, 0.3 us)
Async XLA Ops:
  2.0 6.1 %collective-permute-start = (bf16[4,16,256]{2,1,0:T(8,128)(2,1)S(1)}, bf16[4,16,256]{2,1,0:T(8,128)(2,1)S(1)}, u32[]{:S(2)}, u32[]{:S(2)}) collective-permute-start(bf16[4,16,256]{2,1,0:T(8,128)(2,1)S(1)} %get-tuple-element.93), channel_id=1, source_target_pairs={{0,18},{2,16},{4,22},{6,20},{8,26},{10,24},{12,30},{14,28},{16,2},... | collective-permute-start | bytes 98312 | tf_op jit(solution)/shard_map/ppermute | solution.py:300
  5.5 6.7 %collective-permute-start.1 = (bf16[528,128]{1,0:T(8,128)(2,1)S(1)}, bf16[528,128]{1,0:T(8,128)(2,1)S(1)}, u32[]{:S(2)}, u32[]{:S(2)}) collective-permute-start(bf16[528,128]{1,0:T(8,128)(2,1)S(1)} %get-tuple-element.120), channel_id=1, source_target_pairs={{0,1},{1,0},{2,3},{3,2},{4,5},{5,4},{6,7},{7,6},{8,9},{9,8},{10,11... | collective-permute-start | bytes 405512 | tf_op jit(solution)/shard_map/ppermute | solution.py:474
  8.1 5.5 %collective-permute-start.2 = (bf16[2,4,16,256]{3,2,1,0:T(8,128)(2,1)S(1)}, bf16[2,4,16,256]{3,2,1,0:T(8,128)(2,1)S(1)}, u32[]{:S(2)}, u32[]{:S(2)}) collective-permute-start(bf16[2,4,16,256]{3,2,1,0:T(8,128)(2,1)S(1)} %maximum_select_fusion.4), channel_id=1, source_target_pairs={{0,14},{2,12},{4,10},{6,8},{8,6},{10,4},{12,2},{14,0},{16,30},{18,... | collective-permute-start | bytes 196616 | tf_op jit(solution)/shard_map/ppermute | solution.py:300
  10.8 4.3 %collective-permute-start.3 = (bf16[2,4,16,256]{3,2,1,0:T(8,128)(2,1)S(1)}, bf16[2,4,16,256]{3,2,1,0:T(8,128)(2,1)S(1)}, u32[]{:S(2)}, u32[]{:S(2)}) collective-permute-start(bf16[2,4,16,256]{3,2,1,0:T(8,128)(2,1)S(1)} %maximum_select_fusion.4), channel_id=1, source_target_pairs={{0,8},{2,10},{4,12},{6,14},{8,0},{10,2},{12,4},{14,6},{16,24},{18,... | collective-permute-start | bytes 196616 | tf_op jit(solution)/shard_map/ppermute | solution.py:300
  11.2 4.4 %collective-permute-start.4 = (bf16[2,4,16,256]{3,2,1,0:T(8,128)(2,1)S(1)}, bf16[2,4,16,256]{3,2,1,0:T(8,128)(2,1)S(1)}, u32[]{:S(2)}, u32[]{:S(2)}) collective-permute-start(bf16[2,4,16,256]{3,2,1,0:T(8,128)(2,1)S(1)} %maximum_select_fusion.4), channel_id=1, source_target_pairs={{0,6},{2,4},{4,2},{6,0},{8,14},{10,12},{12,10},{14,8},{16,22},{18,... | collective-permute-start | bytes 196616 | tf_op jit(solution)/shard_map/ppermute | solution.py:300
  15.6 1.6 %collective-permute-start.5 = (bf16[2,2,2,4,16,256]{5,4,3,2,1,0:T(8,128)(2,1)S(1)}, bf16[2,2,2,4,16,256]{5,4,3,2,1,0:T(8,128)(2,1)S(1)}, u32[]{:S(2)}, u32[]{:S(2)}) collective-permute-start(bf16[2,2,2,4,16,256]{5,4,3,2,1,0:T(8,128)(2,1)S(1)} %maximum_select_fusion), channel_id=1, source_target_pairs={{0,2},{2,0},{4,6},{6,4},{8,10},{10,8},{12,14},{14,12},{16,18},{18,... | collective-permute-start | bytes 786440 | tf_op jit(solution)/shard_map/ppermute | solution.py:300
  21.7 1.6 %collective-permute-start.6 = (bf16[8,4,16,256]{3,2,1,0:T(8,128)(2,1)S(1)}, bf16[8,4,16,256]{3,2,1,0:T(8,128)(2,1)S(1)}, u32[]{:S(2)}, u32[]{:S(2)}) collective-permute-start(bf16[8,4,16,256]{3,2,1,0:T(8,128)(2,1)S(1)} %select_convert_fusion), channel_id=1, source_target_pairs={{0,2},{2,0},{4,6},{6,4},{8,10},{10,8},{12,14},{14,12},{16,18},{18,... | collective-permute-start | bytes 786440 | tf_op jit(solution)/shard_map/ppermute | solution.py:300
  23.5 4.1 %collective-permute-start.7 = (bf16[2,4,16,256]{3,2,1,0:T(8,128)(2,1)S(1)}, bf16[2,4,16,256]{3,2,1,0:T(8,128)(2,1)S(1)}, u32[]{:S(2)}, u32[]{:S(2)}) collective-permute-start(bf16[2,4,16,256]{3,2,1,0:T(8,128)(2,1)S(1)} %get-tuple-element.187), channel_id=1, source_target_pairs={{0,10},{2,8},{4,14},{6,12},{8,2},{10,0},{12,6},{14,4},{16,26},{18,... | collective-permute-start | bytes 196616 | tf_op jit(solution)/shard_map/ppermute | solution.py:300
  24.9 4.4 %collective-permute-start.8 = (bf16[2,4,16,256]{3,2,1,0:T(8,128)(2,1)S(1)}, bf16[2,4,16,256]{3,2,1,0:T(8,128)(2,1)S(1)}, u32[]{:S(2)}, u32[]{:S(2)}) collective-permute-start(bf16[2,4,16,256]{3,2,1,0:T(8,128)(2,1)S(1)} %get-tuple-element.189), channel_id=1, source_target_pairs={{0,4},{2,6},{4,0},{6,2},{8,12},{10,14},{12,8},{14,10},{16,20},{18,... | collective-permute-start | bytes 196616 | tf_op jit(solution)/shard_map/ppermute | solution.py:300
  25.8 5.0 %collective-permute-start.9 = (bf16[2,4,16,256]{3,2,1,0:T(8,128)(2,1)S(1)}, bf16[2,4,16,256]{3,2,1,0:T(8,128)(2,1)S(1)}, u32[]{:S(2)}, u32[]{:S(2)}) collective-permute-start(bf16[2,4,16,256]{3,2,1,0:T(8,128)(2,1)S(1)} %get-tuple-element.188), channel_id=1, source_target_pairs={{0,14},{2,12},{4,10},{6,8},{8,6},{10,4},{12,2},{14,0},{16,30},{18,... | collective-permute-start | bytes 196616 | tf_op jit(solution)/shard_map/ppermute | solution.py:300
  30.9 5.3 %copy-start.1 = (f32[4,16,256]{2,1,0:T(8,128)S(1)}, f32[4,16,256]{2,1,0:T(8,128)}, u32[]{:S(2)}) copy-start(f32[4,16,256]{2,1,0:T(8,128)} %param.26) | copy-start | bytes 196612
  30.9 5.3 %copy-start = (f32[4,16,256]{2,1,0:T(8,128)S(1)}, f32[4,16,256]{2,1,0:T(8,128)}, u32[]{:S(2)}) copy-start(f32[4,16,256]{2,1,0:T(8,128)} %param.27) | copy-start | bytes 196612
  30.9 5.2 %collective-permute-start.10 = (bf16[4,16,256]{2,1,0:T(8,128)(2,1)S(1)}, bf16[4,16,256]{2,1,0:T(8,128)(2,1)S(1)}, u32[]{:S(2)}, u32[]{:S(2)}) collective-permute-start(bf16[4,16,256]{2,1,0:T(8,128)(2,1)S(1)} %fusion.9), channel_id=1, source_target_pairs={{0,18},{1,19},{2,16},{3,17},{4,22},{5,23},{6,20},{7,21},{8,26},{9,... | collective-permute-start | bytes 98312 | tf_op jit(solution)/shard_map/ppermute | solution.py:379

commit v7 on v6

--- a/solution.py
+++ b/solution.py
@@ -170,46 +170,46 @@
         lax.fori_loop(DEPTH, jnp.max(rank) + 1, layer, 0)
 
 
-def sweep_kernel(count, weights, readout, *refs):
+def sweep_kernel(count, cells, held, arrived, readout, *refs):
     operands, scratch = 9, 4
-    energies, grads = refs[operands * count : operands * count + 2]
+    energies, keep, send = refs[operands * count : operands * count + 3]
     bricks = [refs[operands * i : operands * (i + 1)] for i in range(count)]
-    start = operands * count + 2
+    start = operands * count + 3
+    weights = refs[-1]
+    assemble(held, arrived, weights, cells)
     memory = [refs[start + scratch * i : start + scratch * (i + 1)] for i in range(count)]
     atoms, width = bricks[0][0].shape
     heads = bricks[0][4].shape[0]
     head_size = width // heads
     scale = 1.0 / math.sqrt(head_size)
     head_of = lax.broadcasted_iota(jnp.int32, (atoms, width), 1) // head_size
-    group = math.gcd(heads, 4)
+    group = math.gcd(heads, 2)
     out_proj = weights[3]
 
     def stacked(array):
         zero = jnp.zeros_like(array)
         return jnp.concatenate([jnp.where(head_of == h, array, zero) for h in range(heads)], axis=0)
 
-    def own_channels(turned, blocks):
-        parts = []
-        for h in range(0, heads, group):
-            channels = turned[h * head_size : (h + group) * head_size]
-            wide = dot(channels, blocks[:, h * atoms : (h + group) * atoms])
-            for i in range(group):
-                parts.append(wide[i * head_size : (i + 1) * head_size, i * atoms : (i + 1) * atoms])
-        return jnp.concatenate(parts, axis=0)
-
-    def forward(i):
+    def own_channels(turned, blocks, h):
+        channels = turned[h * head_size : (h + group) * head_size]
+        wide = dot(channels, blocks[:, h * atoms : (h + group) * atoms])
+        return [wide[i * head_size : (i + 1) * head_size, i * atoms : (i + 1) * atoms] for i in range(group)]
+
+    def work(i):
         normed, normed_t, ghosts, embedded, weight, absent, weight_rest, absent_rest, targets = bricks[i]
-        score_ref, att_ref, att_half, _ = memory[i]
+        score_ref, att_ref, att_half, grad_score = memory[i]
         norm = normed[...]
         table = jnp.concatenate([norm, ghosts[...]], axis=0)
-        table_t = jnp.concatenate([normed_t[...], ghosts[...].astype(F32).T.astype(BF16)], axis=1)
         query = stacked(dot(norm, weights[0]).astype(BF16))
         keys = dot(table, weights[1])
         values = dot(table, weights[2])
+        yield
         keys_t, values_t = keys.T.astype(BF16), values.T.astype(BF16)
         keys, values = keys.astype(BF16), values.astype(BF16)
         score_ref[...] = dot_nt(keys, query)
+        yield
         gone = jnp.concatenate([absent[...], absent_rest[...]], axis=0)
+        parts = []
         for h in range(heads):
             at = pl.ds(h * atoms, atoms)
             score = score_ref[:, at] + gone
@@ -219,10 +219,10 @@
             attention = terms * (1.0 / jnp.sum(terms, axis=0, keepdims=True))
             att_ref[:, at] = attention
             att_half[:, at] = attention.astype(BF16)
-        return table_t, query, keys_t, values, own_channels(values_t, att_half[...])
-
-    def middle(i, attended_t):
-        embedded, targets = bricks[i][3], bricks[i][8]
+            if h % group == group - 1:
+                parts += own_channels(values_t, att_half, h - group + 1)
+        attended_t = jnp.concatenate(parts, axis=0)
+        yield
         updated = embedded[...] + dot(attended_t.T.astype(BF16), out_proj)
         sigmoid = 1.0 / (1.0 + jnp.exp(-updated))
         energy = jnp.sum(readout[...] * (updated * sigmoid), axis=1, keepdims=True)
@@ -231,32 +231,48 @@
         grad_energy = loss_weight * (energy - to_column(targets[...]))
         slope = sigmoid * (1.0 + updated * (1.0 - sigmoid))
         grad_updated = (grad_energy * readout[...] * slope).astype(BF16)
+        yield
         grad_out = dot(attended_t.astype(BF16), grad_updated)
-        return grad_out, stacked(dot_nt(grad_updated, out_proj).astype(BF16))
-
-    def backward(i, table_t, query, keys_t, values, grad_attended):
-        normed_t = bricks[i][1]
-        score_ref, att_ref, att_half, grad_score = memory[i]
+        grad_attended = stacked(dot_nt(grad_updated, out_proj).astype(BF16))
+        yield
         score_ref[...] = dot_nt(values, grad_attended)
+        yield
+        table_t = jnp.concatenate([normed_t[...], ghosts[...].astype(F32).T.astype(BF16)], axis=1)
+        value_grads = dot(att_half[...], grad_attended)
+        grad_value = dot(table_t, value_grads.astype(BF16))
+        yield
+        parts = []
         for h in range(heads):
             at = pl.ds(h * atoms, atoms)
             attention = att_ref[:, at]
             grad_weights = score_ref[:, at]
             mean = jnp.sum(attention * grad_weights, axis=0, keepdims=True)
             grad_score[:, at] = (attention * (grad_weights - mean)).astype(BF16)
-        value_grads = dot(att_half[...], grad_attended)
-        grad_value = dot(table_t, value_grads.astype(BF16))
-        grad_query_t = own_channels(keys_t, grad_score[...]) * scale
+            if h % group == group - 1:
+                parts += own_channels(keys_t, grad_score, h - group + 1)
+        yield
+        key_grads = dot(grad_score[...], query) * scale
+        yield
+        grad_query_t = jnp.concatenate(parts, axis=0) * scale
         grad_query = dot_nt(normed_t[...], grad_query_t.astype(BF16))
-        key_grads = dot(grad_score[...], query) * scale
-        return grad_query, dot(table_t, key_grads.astype(BF16)), grad_value
-
-    first = [forward(i) for i in range(count)]
-    second = [middle(i, first[i][4]) for i in range(count)]
-    third = [backward(i, *first[i][:4], second[i][1]) for i in range(count)]
-    for place in range(3):
-        grads[place] = sum(third[i][place] for i in range(1, count)) + third[0][place]
-    grads[3] = sum(second[i][0] for i in range(1, count)) + second[0][0]
+        yield grad_query, dot(table_t, key_grads.astype(BF16)), grad_value, grad_out
+
+    running = [work(i) for i in range(count)]
+    found = [None] * count
+    while found[0] is None:
+        found = [next(step) for step in running]
+    crossed = reduce_groups(cells)[3]
+    place = lax.axis_index("cell")
+    core = place % 2
+    for offset in crossed:
+        core = core ^ ((place // offset) % 2)
+    for matrix in range(4):
+        total = sum(part[matrix] for part in found[1:]) + found[0][matrix]
+        blocks = total.reshape((cells // 2, 2) + keep.shape[2:])
+        for k in range(cells // 2):
+            first = core == sum(2 * k // offset for offset in crossed) % 2
+            keep[k, matrix] = jnp.where(first, blocks[k, 0], blocks[k, 1])
+            send[k, matrix] = jnp.where(first, blocks[k, 1], blocks[k, 0]).astype(BF16)
 
 
 def vmem(count):
@@ -287,15 +303,6 @@
     return offset | 1 if offset in crossed else offset
 
 
-def own_core(cells, crossed):
-    place = lax.axis_index("cell")
-    blocks = 2 * jnp.arange(cells // 2)
-    core = jnp.full((cells // 2,), place % 2)
-    for offset in crossed:
-        core = core ^ ((blocks // offset) % 2) ^ ((place // offset) % 2)
-    return core
-
-
 def swap(array, cells, vector_of):
     return lax.ppermute(array, "cell", [(i, i ^ vector_of(i)) for i in range(cells)])
 
@@ -325,27 +332,41 @@
     over_both, over_a, over_b = step([vectors[0] ^ vectors[1], *vectors])
     held = placed(placed(held, over_b, b), placed(over_a, over_both, b), a)
     (arrived,) = step([1])
-    count = len(offsets)
-    order = (*reversed(range(2, count)), 0, 1, *range(count, held.ndim))
-    held, arrived = held.transpose(order), arrived.transpose(order)
-    core = own_core(cells, crossed).reshape((2,) * count + (1,) * shard.ndim)
-    pair = [jnp.where(core == 0, held, arrived), jnp.where(core == 0, arrived, held)]
-    blocks = jnp.stack(pair, axis=count).reshape((cells,) + shard.shape)
-    return blocks.transpose(1, 0, 2, 3).reshape(shard.shape[0], -1, shard.shape[2]), done
-
-
-def reduce_all(parts, cells, bricks, across):
+    return held, arrived, done
+
+
+def assemble(held, arrived, weights, cells):
+    offsets = halvings(cells)[:-1]
+    far, (a, b) = offsets[:-2], offsets[-2:]
+    crossed = [*far, b]
     place = lax.axis_index("cell")
-    tail = parts.shape[1:]
+    core = place % 2
+    for offset in crossed:
+        core = core ^ ((place // offset) % 2)
+    matrices, rows, _ = held.shape[-3:]
+    for k in range(cells // 2):
+        at = tuple(2 * k // offset % 2 for offset in (a, b, *reversed(far)))
+        first = core == sum(2 * k // offset for offset in crossed) % 2
+        for matrix in range(matrices):
+            own, other = held[(*at, matrix)], arrived[(*at, matrix)]
+            pair = [jnp.where(first, own, other), jnp.where(first, other, own)]
+            if rows % 16:
+                pair = [part.astype(F32) for part in pair]
+            weights[matrix, 2 * k * rows : 2 * (k + 1) * rows, :] = jnp.concatenate(pair, axis=0).astype(BF16)
+
+
+def reduce_groups(cells):
     left = halvings(cells)[:-1]
     near, middle, farthest = left[-2:], left[1:-2], left[0]
-    crossed = [near[0], *middle, farthest]
-    parts = parts.reshape((cells // 2, 2) + tail)
-    core = own_core(cells, crossed).reshape((cells // 2,) + (1,) * len(tail))
-    keep = jnp.where(core == 0, parts[:, 0], parts[:, 1])
-    send = jnp.where(core == 0, parts[:, 1], parts[:, 0])
-    total = keep + swap(send.astype(BF16), cells, lambda i: 1).astype(F32)
-    total = total.reshape((2,) * len(left) + tail)
+    return near, middle, farthest, [near[0], *middle, farthest]
+
+
+def reduce_all(keep, send, cells, bricks, across):
+    place = lax.axis_index("cell")
+    left = halvings(cells)[:-1]
+    near, middle, farthest, crossed = reduce_groups(cells)
+    total = keep + swap(send, cells, lambda i: 1).astype(F32)
+    total = total.reshape((2,) * len(left) + keep.shape[1:])
 
     def portion(array, flipped):
         for offset, flip in reversed(flipped):
@@ -516,31 +537,32 @@
 
     steps = [prepare, *[lambda *done: done] * (len(halvings(cells)) - 4)]
     steps += [visit_partner, finish_partner] if paired else [gather_ghosts]
-    weights, (worked, gain) = gather_cells(shard, cells, steps)
+    held, arrived, (worked, gain) = gather_cells(shard, cells, steps)
     operands = []
     for (embedded, normed, normed_t, _), ghosts, wanted, half, rest in worked:
         operands += [normed, normed_t, ghosts, embedded, *half, *rest, wanted]
 
     columns = heads * atoms
-    energies, grads = pl.pallas_call(
-        functools.partial(sweep_kernel, count),
-        out_shape=(struct((1, atoms), F32), struct((4, width, width), F32)),
-        in_specs=vmem(2 + len(operands)),
-        out_specs=tuple(vmem(2)),
+    blocks = (cells // 2,) + master.shape
+    energies, keep, send = pl.pallas_call(
+        functools.partial(sweep_kernel, count, cells),
+        out_shape=(struct((1, atoms), F32), pinned(blocks, F32), pinned(blocks, BF16)),
+        in_specs=vmem(3 + len(operands)),
+        out_specs=tuple(vmem(3)),
         scratch_shapes=[
             pltpu.VMEM((table_rows, columns), F32),
             pltpu.VMEM((table_rows, columns), F32),
             pltpu.VMEM((table_rows, columns), BF16),
             pltpu.VMEM((table_rows, columns), BF16),
         ]
-        * count,
+        * count
+        + [pltpu.VMEM((master.shape[0], width, width), BF16)],
         compiler_params=pltpu.CompilerParams(vmem_limit_bytes=32 * 1024 * 1024),
         name="sweep",
-    )(weights, gain, *operands)
-
-    parts = grads.reshape(4, cells, width // cells, width).transpose(1, 0, 2, 3)
+    )(held, arrived, gain, *operands)
+
     across = [] if paired else list(reversed(halvings(bricks)))
-    owned = reduce_all(parts, cells, bricks, across)
+    owned = reduce_all(keep, send, cells, bricks, across)
     moment_new = 0.9 * moment + 0.1 * owned
     second_new = 0.999 * second + 0.001 * owned * owned
     adam_step = moment_new / (jnp.sqrt(second_new) + 1e-08)

time: 37 us -> 35.9 us (0.970)
  Pallas kernels: 9.64 us -> 9.09 us
  other arithmetic: 1.27 us -> 0.9 us
    pallas_call x1, Pallas kernels: 4.01 us -> 3.46 us  [body(): pl.pallas_call(functools.partial(sweep_kernel, count, cells), out_shape=(...]
where the time goes in v7:
time: 35.9 us; the launch traced here: 35.7 us
  starting transfers between devices  14.6 us (41%)
  waiting for transfers between devices  10.3 us (29%)
  Pallas kernels  9.09 us (25%)
  other arithmetic  0.9 us (3%)
  between operations  0.79 us (2%)
    ppermute x9, starting transfers between devices, swap(): lax.ppermute(array, 'cell', [(i, i ^ vector_of(i)) for i in range(cells)])  10.2 us
    ppermute x9, waiting for transfers between devices, swap(): lax.ppermute(array, 'cell', [(i, i ^ vector_of(i)) for i in range(cells)])  7.9 us
    pallas_call x4, Pallas kernels, index(): pl.pallas_call(functools.partial(index_kernel, first), out_shape=(pinned(...  3.95 us
    pallas_call x1, Pallas kernels, body(): pl.pallas_call(functools.partial(sweep_kernel, count, cells), out_shape=(...  3.46 us
    ppermute x1, starting transfers between devices, meet(): return lax.ppermute(array, ('cell', 'brick'), pairs).astype(F32)  2.91 us
    ppermute x1, waiting for transfers between devices, meet(): return lax.ppermute(array, ('cell', 'brick'), pairs).astype(F32)  2.4 us
    ppermute x1, starting transfers between devices, over_bricks(): lax.ppermute(array, 'brick', [(i, i ^ offset) for i in range(bricks)])  1.49 us
    pallas_call x1, Pallas kernels, embed_own(): pl.pallas_call(functools.partial(embed_kernel, int(paired)), out_shape=sh...  1.34 us
  transfers between devices with their start and end apart: 11, of which 8 were waited for; matrix products, arithmetic and copies ran while one was open for 0% of the time, Pallas kernels for 12%

profile of v7, /device:TPU:0, one launch (start us, length us, event | category | flops | bytes accessed | tf_op | source)
XLA Modules:
  0.0 35.7 jit_solution(13260771046248922752)
XLA Ops:
  0.6 1.3 %embed.1 = (bf16[4,16,256]{2,1,0:T(8,128)(2,1)S(1)}, f32[128,256]{1,0:T(8,128)S(1)}, bf16[128,256]{1,0:T(8,128)(2,1)S(1)}, bf16[256,128]{1,0:T(8,128)(2,1)S(1)},...) custom-call(f32[4,16,256]{2,1,0:T(8,128)} %master.1, ...), custom_call_target="tpu_custom_call" | custom-call | tf_op jit(solution)/shard_map/embed/pallas_call | solution.py:463
  2.0 3.5 %collective-permute-start = (bf16[4,16,256]{2,1,0:T(8,128)(2,1)S(1)}, bf16[4,16,256]{2,1,0:T(8,128)(2,1)S(1)}, u32[]{:S(2)}, u32[]{:S(2)}) collective-permute-start(bf16[4,16,256]{2,1,0:T(8,128)(2,1)S(1)} %get-tuple-element.94), channel_id=1, source_target_pairs={{0,18},{2,16},{4,22},{6,20},{8,26},{10,24},{12,30},{14,28},{16,2},... | collective-permute-start | bytes 98312 | tf_op jit(solution)/shard_map/ppermute | solution.py:307
  5.5 1.5 %collective-permute-start.1 = (bf16[528,128]{1,0:T(8,128)(2,1)S(1)}, bf16[528,128]{1,0:T(8,128)(2,1)S(1)}, u32[]{:S(2)}, u32[]{:S(2)}) collective-permute-start(bf16[528,128]{1,0:T(8,128)(2,1)S(1)} %get-tuple-element.121), channel_id=1, source_target_pairs={{0,1},{1,0},{2,3},{3,2},{4,5},{5,4},{6,7},{7,6},{8,9},{9,8},{10,11... | collective-permute-start | bytes 405512 | tf_op jit(solution)/shard_map/ppermute | solution.py:495
  7.0 1.0 %index.4 = (f32[8,96,128]{2,1,0:T(8,128)S(1)}, f32[96,128]{1,0:T(8,128)S(1)}) custom-call(s32[64,128]{1,0:T(8,128)S(1)} %get-tuple-element.115.neighbours, s32[1,128]{1,0:T(1,128)S(1)} %get-tuple-element.116.counts, f32[64,128]{1,0:T(8,128)S(1)} %get-tuple-element.117.distances, f32[1,8]{1,0:T(1,128)S(1)} %get-tuple-element.157.decay), custom_call_target="tpu_custom_call" | custom-call | tf_op jit(solution)/shard_map/index/pallas_call | solution.py:484
  8.0 0.0 collective-permute-done
  8.0 2.6 %collective-permute-start.2 = (bf16[2,4,16,256]{3,2,1,0:T(8,128)(2,1)S(1)}, bf16[2,4,16,256]{3,2,1,0:T(8,128)(2,1)S(1)}, u32[]{:S(2)}, u32[]{:S(2)}) collective-permute-start(bf16[2,4,16,256]{3,2,1,0:T(8,128)(2,1)S(1)} %maximum_select_fusion.4), channel_id=1, source_target_pairs={{0,14},{2,12},{4,10},{6,8},{8,6},{10,4},{12,2},{14,0},{16,30},{18,... | collective-permute-start | bytes 196616 | tf_op jit(solution)/shard_map/ppermute | solution.py:307
  10.7 0.4 %collective-permute-start.3 = (bf16[2,4,16,256]{3,2,1,0:T(8,128)(2,1)S(1)}, bf16[2,4,16,256]{3,2,1,0:T(8,128)(2,1)S(1)}, u32[]{:S(2)}, u32[]{:S(2)}) collective-permute-start(bf16[2,4,16,256]{3,2,1,0:T(8,128)(2,1)S(1)} %maximum_select_fusion.4), channel_id=1, source_target_pairs={{0,8},{2,10},{4,12},{6,14},{8,0},{10,2},{12,4},{14,6},{16,24},{18,... | collective-permute-start | bytes 196616 | tf_op jit(solution)/shard_map/ppermute | solution.py:307
  11.1 0.0 collective-permute-start.4
  11.1 1.0 %index.5 = (f32[8,96,128]{2,1,0:T(8,128)S(1)}, f32[96,128]{1,0:T(8,128)S(1)}) custom-call(s32[64,128]{1,0:T(8,128)S(1)} %get-tuple-element.115.neighbours, s32[1,128]{1,0:T(1,128)S(1)} %get-tuple-element.116.counts, f32[64,128]{1,0:T(8,128)S(1)} %get-tuple-element.117.distances, f32[1,8]{1,0:T(1,128)S(1)} %get-tuple-element.157.decay), custom_call_target="tpu_custom_call" | custom-call | tf_op jit(solution)/shard_map/index/pallas_call | solution.py:484
  12.1 0.0 collective-permute-done.1.packed
  12.1 0.3 unpack.1
  12.5 1.0 %index.6 = (f32[8,96,128]{2,1,0:T(8,128)S(1)}, f32[96,128]{1,0:T(8,128)S(1)}) custom-call(s32[64,128]{1,0:T(8,128)S(1)} %get-tuple-element.154.neighbours, s32[1,128]{1,0:T(1,128)S(1)} %get-tuple-element.155.counts, f32[64,128]{1,0:T(8,128)S(1)} %get-tuple-element.156.distances, f32[1,8]{1,0:T(1,128)S(1)} %get-tuple-element.157.decay), custom_call_target="tpu_custom_call" | custom-call | tf_op jit(solution)/shard_map/index/pallas_call | solution.py:484
  13.5 0.0 collective-permute-done.2
  13.5 1.4 %collective-permute-done.3 = bf16[2,4,16,256]{3,2,1,0:T(8,128)(2,1)S(1)} collective-permute-done((bf16[2,4,16,256]{3,2,1,0:T(8,128)(2,1)S(1)}, bf16[2,4,16,256]{3,2,1,0:T(8,128)(2,1)S(1)}, u32[]{:S(2)}, u32[]{:S(2)}) %collective-permute-start.3) | collective-permute-done | bytes 65568 | tf_op jit(solution)/shard_map/ppermute | solution.py:307
  14.9 0.6 %collective-permute-done.4 = bf16[2,4,16,256]{3,2,1,0:T(8,128)(2,1)S(1)} collective-permute-done((bf16[2,4,16,256]{3,2,1,0:T(8,128)(2,1)S(1)}, bf16[2,4,16,256]{3,2,1,0:T(8,128)(2,1)S(1)}, u32[]{:S(2)}, u32[]{:S(2)}) %collective-permute-start.4) | collective-permute-done | bytes 65568 | tf_op jit(solution)/shard_map/ppermute | solution.py:307
  15.6 0.2 collective-permute-start.5
  15.7 1.0 %index.7 = (f32[8,96,128]{2,1,0:T(8,128)S(1)}, f32[96,128]{1,0:T(8,128)S(1)}) custom-call(s32[64,128]{1,0:T(8,128)S(1)} %get-tuple-element.154.neighbours, s32[1,128]{1,0:T(1,128)S(1)} %get-tuple-element.155.counts, f32[64,128]{1,0:T(8,128)S(1)} %get-tuple-element.156.distances, f32[1,8]{1,0:T(1,128)S(1)} %get-tuple-element.157.decay), custom_call_target="tpu_custom_call" | custom-call | tf_op jit(solution)/shard_map/index/pallas_call | solution.py:484
  16.7 0.4 %collective-permute-done.5.arrived = bf16[2,2,2,4,16,256]{5,4,3,2,1,0:T(8,128)(2,1)S(1)} collective-permute-done((bf16[2,2,2,4,16,256]{5,4,3,2,1,0:T(8,128)(2,1)S(1)}, bf16[2,2,2,4,16,256]{5,4,3,2,1,0:T(8,128)(2,1)S(1)}, u32[]{:S(2)}, u32[]{:S(2)}) %collective-permute-start.5) | collective-permute-done | bytes 262176 | tf_op jit(solution)/shard_map/ppermute | solution.py:307
  17.2 3.5 %sweep.1 = (f32[1,128]{1,0:T(1,128)}, f32[8,4,16,256]{3,2,1,0:T(8,128)S(1)}, bf16[8,4,16,256]{3,2,1,0:T(8,128)(2,1)S(1)}) custom-call(bf16[2,2,2,4,16,256]{5,4,3,2,1,0:T(8,128)(2,1)S(1)} %maximum_select_fusion.held, bf16[2,2,2,4,16,256]{5,4,3,2,1,0:T(8,128)(2,1)S(1)} %collective-permute-done.5.arrived, f32[1,256]{1,0:T(1,128)S(1)} %get-tuple-element.162.readout, ...), custom_call_target="tpu_custom_call" | custom-call | tf_op jit(solution)/shard_map/sweep/pallas_call | solution.py:547
  20.6 0.4 %collective-permute-start.6 = (bf16[8,4,16,256]{3,2,1,0:T(8,128)(2,1)S(1)}, bf16[8,4,16,256]{3,2,1,0:T(8,128)(2,1)S(1)}, u32[]{:S(2)}, u32[]{:S(2)}) collective-permute-start(bf16[8,4,16,256]{3,2,1,0:T(8,128)(2,1)S(1)} %get-tuple-element.183), channel_id=1, source_target_pairs={{0,2},{2,0},{4,6},{6,4},{8,10},{10,8},{12,14},{14,12},{16,18},{18,... | collective-permute-start | bytes 786440 | tf_op jit(solution)/shard_map/ppermute | solution.py:307
  21.0 1.2 %collective-permute-done.6 = bf16[8,4,16,256]{3,2,1,0:T(8,128)(2,1)S(1)} collective-permute-done((bf16[8,4,16,256]{3,2,1,0:T(8,128)(2,1)S(1)}, bf16[8,4,16,256]{3,2,1,0:T(8,128)(2,1)S(1)}, u32[]{:S(2)}, u32[]{:S(2)}) %collective-permute-start.6) | collective-permute-done | bytes 262176 | tf_op jit(solution)/shard_map/ppermute | solution.py:307
  22.2 0.1 convert_add_fusion
  22.3 1.4 %collective-permute-start.7 = (bf16[2,4,16,256]{3,2,1,0:T(8,128)(2,1)S(1)}, bf16[2,4,16,256]{3,2,1,0:T(8,128)(2,1)S(1)}, u32[]{:S(2)}, u32[]{:S(2)}) collective-permute-start(bf16[2,4,16,256]{3,2,1,0:T(8,128)(2,1)S(1)} %get-tuple-element.187), channel_id=1, source_target_pairs={{0,10},{2,8},{4,14},{6,12},{8,2},{10,0},{12,6},{14,4},{16,26},{18,... | collective-permute-start | bytes 196616 | tf_op jit(solution)/shard_map/ppermute | solution.py:307
  23.7 0.9 %collective-permute-start.8 = (bf16[2,4,16,256]{3,2,1,0:T(8,128)(2,1)S(1)}, bf16[2,4,16,256]{3,2,1,0:T(8,128)(2,1)S(1)}, u32[]{:S(2)}, u32[]{:S(2)}) collective-permute-start(bf16[2,4,16,256]{3,2,1,0:T(8,128)(2,1)S(1)} %get-tuple-element.188), channel_id=1, source_target_pairs={{0,4},{2,6},{4,0},{6,2},{8,12},{10,14},{12,8},{14,10},{16,20},{18,... | collective-permute-start | bytes 196616 | tf_op jit(solution)/shard_map/ppermute | solution.py:307
  24.6 0.7 %collective-permute-start.9 = (bf16[2,4,16,256]{3,2,1,0:T(8,128)(2,1)S(1)}, bf16[2,4,16,256]{3,2,1,0:T(8,128)(2,1)S(1)}, u32[]{:S(2)}, u32[]{:S(2)}) collective-permute-start(bf16[2,4,16,256]{3,2,1,0:T(8,128)(2,1)S(1)} %get-tuple-element.189), channel_id=1, source_target_pairs={{0,14},{2,12},{4,10},{6,8},{8,6},{10,4},{12,2},{14,0},{16,30},{18,... | collective-permute-start | bytes 196616 | tf_op jit(solution)/shard_map/ppermute | solution.py:307
  25.3 1.0 %collective-permute-done.7 = bf16[2,4,16,256]{3,2,1,0:T(8,128)(2,1)S(1)} collective-permute-done((bf16[2,4,16,256]{3,2,1,0:T(8,128)(2,1)S(1)}, bf16[2,4,16,256]{3,2,1,0:T(8,128)(2,1)S(1)}, u32[]{:S(2)}, u32[]{:S(2)}) %collective-permute-start.7) | collective-permute-done | bytes 65568 | tf_op jit(solution)/shard_map/ppermute | solution.py:307
  26.3 1.8 %collective-permute-done.8 = bf16[2,4,16,256]{3,2,1,0:T(8,128)(2,1)S(1)} collective-permute-done((bf16[2,4,16,256]{3,2,1,0:T(8,128)(2,1)S(1)}, bf16[2,4,16,256]{3,2,1,0:T(8,128)(2,1)S(1)}, u32[]{:S(2)}, u32[]{:S(2)}) %collective-permute-start.8) | collective-permute-done | bytes 65568 | tf_op jit(solution)/shard_map/ppermute | solution.py:307
  28.0 1.6 %collective-permute-done.9 = bf16[2,4,16,256]{3,2,1,0:T(8,128)(2,1)S(1)} collective-permute-done((bf16[2,4,16,256]{3,2,1,0:T(8,128)(2,1)S(1)}, bf16[2,4,16,256]{3,2,1,0:T(8,128)(2,1)S(1)}, u32[]{:S(2)}, u32[]{:S(2)}) %collective-permute-start.9) | collective-permute-done | bytes 65568 | tf_op jit(solution)/shard_map/ppermute | solution.py:307
  29.6 0.0 copy-start.1
  29.7 0.0 copy-start
  29.7 2.9 %collective-permute-start.10 = (bf16[4,16,256]{2,1,0:T(8,128)(2,1)S(1)}, bf16[4,16,256]{2,1,0:T(8,128)(2,1)S(1)}, u32[]{:S(2)}, u32[]{:S(2)}) collective-permute-start(bf16[4,16,256]{2,1,0:T(8,128)(2,1)S(1)} %fusion.7), channel_id=1, source_target_pairs={{0,18},{1,19},{2,16},{3,17},{4,22},{5,23},{6,20},{7,21},{8,26},{9,... | collective-permute-start | bytes 98312 | tf_op jit(solution)/shard_map/ppermute | solution.py:400
  32.6 2.4 %collective-permute-done.10 = bf16[4,16,256]{2,1,0:T(8,128)(2,1)S(1)} collective-permute-done((bf16[4,16,256]{2,1,0:T(8,128)(2,1)S(1)}, bf16[4,16,256]{2,1,0:T(8,128)(2,1)S(1)}, u32[]{:S(2)}, u32[]{:S(2)}) %collective-permute-start.10) | collective-permute-done | bytes 32800 | tf_op jit(solution)/shard_map/ppermute | solution.py:400
  35.0 0.0 copy-done.1
  35.0 0.0 copy-done
  35.0 0.7 %add_divide_fusion = (f32[4,16,256]{2,1,0:T(8,128)}, f32[4,16,256]{2,1,0:T(8,128)}, f32[4,16,256]{2,1,0:T(8,128)}) fusion(bf16[4,16,256]{2,1,0:T(8,128)(2,1)S(1)} %collective-permute-done.10, f32[2,4,16,256]{3,2,1,0:T(8,128)S(1)} %fusion.1, s32[]{:T(128)S(6)} %select_n.212, f32[4,16,256]{2,1,0:T(8,128)S(1)} %copy-done, f32[4,16,256]{2,1,0:T(8,128)S(1)} %copy-done.1), kind=kLoop, calls=%fused_computation.19 | loop fusion | flops 180224 | bytes 425988 | tf_op jit(solution)/shard_map/div | solution.py:568
  (10 shorter events, 0.2 us)
Async XLA Ops:
  2.0 6.0 %collective-permute-start = (bf16[4,16,256]{2,1,0:T(8,128)(2,1)S(1)}, bf16[4,16,256]{2,1,0:T(8,128)(2,1)S(1)}, u32[]{:S(2)}, u32[]{:S(2)}) collective-permute-start(bf16[4,16,256]{2,1,0:T(8,128)(2,1)S(1)} %get-tuple-element.94), channel_id=1, source_target_pairs={{0,18},{2,16},{4,22},{6,20},{8,26},{10,24},{12,30},{14,28},{16,2},... | collective-permute-start | bytes 98312 | tf_op jit(solution)/shard_map/ppermute | solution.py:307
  5.5 6.6 %collective-permute-start.1 = (bf16[528,128]{1,0:T(8,128)(2,1)S(1)}, bf16[528,128]{1,0:T(8,128)(2,1)S(1)}, u32[]{:S(2)}, u32[]{:S(2)}) collective-permute-start(bf16[528,128]{1,0:T(8,128)(2,1)S(1)} %get-tuple-element.121), channel_id=1, source_target_pairs={{0,1},{1,0},{2,3},{3,2},{4,5},{5,4},{6,7},{7,6},{8,9},{9,8},{10,11... | collective-permute-start | bytes 405512 | tf_op jit(solution)/shard_map/ppermute | solution.py:495
  8.0 5.5 %collective-permute-start.2 = (bf16[2,4,16,256]{3,2,1,0:T(8,128)(2,1)S(1)}, bf16[2,4,16,256]{3,2,1,0:T(8,128)(2,1)S(1)}, u32[]{:S(2)}, u32[]{:S(2)}) collective-permute-start(bf16[2,4,16,256]{3,2,1,0:T(8,128)(2,1)S(1)} %maximum_select_fusion.4), channel_id=1, source_target_pairs={{0,14},{2,12},{4,10},{6,8},{8,6},{10,4},{12,2},{14,0},{16,30},{18,... | collective-permute-start | bytes 196616 | tf_op jit(solution)/shard_map/ppermute | solution.py:307
  10.7 4.3 %collective-permute-start.3 = (bf16[2,4,16,256]{3,2,1,0:T(8,128)(2,1)S(1)}, bf16[2,4,16,256]{3,2,1,0:T(8,128)(2,1)S(1)}, u32[]{:S(2)}, u32[]{:S(2)}) collective-permute-start(bf16[2,4,16,256]{3,2,1,0:T(8,128)(2,1)S(1)} %maximum_select_fusion.4), channel_id=1, source_target_pairs={{0,8},{2,10},{4,12},{6,14},{8,0},{10,2},{12,4},{14,6},{16,24},{18,... | collective-permute-start | bytes 196616 | tf_op jit(solution)/shard_map/ppermute | solution.py:307
  11.1 4.4 %collective-permute-start.4 = (bf16[2,4,16,256]{3,2,1,0:T(8,128)(2,1)S(1)}, bf16[2,4,16,256]{3,2,1,0:T(8,128)(2,1)S(1)}, u32[]{:S(2)}, u32[]{:S(2)}) collective-permute-start(bf16[2,4,16,256]{3,2,1,0:T(8,128)(2,1)S(1)} %maximum_select_fusion.4), channel_id=1, source_target_pairs={{0,6},{2,4},{4,2},{6,0},{8,14},{10,12},{12,10},{14,8},{16,22},{18,... | collective-permute-start | bytes 196616 | tf_op jit(solution)/shard_map/ppermute | solution.py:307
  15.6 1.6 %collective-permute-start.5 = (bf16[2,2,2,4,16,256]{5,4,3,2,1,0:T(8,128)(2,1)S(1)}, bf16[2,2,2,4,16,256]{5,4,3,2,1,0:T(8,128)(2,1)S(1)}, u32[]{:S(2)}, u32[]{:S(2)}) collective-permute-start(bf16[2,2,2,4,16,256]{5,4,3,2,1,0:T(8,128)(2,1)S(1)} %maximum_select_fusion.held), channel_id=1, source_target_pairs={{0,2},{2,0},{4,6},{6,4},{8,10},{10,8},{12,14},{14,12},{16,18},{18,... | collective-permute-start | bytes 786440 | tf_op jit(solution)/shard_map/ppermute | solution.py:307
  20.6 1.5 %collective-permute-start.6 = (bf16[8,4,16,256]{3,2,1,0:T(8,128)(2,1)S(1)}, bf16[8,4,16,256]{3,2,1,0:T(8,128)(2,1)S(1)}, u32[]{:S(2)}, u32[]{:S(2)}) collective-permute-start(bf16[8,4,16,256]{3,2,1,0:T(8,128)(2,1)S(1)} %get-tuple-element.183), channel_id=1, source_target_pairs={{0,2},{2,0},{4,6},{6,4},{8,10},{10,8},{12,14},{14,12},{16,18},{18,... | collective-permute-start | bytes 786440 | tf_op jit(solution)/shard_map/ppermute | solution.py:307
  22.3 4.0 %collective-permute-start.7 = (bf16[2,4,16,256]{3,2,1,0:T(8,128)(2,1)S(1)}, bf16[2,4,16,256]{3,2,1,0:T(8,128)(2,1)S(1)}, u32[]{:S(2)}, u32[]{:S(2)}) collective-permute-start(bf16[2,4,16,256]{3,2,1,0:T(8,128)(2,1)S(1)} %get-tuple-element.187), channel_id=1, source_target_pairs={{0,10},{2,8},{4,14},{6,12},{8,2},{10,0},{12,6},{14,4},{16,26},{18,... | collective-permute-start | bytes 196616 | tf_op jit(solution)/shard_map/ppermute | solution.py:307
  23.7 4.4 %collective-permute-start.8 = (bf16[2,4,16,256]{3,2,1,0:T(8,128)(2,1)S(1)}, bf16[2,4,16,256]{3,2,1,0:T(8,128)(2,1)S(1)}, u32[]{:S(2)}, u32[]{:S(2)}) collective-permute-start(bf16[2,4,16,256]{3,2,1,0:T(8,128)(2,1)S(1)} %get-tuple-element.188), channel_id=1, source_target_pairs={{0,4},{2,6},{4,0},{6,2},{8,12},{10,14},{12,8},{14,10},{16,20},{18,... | collective-permute-start | bytes 196616 | tf_op jit(solution)/shard_map/ppermute | solution.py:307
  24.6 5.0 %collective-permute-start.9 = (bf16[2,4,16,256]{3,2,1,0:T(8,128)(2,1)S(1)}, bf16[2,4,16,256]{3,2,1,0:T(8,128)(2,1)S(1)}, u32[]{:S(2)}, u32[]{:S(2)}) collective-permute-start(bf16[2,4,16,256]{3,2,1,0:T(8,128)(2,1)S(1)} %get-tuple-element.189), channel_id=1, source_target_pairs={{0,14},{2,12},{4,10},{6,8},{8,6},{10,4},{12,2},{14,0},{16,30},{18,... | collective-permute-start | bytes 196616 | tf_op jit(solution)/shard_map/ppermute | solution.py:307
  29.6 5.4 %copy-start.1 = (f32[4,16,256]{2,1,0:T(8,128)S(1)}, f32[4,16,256]{2,1,0:T(8,128)}, u32[]{:S(2)}) copy-start(f32[4,16,256]{2,1,0:T(8,128)} %param.26) | copy-start | bytes 196612
  29.7 5.3 %copy-start = (f32[4,16,256]{2,1,0:T(8,128)S(1)}, f32[4,16,256]{2,1,0:T(8,128)}, u32[]{:S(2)}) copy-start(f32[4,16,256]{2,1,0:T(8,128)} %param.27) | copy-start | bytes 196612
  29.7 5.3 %collective-permute-start.10 = (bf16[4,16,256]{2,1,0:T(8,128)(2,1)S(1)}, bf16[4,16,256]{2,1,0:T(8,128)(2,1)S(1)}, u32[]{:S(2)}, u32[]{:S(2)}) collective-permute-start(bf16[4,16,256]{2,1,0:T(8,128)(2,1)S(1)} %fusion.7), channel_id=1, source_target_pairs={{0,18},{1,19},{2,16},{3,17},{4,22},{5,23},{6,20},{7,21},{8,26},{9,... | collective-permute-start | bytes 98312 | tf_op jit(solution)/shard_map/ppermute | solution.py:400

commit v8 on v7

--- a/solution.py
+++ b/solution.py
@@ -377,7 +377,7 @@
     def exchange(group):
         nonlocal total, left
         mine = portion(total, [(offset, 0) for offset in group])
-        for step in range(1, 1 << len(group)):
+        for step in (2, 3, 1) if len(group) == 2 else (1,):
             flipped = [(offset, step >> k & 1) for k, offset in enumerate(group)]
             vector = 0
             for offset, flip in flipped:

time: 35.9 us -> 34.3 us (0.955)
  waiting for transfers between devices: 10.3 us -> 9.07 us
  starting transfers between devices: 14.6 us -> 14.2 us
    ppermute x1, waiting for transfers between devices: 2.4 us -> 1.76 us  [meet(): return lax.ppermute(array, ('cell', 'brick'), pairs).astype(F32)]
    ppermute x9, waiting for transfers between devices: 7.9 us -> 7.31 us  [swap(): lax.ppermute(array, 'cell', [(i, i ^ vector_of(i)) for i in range(cells)])]
  transfers between devices with their start and end apart: 11 -> 11, of which waited for: 8 -> 8; matrix products, arithmetic and copies ran while one was open for 0% -> 0% of each run, Pallas kernels for 12% -> 13%
where the time goes in v8:
time: 34.3 us; the launch traced here: 34.2 us
  starting transfers between devices  14.2 us (41%)
  Pallas kernels  9.09 us (27%)
  waiting for transfers between devices  9.07 us (26%)
  other arithmetic  0.9 us (3%)
  between operations  0.79 us (2%)
    ppermute x9, starting transfers between devices, swap(): lax.ppermute(array, 'cell', [(i, i ^ vector_of(i)) for i in range(cells)])  10.2 us
    ppermute x9, waiting for transfers between devices, swap(): lax.ppermute(array, 'cell', [(i, i ^ vector_of(i)) for i in range(cells)])  7.31 us
    pallas_call x4, Pallas kernels, index(): pl.pallas_call(functools.partial(index_kernel, first), out_shape=(pinned(...  3.95 us
    pallas_call x1, Pallas kernels, body(): pl.pallas_call(functools.partial(sweep_kernel, count, cells), out_shape=(...  3.46 us
    ppermute x1, starting transfers between devices, meet(): return lax.ppermute(array, ('cell', 'brick'), pairs).astype(F32)  2.56 us
    ppermute x1, waiting for transfers between devices, meet(): return lax.ppermute(array, ('cell', 'brick'), pairs).astype(F32)  1.76 us
    ppermute x1, starting transfers between devices, over_bricks(): lax.ppermute(array, 'brick', [(i, i ^ offset) for i in range(bricks)])  1.49 us
    pallas_call x1, Pallas kernels, embed_own(): pl.pallas_call(functools.partial(embed_kernel, int(paired)), out_shape=sh...  1.34 us
  transfers between devices with their start and end apart: 11, of which 8 were waited for; matrix products, arithmetic and copies ran while one was open for 0% of the time, Pallas kernels for 13%

profile of v8, /device:TPU:0, one launch (start us, length us, event | category | flops | bytes accessed | tf_op | source)
XLA Modules:
  0.0 34.2 jit_solution(7233799430598210533)
XLA Ops:
  0.6 1.3 %embed.1 = (bf16[4,16,256]{2,1,0:T(8,128)(2,1)S(1)}, f32[128,256]{1,0:T(8,128)S(1)}, bf16[128,256]{1,0:T(8,128)(2,1)S(1)}, bf16[256,128]{1,0:T(8,128)(2,1)S(1)},...) custom-call(f32[4,16,256]{2,1,0:T(8,128)} %master.1, ...), custom_call_target="tpu_custom_call" | custom-call | tf_op jit(solution)/shard_map/embed/pallas_call | solution.py:463
  2.0 3.5 %collective-permute-start = (bf16[4,16,256]{2,1,0:T(8,128)(2,1)S(1)}, bf16[4,16,256]{2,1,0:T(8,128)(2,1)S(1)}, u32[]{:S(2)}, u32[]{:S(2)}) collective-permute-start(bf16[4,16,256]{2,1,0:T(8,128)(2,1)S(1)} %get-tuple-element.94), channel_id=1, source_target_pairs={{0,18},{2,16},{4,22},{6,20},{8,26},{10,24},{12,30},{14,28},{16,2},... | collective-permute-start | bytes 98312 | tf_op jit(solution)/shard_map/ppermute | solution.py:307
  5.5 1.5 %collective-permute-start.1 = (bf16[528,128]{1,0:T(8,128)(2,1)S(1)}, bf16[528,128]{1,0:T(8,128)(2,1)S(1)}, u32[]{:S(2)}, u32[]{:S(2)}) collective-permute-start(bf16[528,128]{1,0:T(8,128)(2,1)S(1)} %get-tuple-element.121), channel_id=1, source_target_pairs={{0,1},{1,0},{2,3},{3,2},{4,5},{5,4},{6,7},{7,6},{8,9},{9,8},{10,11... | collective-permute-start | bytes 405512 | tf_op jit(solution)/shard_map/ppermute | solution.py:495
  7.0 1.0 %index.4 = (f32[8,96,128]{2,1,0:T(8,128)S(1)}, f32[96,128]{1,0:T(8,128)S(1)}) custom-call(s32[64,128]{1,0:T(8,128)S(1)} %get-tuple-element.115.neighbours, s32[1,128]{1,0:T(1,128)S(1)} %get-tuple-element.116.counts, f32[64,128]{1,0:T(8,128)S(1)} %get-tuple-element.117.distances, f32[1,8]{1,0:T(1,128)S(1)} %get-tuple-element.157.decay), custom_call_target="tpu_custom_call" | custom-call | tf_op jit(solution)/shard_map/index/pallas_call | solution.py:484
  8.0 0.0 collective-permute-done
  8.0 2.6 %collective-permute-start.2 = (bf16[2,4,16,256]{3,2,1,0:T(8,128)(2,1)S(1)}, bf16[2,4,16,256]{3,2,1,0:T(8,128)(2,1)S(1)}, u32[]{:S(2)}, u32[]{:S(2)}) collective-permute-start(bf16[2,4,16,256]{3,2,1,0:T(8,128)(2,1)S(1)} %maximum_select_fusion.4), channel_id=1, source_target_pairs={{0,14},{2,12},{4,10},{6,8},{8,6},{10,4},{12,2},{14,0},{16,30},{18,... | collective-permute-start | bytes 196616 | tf_op jit(solution)/shard_map/ppermute | solution.py:307
  10.7 0.4 %collective-permute-start.3 = (bf16[2,4,16,256]{3,2,1,0:T(8,128)(2,1)S(1)}, bf16[2,4,16,256]{3,2,1,0:T(8,128)(2,1)S(1)}, u32[]{:S(2)}, u32[]{:S(2)}) collective-permute-start(bf16[2,4,16,256]{3,2,1,0:T(8,128)(2,1)S(1)} %maximum_select_fusion.4), channel_id=1, source_target_pairs={{0,8},{2,10},{4,12},{6,14},{8,0},{10,2},{12,4},{14,6},{16,24},{18,... | collective-permute-start | bytes 196616 | tf_op jit(solution)/shard_map/ppermute | solution.py:307
  11.1 0.0 collective-permute-start.4
  11.1 1.0 %index.5 = (f32[8,96,128]{2,1,0:T(8,128)S(1)}, f32[96,128]{1,0:T(8,128)S(1)}) custom-call(s32[64,128]{1,0:T(8,128)S(1)} %get-tuple-element.115.neighbours, s32[1,128]{1,0:T(1,128)S(1)} %get-tuple-element.116.counts, f32[64,128]{1,0:T(8,128)S(1)} %get-tuple-element.117.distances, f32[1,8]{1,0:T(1,128)S(1)} %get-tuple-element.157.decay), custom_call_target="tpu_custom_call" | custom-call | tf_op jit(solution)/shard_map/index/pallas_call | solution.py:484
  12.1 0.0 collective-permute-done.1.packed
  12.1 0.3 %unpack.1 = (f32[128,256]{1,0:T(8,128)S(1)}, bf16[128,256]{1,0:T(8,128)(2,1)S(1)}, bf16[256,128]{1,0:T(8,128)(2,1)S(1)}, bf16[2,32,256]{2,1,0:T(8,128)(2,1)S(1)}...) custom-call(bf16[528,128]{1,0:T(8,128)(2,1)S(1)} %collective-permute-done.1.packed, ...), custom_call_target="tpu_custom_call" | custom-call | tf_op jit(solution)/shard_map/unpack/pallas_call | solution.py:473
  12.5 1.0 %index.6 = (f32[8,96,128]{2,1,0:T(8,128)S(1)}, f32[96,128]{1,0:T(8,128)S(1)}) custom-call(s32[64,128]{1,0:T(8,128)S(1)} %get-tuple-element.154.neighbours, s32[1,128]{1,0:T(1,128)S(1)} %get-tuple-element.155.counts, f32[64,128]{1,0:T(8,128)S(1)} %get-tuple-element.156.distances, f32[1,8]{1,0:T(1,128)S(1)} %get-tuple-element.157.decay), custom_call_target="tpu_custom_call" | custom-call | tf_op jit(solution)/shard_map/index/pallas_call | solution.py:484
  13.5 0.0 collective-permute-done.2
  13.5 1.4 %collective-permute-done.3 = bf16[2,4,16,256]{3,2,1,0:T(8,128)(2,1)S(1)} collective-permute-done((bf16[2,4,16,256]{3,2,1,0:T(8,128)(2,1)S(1)}, bf16[2,4,16,256]{3,2,1,0:T(8,128)(2,1)S(1)}, u32[]{:S(2)}, u32[]{:S(2)}) %collective-permute-start.3) | collective-permute-done | bytes 65568 | tf_op jit(solution)/shard_map/ppermute | solution.py:307
  14.9 0.6 %collective-permute-done.4 = bf16[2,4,16,256]{3,2,1,0:T(8,128)(2,1)S(1)} collective-permute-done((bf16[2,4,16,256]{3,2,1,0:T(8,128)(2,1)S(1)}, bf16[2,4,16,256]{3,2,1,0:T(8,128)(2,1)S(1)}, u32[]{:S(2)}, u32[]{:S(2)}) %collective-permute-start.4) | collective-permute-done | bytes 65568 | tf_op jit(solution)/shard_map/ppermute | solution.py:307
  15.6 0.2 collective-permute-start.5
  15.7 1.0 %index.7 = (f32[8,96,128]{2,1,0:T(8,128)S(1)}, f32[96,128]{1,0:T(8,128)S(1)}) custom-call(s32[64,128]{1,0:T(8,128)S(1)} %get-tuple-element.154.neighbours, s32[1,128]{1,0:T(1,128)S(1)} %get-tuple-element.155.counts, f32[64,128]{1,0:T(8,128)S(1)} %get-tuple-element.156.distances, f32[1,8]{1,0:T(1,128)S(1)} %get-tuple-element.157.decay), custom_call_target="tpu_custom_call" | custom-call | tf_op jit(solution)/shard_map/index/pallas_call | solution.py:484
  16.7 0.4 %collective-permute-done.5.arrived = bf16[2,2,2,4,16,256]{5,4,3,2,1,0:T(8,128)(2,1)S(1)} collective-permute-done((bf16[2,2,2,4,16,256]{5,4,3,2,1,0:T(8,128)(2,1)S(1)}, bf16[2,2,2,4,16,256]{5,4,3,2,1,0:T(8,128)(2,1)S(1)}, u32[]{:S(2)}, u32[]{:S(2)}) %collective-permute-start.5) | collective-permute-done | bytes 262176 | tf_op jit(solution)/shard_map/ppermute | solution.py:307
  17.2 3.5 %sweep.1 = (f32[1,128]{1,0:T(1,128)}, f32[8,4,16,256]{3,2,1,0:T(8,128)S(1)}, bf16[8,4,16,256]{3,2,1,0:T(8,128)(2,1)S(1)}) custom-call(bf16[2,2,2,4,16,256]{5,4,3,2,1,0:T(8,128)(2,1)S(1)} %maximum_select_fusion.held, bf16[2,2,2,4,16,256]{5,4,3,2,1,0:T(8,128)(2,1)S(1)} %collective-permute-done.5.arrived, f32[1,256]{1,0:T(1,128)S(1)} %get-tuple-element.162.readout, ...), custom_call_target="tpu_custom_call" | custom-call | tf_op jit(solution)/shard_map/sweep/pallas_call | solution.py:547
  20.6 0.1 collective-permute-start.6
  20.8 1.4 %collective-permute-done.6 = bf16[8,4,16,256]{3,2,1,0:T(8,128)(2,1)S(1)} collective-permute-done((bf16[8,4,16,256]{3,2,1,0:T(8,128)(2,1)S(1)}, bf16[8,4,16,256]{3,2,1,0:T(8,128)(2,1)S(1)}, u32[]{:S(2)}, u32[]{:S(2)}) %collective-permute-start.6) | collective-permute-done | bytes 262176 | tf_op jit(solution)/shard_map/ppermute | solution.py:307
  22.2 0.1 convert_add_fusion
  22.3 0.9 %collective-permute-start.7 = (bf16[2,4,16,256]{3,2,1,0:T(8,128)(2,1)S(1)}, bf16[2,4,16,256]{3,2,1,0:T(8,128)(2,1)S(1)}, u32[]{:S(2)}, u32[]{:S(2)}) collective-permute-start(bf16[2,4,16,256]{3,2,1,0:T(8,128)(2,1)S(1)} %get-tuple-element.187), channel_id=1, source_target_pairs={{0,4},{2,6},{4,0},{6,2},{8,12},{10,14},{12,8},{14,10},{16,20},{18,... | collective-permute-start | bytes 196616 | tf_op jit(solution)/shard_map/ppermute | solution.py:307
  23.2 1.7 %collective-permute-start.8 = (bf16[2,4,16,256]{3,2,1,0:T(8,128)(2,1)S(1)}, bf16[2,4,16,256]{3,2,1,0:T(8,128)(2,1)S(1)}, u32[]{:S(2)}, u32[]{:S(2)}) collective-permute-start(bf16[2,4,16,256]{3,2,1,0:T(8,128)(2,1)S(1)} %get-tuple-element.188), channel_id=1, source_target_pairs={{0,14},{2,12},{4,10},{6,8},{8,6},{10,4},{12,2},{14,0},{16,30},{18,... | collective-permute-start | bytes 196616 | tf_op jit(solution)/shard_map/ppermute | solution.py:307
  24.9 0.7 %collective-permute-start.9 = (bf16[2,4,16,256]{3,2,1,0:T(8,128)(2,1)S(1)}, bf16[2,4,16,256]{3,2,1,0:T(8,128)(2,1)S(1)}, u32[]{:S(2)}, u32[]{:S(2)}) collective-permute-start(bf16[2,4,16,256]{3,2,1,0:T(8,128)(2,1)S(1)} %get-tuple-element.189), channel_id=1, source_target_pairs={{0,10},{2,8},{4,14},{6,12},{8,2},{10,0},{12,6},{14,4},{16,26},{18,... | collective-permute-start | bytes 196616 | tf_op jit(solution)/shard_map/ppermute | solution.py:307
  25.6 1.1 %collective-permute-done.7 = bf16[2,4,16,256]{3,2,1,0:T(8,128)(2,1)S(1)} collective-permute-done((bf16[2,4,16,256]{3,2,1,0:T(8,128)(2,1)S(1)}, bf16[2,4,16,256]{3,2,1,0:T(8,128)(2,1)S(1)}, u32[]{:S(2)}, u32[]{:S(2)}) %collective-permute-start.7) | collective-permute-done | bytes 65568 | tf_op jit(solution)/shard_map/ppermute | solution.py:307
  26.6 1.8 %collective-permute-done.8 = bf16[2,4,16,256]{3,2,1,0:T(8,128)(2,1)S(1)} collective-permute-done((bf16[2,4,16,256]{3,2,1,0:T(8,128)(2,1)S(1)}, bf16[2,4,16,256]{3,2,1,0:T(8,128)(2,1)S(1)}, u32[]{:S(2)}, u32[]{:S(2)}) %collective-permute-start.8) | collective-permute-done | bytes 65568 | tf_op jit(solution)/shard_map/ppermute | solution.py:307
  28.4 0.7 %collective-permute-done.9 = bf16[2,4,16,256]{3,2,1,0:T(8,128)(2,1)S(1)} collective-permute-done((bf16[2,4,16,256]{3,2,1,0:T(8,128)(2,1)S(1)}, bf16[2,4,16,256]{3,2,1,0:T(8,128)(2,1)S(1)}, u32[]{:S(2)}, u32[]{:S(2)}) %collective-permute-start.9) | collective-permute-done | bytes 65568 | tf_op jit(solution)/shard_map/ppermute | solution.py:307
  29.1 0.0 copy-start.1
  29.1 0.0 copy-start
  29.2 2.6 %collective-permute-start.10 = (bf16[4,16,256]{2,1,0:T(8,128)(2,1)S(1)}, bf16[4,16,256]{2,1,0:T(8,128)(2,1)S(1)}, u32[]{:S(2)}, u32[]{:S(2)}) collective-permute-start(bf16[4,16,256]{2,1,0:T(8,128)(2,1)S(1)} %fusion.7), channel_id=1, source_target_pairs={{0,18},{1,19},{2,16},{3,17},{4,22},{5,23},{6,20},{7,21},{8,26},{9,... | collective-permute-start | bytes 98312 | tf_op jit(solution)/shard_map/ppermute | solution.py:400
  31.7 1.8 %collective-permute-done.10 = bf16[4,16,256]{2,1,0:T(8,128)(2,1)S(1)} collective-permute-done((bf16[4,16,256]{2,1,0:T(8,128)(2,1)S(1)}, bf16[4,16,256]{2,1,0:T(8,128)(2,1)S(1)}, u32[]{:S(2)}, u32[]{:S(2)}) %collective-permute-start.10) | collective-permute-done | bytes 32800 | tf_op jit(solution)/shard_map/ppermute | solution.py:400
  33.5 0.0 copy-done.1
  33.5 0.0 copy-done
  33.5 0.7 %add_divide_fusion = (f32[4,16,256]{2,1,0:T(8,128)}, f32[4,16,256]{2,1,0:T(8,128)}, f32[4,16,256]{2,1,0:T(8,128)}) fusion(bf16[4,16,256]{2,1,0:T(8,128)(2,1)S(1)} %collective-permute-done.10, f32[2,4,16,256]{3,2,1,0:T(8,128)S(1)} %fusion.1, s32[]{:T(128)S(6)} %select_n.212, f32[4,16,256]{2,1,0:T(8,128)S(1)} %copy-done, f32[4,16,256]{2,1,0:T(8,128)S(1)} %copy-done.1), kind=kLoop, calls=%fused_computation.19 | loop fusion | flops 180224 | bytes 425988 | tf_op jit(solution)/shard_map/div | solution.py:568
  (10 shorter events, 0.2 us)
Async XLA Ops:
  2.0 6.0 %collective-permute-start = (bf16[4,16,256]{2,1,0:T(8,128)(2,1)S(1)}, bf16[4,16,256]{2,1,0:T(8,128)(2,1)S(1)}, u32[]{:S(2)}, u32[]{:S(2)}) collective-permute-start(bf16[4,16,256]{2,1,0:T(8,128)(2,1)S(1)} %get-tuple-element.94), channel_id=1, source_target_pairs={{0,18},{2,16},{4,22},{6,20},{8,26},{10,24},{12,30},{14,28},{16,2},... | collective-permute-start | bytes 98312 | tf_op jit(solution)/shard_map/ppermute | solution.py:307
  5.5 6.6 %collective-permute-start.1 = (bf16[528,128]{1,0:T(8,128)(2,1)S(1)}, bf16[528,128]{1,0:T(8,128)(2,1)S(1)}, u32[]{:S(2)}, u32[]{:S(2)}) collective-permute-start(bf16[528,128]{1,0:T(8,128)(2,1)S(1)} %get-tuple-element.121), channel_id=1, source_target_pairs={{0,1},{1,0},{2,3},{3,2},{4,5},{5,4},{6,7},{7,6},{8,9},{9,8},{10,11... | collective-permute-start | bytes 405512 | tf_op jit(solution)/shard_map/ppermute | solution.py:495
  8.0 5.5 %collective-permute-start.2 = (bf16[2,4,16,256]{3,2,1,0:T(8,128)(2,1)S(1)}, bf16[2,4,16,256]{3,2,1,0:T(8,128)(2,1)S(1)}, u32[]{:S(2)}, u32[]{:S(2)}) collective-permute-start(bf16[2,4,16,256]{3,2,1,0:T(8,128)(2,1)S(1)} %maximum_select_fusion.4), channel_id=1, source_target_pairs={{0,14},{2,12},{4,10},{6,8},{8,6},{10,4},{12,2},{14,0},{16,30},{18,... | collective-permute-start | bytes 196616 | tf_op jit(solution)/shard_map/ppermute | solution.py:307
  10.7 4.3 %collective-permute-start.3 = (bf16[2,4,16,256]{3,2,1,0:T(8,128)(2,1)S(1)}, bf16[2,4,16,256]{3,2,1,0:T(8,128)(2,1)S(1)}, u32[]{:S(2)}, u32[]{:S(2)}) collective-permute-start(bf16[2,4,16,256]{3,2,1,0:T(8,128)(2,1)S(1)} %maximum_select_fusion.4), channel_id=1, source_target_pairs={{0,8},{2,10},{4,12},{6,14},{8,0},{10,2},{12,4},{14,6},{16,24},{18,... | collective-permute-start | bytes 196616 | tf_op jit(solution)/shard_map/ppermute | solution.py:307
  11.1 4.4 %collective-permute-start.4 = (bf16[2,4,16,256]{3,2,1,0:T(8,128)(2,1)S(1)}, bf16[2,4,16,256]{3,2,1,0:T(8,128)(2,1)S(1)}, u32[]{:S(2)}, u32[]{:S(2)}) collective-permute-start(bf16[2,4,16,256]{3,2,1,0:T(8,128)(2,1)S(1)} %maximum_select_fusion.4), channel_id=1, source_target_pairs={{0,6},{2,4},{4,2},{6,0},{8,14},{10,12},{12,10},{14,8},{16,22},{18,... | collective-permute-start | bytes 196616 | tf_op jit(solution)/shard_map/ppermute | solution.py:307
  15.6 1.6 %collective-permute-start.5 = (bf16[2,2,2,4,16,256]{5,4,3,2,1,0:T(8,128)(2,1)S(1)}, bf16[2,2,2,4,16,256]{5,4,3,2,1,0:T(8,128)(2,1)S(1)}, u32[]{:S(2)}, u32[]{:S(2)}) collective-permute-start(bf16[2,2,2,4,16,256]{5,4,3,2,1,0:T(8,128)(2,1)S(1)} %maximum_select_fusion.held), channel_id=1, source_target_pairs={{0,2},{2,0},{4,6},{6,4},{8,10},{10,8},{12,14},{14,12},{16,18},{18,... | collective-permute-start | bytes 786440 | tf_op jit(solution)/shard_map/ppermute | solution.py:307
  20.6 1.5 %collective-permute-start.6 = (bf16[8,4,16,256]{3,2,1,0:T(8,128)(2,1)S(1)}, bf16[8,4,16,256]{3,2,1,0:T(8,128)(2,1)S(1)}, u32[]{:S(2)}, u32[]{:S(2)}) collective-permute-start(bf16[8,4,16,256]{3,2,1,0:T(8,128)(2,1)S(1)} %get-tuple-element.183), channel_id=1, source_target_pairs={{0,2},{2,0},{4,6},{6,4},{8,10},{10,8},{12,14},{14,12},{16,18},{18,... | collective-permute-start | bytes 786440 | tf_op jit(solution)/shard_map/ppermute | solution.py:307
  22.3 4.3 %collective-permute-start.7 = (bf16[2,4,16,256]{3,2,1,0:T(8,128)(2,1)S(1)}, bf16[2,4,16,256]{3,2,1,0:T(8,128)(2,1)S(1)}, u32[]{:S(2)}, u32[]{:S(2)}) collective-permute-start(bf16[2,4,16,256]{3,2,1,0:T(8,128)(2,1)S(1)} %get-tuple-element.187), channel_id=1, source_target_pairs={{0,4},{2,6},{4,0},{6,2},{8,12},{10,14},{12,8},{14,10},{16,20},{18,... | collective-permute-start | bytes 196616 | tf_op jit(solution)/shard_map/ppermute | solution.py:307
  23.2 5.2 %collective-permute-start.8 = (bf16[2,4,16,256]{3,2,1,0:T(8,128)(2,1)S(1)}, bf16[2,4,16,256]{3,2,1,0:T(8,128)(2,1)S(1)}, u32[]{:S(2)}, u32[]{:S(2)}) collective-permute-start(bf16[2,4,16,256]{3,2,1,0:T(8,128)(2,1)S(1)} %get-tuple-element.188), channel_id=1, source_target_pairs={{0,14},{2,12},{4,10},{6,8},{8,6},{10,4},{12,2},{14,0},{16,30},{18,... | collective-permute-start | bytes 196616 | tf_op jit(solution)/shard_map/ppermute | solution.py:307
  24.9 4.2 %collective-permute-start.9 = (bf16[2,4,16,256]{3,2,1,0:T(8,128)(2,1)S(1)}, bf16[2,4,16,256]{3,2,1,0:T(8,128)(2,1)S(1)}, u32[]{:S(2)}, u32[]{:S(2)}) collective-permute-start(bf16[2,4,16,256]{3,2,1,0:T(8,128)(2,1)S(1)} %get-tuple-element.189), channel_id=1, source_target_pairs={{0,10},{2,8},{4,14},{6,12},{8,2},{10,0},{12,6},{14,4},{16,26},{18,... | collective-permute-start | bytes 196616 | tf_op jit(solution)/shard_map/ppermute | solution.py:307
  29.1 4.4 %copy-start.1 = (f32[4,16,256]{2,1,0:T(8,128)S(1)}, f32[4,16,256]{2,1,0:T(8,128)}, u32[]{:S(2)}) copy-start(f32[4,16,256]{2,1,0:T(8,128)} %param.26) | copy-start | bytes 196612
  29.1 4.4 %copy-start = (f32[4,16,256]{2,1,0:T(8,128)S(1)}, f32[4,16,256]{2,1,0:T(8,128)}, u32[]{:S(2)}) copy-start(f32[4,16,256]{2,1,0:T(8,128)} %param.27) | copy-start | bytes 196612
  29.2 4.3 %collective-permute-start.10 = (bf16[4,16,256]{2,1,0:T(8,128)(2,1)S(1)}, bf16[4,16,256]{2,1,0:T(8,128)(2,1)S(1)}, u32[]{:S(2)}, u32[]{:S(2)}) collective-permute-start(bf16[4,16,256]{2,1,0:T(8,128)(2,1)S(1)} %fusion.7), channel_id=1, source_target_pairs={{0,18},{1,19},{2,16},{3,17},{4,22},{5,23},{6,20},{7,21},{8,26},{9,... | collective-permute-start | bytes 98312 | tf_op jit(solution)/shard_map/ppermute | solution.py:400

commit v9 on v8

--- a/solution.py
+++ b/solution.py
@@ -311,7 +311,7 @@
     place = lax.axis_index("cell")
     offsets = halvings(cells)[:-1]
     far, (a, b) = offsets[:-2], offsets[-2:]
-    crossed = [*far, b]
+    crossed = [*far, a]
     held = shard
     done = ()
 
@@ -338,7 +338,7 @@
 def assemble(held, arrived, weights, cells):
     offsets = halvings(cells)[:-1]
     far, (a, b) = offsets[:-2], offsets[-2:]
-    crossed = [*far, b]
+    crossed = [*far, a]
     place = lax.axis_index("cell")
     core = place % 2
     for offset in crossed:

time: 34.3 us -> 34.2 us (level)
  starting transfers between devices: 14.2 us -> 14.8 us
  waiting for transfers between devices: 9.07 us -> 8.49 us
    ppermute x9, waiting for transfers between devices: 7.31 us -> 6.89 us  [swap(): lax.ppermute(array, 'cell', [(i, i ^ vector_of(i)) for i in range(cells)])]
    ppermute x1, starting transfers between devices: 2.56 us -> 2.93 us  [meet(): return lax.ppermute(array, ('cell', 'brick'), pairs).astype(F32)]
where the time goes in v9:
time: 34.2 us; the launch traced here: 34 us
  starting transfers between devices  14.8 us (43%)
  Pallas kernels  8.96 us (26%)
  waiting for transfers between devices  8.49 us (25%)
  other arithmetic  0.9 us (3%)
  between operations  0.81 us (2%)
    ppermute x9, starting transfers between devices, swap(): lax.ppermute(array, 'cell', [(i, i ^ vector_of(i)) for i in range(cells)])  10.4 us
    ppermute x9, waiting for transfers between devices, swap(): lax.ppermute(array, 'cell', [(i, i ^ vector_of(i)) for i in range(cells)])  6.89 us
    pallas_call x4, Pallas kernels, index(): pl.pallas_call(functools.partial(index_kernel, first), out_shape=(pinned(...  3.95 us
    pallas_call x1, Pallas kernels, body(): pl.pallas_call(functools.partial(sweep_kernel, count, cells), out_shape=(...  3.32 us
    ppermute x1, starting transfers between devices, meet(): return lax.ppermute(array, ('cell', 'brick'), pairs).astype(F32)  2.93 us
    ppermute x1, waiting for transfers between devices, meet(): return lax.ppermute(array, ('cell', 'brick'), pairs).astype(F32)  1.6 us
    ppermute x1, starting transfers between devices, over_bricks(): lax.ppermute(array, 'brick', [(i, i ^ offset) for i in range(bricks)])  1.49 us
    pallas_call x1, Pallas kernels, embed_own(): pl.pallas_call(functools.partial(embed_kernel, int(paired)), out_shape=sh...  1.34 us
  transfers between devices with their start and end apart: 11, of which 8 were waited for; matrix products, arithmetic and copies ran while one was open for 0% of the time, Pallas kernels for 13%

profile of v9, /device:TPU:0, one launch (start us, length us, event | category | flops | bytes accessed | tf_op | source)
XLA Modules:
  0.0 34.0 jit_solution(10005270227052394090)
XLA Ops:
  0.6 1.3 %embed.1 = (bf16[4,16,256]{2,1,0:T(8,128)(2,1)S(1)}, f32[128,256]{1,0:T(8,128)S(1)}, bf16[128,256]{1,0:T(8,128)(2,1)S(1)}, bf16[256,128]{1,0:T(8,128)(2,1)S(1)},...) custom-call(f32[4,16,256]{2,1,0:T(8,128)} %master.1, ...), custom_call_target="tpu_custom_call" | custom-call | tf_op jit(solution)/shard_map/embed/pallas_call | solution.py:463
  2.0 3.5 %collective-permute-start = (bf16[4,16,256]{2,1,0:T(8,128)(2,1)S(1)}, bf16[4,16,256]{2,1,0:T(8,128)(2,1)S(1)}, u32[]{:S(2)}, u32[]{:S(2)}) collective-permute-start(bf16[4,16,256]{2,1,0:T(8,128)(2,1)S(1)} %get-tuple-element.94), channel_id=1, source_target_pairs={{0,18},{2,16},{4,22},{6,20},{8,26},{10,24},{12,30},{14,28},{16,2},... | collective-permute-start | bytes 98312 | tf_op jit(solution)/shard_map/ppermute | solution.py:307
  5.5 1.5 %collective-permute-start.1 = (bf16[528,128]{1,0:T(8,128)(2,1)S(1)}, bf16[528,128]{1,0:T(8,128)(2,1)S(1)}, u32[]{:S(2)}, u32[]{:S(2)}) collective-permute-start(bf16[528,128]{1,0:T(8,128)(2,1)S(1)} %get-tuple-element.121), channel_id=1, source_target_pairs={{0,1},{1,0},{2,3},{3,2},{4,5},{5,4},{6,7},{7,6},{8,9},{9,8},{10,11... | collective-permute-start | bytes 405512 | tf_op jit(solution)/shard_map/ppermute | solution.py:495
  7.0 1.0 %index.4 = (f32[8,96,128]{2,1,0:T(8,128)S(1)}, f32[96,128]{1,0:T(8,128)S(1)}) custom-call(s32[64,128]{1,0:T(8,128)S(1)} %get-tuple-element.115.neighbours, s32[1,128]{1,0:T(1,128)S(1)} %get-tuple-element.116.counts, f32[64,128]{1,0:T(8,128)S(1)} %get-tuple-element.117.distances, f32[1,8]{1,0:T(1,128)S(1)} %get-tuple-element.157.decay), custom_call_target="tpu_custom_call" | custom-call | tf_op jit(solution)/shard_map/index/pallas_call | solution.py:484
  8.0 0.0 collective-permute-done
  8.0 2.6 %collective-permute-start.2 = (bf16[2,4,16,256]{3,2,1,0:T(8,128)(2,1)S(1)}, bf16[2,4,16,256]{3,2,1,0:T(8,128)(2,1)S(1)}, u32[]{:S(2)}, u32[]{:S(2)}) collective-permute-start(bf16[2,4,16,256]{3,2,1,0:T(8,128)(2,1)S(1)} %maximum_select_fusion.4), channel_id=1, source_target_pairs={{0,14},{2,12},{4,10},{6,8},{8,6},{10,4},{12,2},{14,0},{16,30},{18,... | collective-permute-start | bytes 196616 | tf_op jit(solution)/shard_map/ppermute | solution.py:307
  10.7 0.1 collective-permute-start.3
  10.8 0.5 %collective-permute-start.4 = (bf16[2,4,16,256]{3,2,1,0:T(8,128)(2,1)S(1)}, bf16[2,4,16,256]{3,2,1,0:T(8,128)(2,1)S(1)}, u32[]{:S(2)}, u32[]{:S(2)}) collective-permute-start(bf16[2,4,16,256]{3,2,1,0:T(8,128)(2,1)S(1)} %maximum_select_fusion.4), channel_id=1, source_target_pairs={{0,4},{2,6},{4,0},{6,2},{8,12},{10,14},{12,8},{14,10},{16,20},{18,... | collective-permute-start | bytes 196616 | tf_op jit(solution)/shard_map/ppermute | solution.py:307
  11.3 1.0 %index.5 = (f32[8,96,128]{2,1,0:T(8,128)S(1)}, f32[96,128]{1,0:T(8,128)S(1)}) custom-call(s32[64,128]{1,0:T(8,128)S(1)} %get-tuple-element.115.neighbours, s32[1,128]{1,0:T(1,128)S(1)} %get-tuple-element.116.counts, f32[64,128]{1,0:T(8,128)S(1)} %get-tuple-element.117.distances, f32[1,8]{1,0:T(1,128)S(1)} %get-tuple-element.157.decay), custom_call_target="tpu_custom_call" | custom-call | tf_op jit(solution)/shard_map/index/pallas_call | solution.py:484
  12.3 0.0 collective-permute-done.1.packed
  12.3 0.3 %unpack.1 = (f32[128,256]{1,0:T(8,128)S(1)}, bf16[128,256]{1,0:T(8,128)(2,1)S(1)}, bf16[256,128]{1,0:T(8,128)(2,1)S(1)}, bf16[2,32,256]{2,1,0:T(8,128)(2,1)S(1)}...) custom-call(bf16[528,128]{1,0:T(8,128)(2,1)S(1)} %collective-permute-done.1.packed, ...), custom_call_target="tpu_custom_call" | custom-call | tf_op jit(solution)/shard_map/unpack/pallas_call | solution.py:473
  12.7 1.0 %index.6 = (f32[8,96,128]{2,1,0:T(8,128)S(1)}, f32[96,128]{1,0:T(8,128)S(1)}) custom-call(s32[64,128]{1,0:T(8,128)S(1)} %get-tuple-element.154.neighbours, s32[1,128]{1,0:T(1,128)S(1)} %get-tuple-element.155.counts, f32[64,128]{1,0:T(8,128)S(1)} %get-tuple-element.156.distances, f32[1,8]{1,0:T(1,128)S(1)} %get-tuple-element.157.decay), custom_call_target="tpu_custom_call" | custom-call | tf_op jit(solution)/shard_map/index/pallas_call | solution.py:484
  13.7 0.0 collective-permute-done.2
  13.7 1.1 %collective-permute-done.3 = bf16[2,4,16,256]{3,2,1,0:T(8,128)(2,1)S(1)} collective-permute-done((bf16[2,4,16,256]{3,2,1,0:T(8,128)(2,1)S(1)}, bf16[2,4,16,256]{3,2,1,0:T(8,128)(2,1)S(1)}, u32[]{:S(2)}, u32[]{:S(2)}) %collective-permute-start.3) | collective-permute-done | bytes 65568 | tf_op jit(solution)/shard_map/ppermute | solution.py:307
  14.8 0.4 %collective-permute-done.4 = bf16[2,4,16,256]{3,2,1,0:T(8,128)(2,1)S(1)} collective-permute-done((bf16[2,4,16,256]{3,2,1,0:T(8,128)(2,1)S(1)}, bf16[2,4,16,256]{3,2,1,0:T(8,128)(2,1)S(1)}, u32[]{:S(2)}, u32[]{:S(2)}) %collective-permute-start.4) | collective-permute-done | bytes 65568 | tf_op jit(solution)/shard_map/ppermute | solution.py:307
  15.3 0.1 collective-permute-start.5
  15.4 1.0 %index.7 = (f32[8,96,128]{2,1,0:T(8,128)S(1)}, f32[96,128]{1,0:T(8,128)S(1)}) custom-call(s32[64,128]{1,0:T(8,128)S(1)} %get-tuple-element.154.neighbours, s32[1,128]{1,0:T(1,128)S(1)} %get-tuple-element.155.counts, f32[64,128]{1,0:T(8,128)S(1)} %get-tuple-element.156.distances, f32[1,8]{1,0:T(1,128)S(1)} %get-tuple-element.157.decay), custom_call_target="tpu_custom_call" | custom-call | tf_op jit(solution)/shard_map/index/pallas_call | solution.py:484
  16.4 0.5 %collective-permute-done.5.arrived = bf16[2,2,2,4,16,256]{5,4,3,2,1,0:T(8,128)(2,1)S(1)} collective-permute-done((bf16[2,2,2,4,16,256]{5,4,3,2,1,0:T(8,128)(2,1)S(1)}, bf16[2,2,2,4,16,256]{5,4,3,2,1,0:T(8,128)(2,1)S(1)}, u32[]{:S(2)}, u32[]{:S(2)}) %collective-permute-start.5) | collective-permute-done | bytes 262176 | tf_op jit(solution)/shard_map/ppermute | solution.py:307
  16.9 3.3 %sweep.1 = (f32[1,128]{1,0:T(1,128)}, f32[8,4,16,256]{3,2,1,0:T(8,128)S(1)}, bf16[8,4,16,256]{3,2,1,0:T(8,128)(2,1)S(1)}) custom-call(bf16[2,2,2,4,16,256]{5,4,3,2,1,0:T(8,128)(2,1)S(1)} %maximum_select_fusion.held, bf16[2,2,2,4,16,256]{5,4,3,2,1,0:T(8,128)(2,1)S(1)} %collective-permute-done.5.arrived, f32[1,256]{1,0:T(1,128)S(1)} %get-tuple-element.162.readout, ...), custom_call_target="tpu_custom_call" | custom-call | tf_op jit(solution)/shard_map/sweep/pallas_call | solution.py:547
  20.2 0.2 collective-permute-start.6
  20.4 1.4 %collective-permute-done.6 = bf16[8,4,16,256]{3,2,1,0:T(8,128)(2,1)S(1)} collective-permute-done((bf16[8,4,16,256]{3,2,1,0:T(8,128)(2,1)S(1)}, bf16[8,4,16,256]{3,2,1,0:T(8,128)(2,1)S(1)}, u32[]{:S(2)}, u32[]{:S(2)}) %collective-permute-start.6) | collective-permute-done | bytes 262176 | tf_op jit(solution)/shard_map/ppermute | solution.py:307
  21.8 0.1 convert_add_fusion
  22.0 1.1 %collective-permute-start.7 = (bf16[2,4,16,256]{3,2,1,0:T(8,128)(2,1)S(1)}, bf16[2,4,16,256]{3,2,1,0:T(8,128)(2,1)S(1)}, u32[]{:S(2)}, u32[]{:S(2)}) collective-permute-start(bf16[2,4,16,256]{3,2,1,0:T(8,128)(2,1)S(1)} %get-tuple-element.187), channel_id=1, source_target_pairs={{0,4},{2,6},{4,0},{6,2},{8,12},{10,14},{12,8},{14,10},{16,20},{18,... | collective-permute-start | bytes 196616 | tf_op jit(solution)/shard_map/ppermute | solution.py:307
  23.1 1.5 %collective-permute-start.8 = (bf16[2,4,16,256]{3,2,1,0:T(8,128)(2,1)S(1)}, bf16[2,4,16,256]{3,2,1,0:T(8,128)(2,1)S(1)}, u32[]{:S(2)}, u32[]{:S(2)}) collective-permute-start(bf16[2,4,16,256]{3,2,1,0:T(8,128)(2,1)S(1)} %get-tuple-element.188), channel_id=1, source_target_pairs={{0,14},{2,12},{4,10},{6,8},{8,6},{10,4},{12,2},{14,0},{16,30},{18,... | collective-permute-start | bytes 196616 | tf_op jit(solution)/shard_map/ppermute | solution.py:307
  24.6 0.7 %collective-permute-start.9 = (bf16[2,4,16,256]{3,2,1,0:T(8,128)(2,1)S(1)}, bf16[2,4,16,256]{3,2,1,0:T(8,128)(2,1)S(1)}, u32[]{:S(2)}, u32[]{:S(2)}) collective-permute-start(bf16[2,4,16,256]{3,2,1,0:T(8,128)(2,1)S(1)} %get-tuple-element.189), channel_id=1, source_target_pairs={{0,10},{2,8},{4,14},{6,12},{8,2},{10,0},{12,6},{14,4},{16,26},{18,... | collective-permute-start | bytes 196616 | tf_op jit(solution)/shard_map/ppermute | solution.py:307
  25.3 1.1 %collective-permute-done.7 = bf16[2,4,16,256]{3,2,1,0:T(8,128)(2,1)S(1)} collective-permute-done((bf16[2,4,16,256]{3,2,1,0:T(8,128)(2,1)S(1)}, bf16[2,4,16,256]{3,2,1,0:T(8,128)(2,1)S(1)}, u32[]{:S(2)}, u32[]{:S(2)}) %collective-permute-start.7) | collective-permute-done | bytes 65568 | tf_op jit(solution)/shard_map/ppermute | solution.py:307
  26.3 2.1 %collective-permute-done.8 = bf16[2,4,16,256]{3,2,1,0:T(8,128)(2,1)S(1)} collective-permute-done((bf16[2,4,16,256]{3,2,1,0:T(8,128)(2,1)S(1)}, bf16[2,4,16,256]{3,2,1,0:T(8,128)(2,1)S(1)}, u32[]{:S(2)}, u32[]{:S(2)}) %collective-permute-start.8) | collective-permute-done | bytes 65568 | tf_op jit(solution)/shard_map/ppermute | solution.py:307
  28.4 0.3 %collective-permute-done.9 = bf16[2,4,16,256]{3,2,1,0:T(8,128)(2,1)S(1)} collective-permute-done((bf16[2,4,16,256]{3,2,1,0:T(8,128)(2,1)S(1)}, bf16[2,4,16,256]{3,2,1,0:T(8,128)(2,1)S(1)}, u32[]{:S(2)}, u32[]{:S(2)}) %collective-permute-start.9) | collective-permute-done | bytes 65568 | tf_op jit(solution)/shard_map/ppermute | solution.py:307
  28.7 0.0 copy-start.1
  28.8 0.0 copy-start
  28.8 2.9 %collective-permute-start.10 = (bf16[4,16,256]{2,1,0:T(8,128)(2,1)S(1)}, bf16[4,16,256]{2,1,0:T(8,128)(2,1)S(1)}, u32[]{:S(2)}, u32[]{:S(2)}) collective-permute-start(bf16[4,16,256]{2,1,0:T(8,128)(2,1)S(1)} %fusion.7), channel_id=1, source_target_pairs={{0,18},{1,19},{2,16},{3,17},{4,22},{5,23},{6,20},{7,21},{8,26},{9,... | collective-permute-start | bytes 98312 | tf_op jit(solution)/shard_map/ppermute | solution.py:400
  31.7 1.6 %collective-permute-done.10 = bf16[4,16,256]{2,1,0:T(8,128)(2,1)S(1)} collective-permute-done((bf16[4,16,256]{2,1,0:T(8,128)(2,1)S(1)}, bf16[4,16,256]{2,1,0:T(8,128)(2,1)S(1)}, u32[]{:S(2)}, u32[]{:S(2)}) %collective-permute-start.10) | collective-permute-done | bytes 32800 | tf_op jit(solution)/shard_map/ppermute | solution.py:400
  33.3 0.0 copy-done.1
  33.3 0.0 copy-done
  33.3 0.7 %add_divide_fusion = (f32[4,16,256]{2,1,0:T(8,128)}, f32[4,16,256]{2,1,0:T(8,128)}, f32[4,16,256]{2,1,0:T(8,128)}) fusion(bf16[4,16,256]{2,1,0:T(8,128)(2,1)S(1)} %collective-permute-done.10, f32[2,4,16,256]{3,2,1,0:T(8,128)S(1)} %fusion.1, s32[]{:T(128)S(6)} %select_n.212, f32[4,16,256]{2,1,0:T(8,128)S(1)} %copy-done, f32[4,16,256]{2,1,0:T(8,128)S(1)} %copy-done.1), kind=kLoop, calls=%fused_computation.19 | loop fusion | flops 180224 | bytes 425988 | tf_op jit(solution)/shard_map/div | solution.py:568
  (10 shorter events, 0.2 us)
Async XLA Ops:
  2.0 6.0 %collective-permute-start = (bf16[4,16,256]{2,1,0:T(8,128)(2,1)S(1)}, bf16[4,16,256]{2,1,0:T(8,128)(2,1)S(1)}, u32[]{:S(2)}, u32[]{:S(2)}) collective-permute-start(bf16[4,16,256]{2,1,0:T(8,128)(2,1)S(1)} %get-tuple-element.94), channel_id=1, source_target_pairs={{0,18},{2,16},{4,22},{6,20},{8,26},{10,24},{12,30},{14,28},{16,2},... | collective-permute-start | bytes 98312 | tf_op jit(solution)/shard_map/ppermute | solution.py:307
  5.5 6.8 %collective-permute-start.1 = (bf16[528,128]{1,0:T(8,128)(2,1)S(1)}, bf16[528,128]{1,0:T(8,128)(2,1)S(1)}, u32[]{:S(2)}, u32[]{:S(2)}) collective-permute-start(bf16[528,128]{1,0:T(8,128)(2,1)S(1)} %get-tuple-element.121), channel_id=1, source_target_pairs={{0,1},{1,0},{2,3},{3,2},{4,5},{5,4},{6,7},{7,6},{8,9},{9,8},{10,11... | collective-permute-start | bytes 405512 | tf_op jit(solution)/shard_map/ppermute | solution.py:495
  8.0 5.6 %collective-permute-start.2 = (bf16[2,4,16,256]{3,2,1,0:T(8,128)(2,1)S(1)}, bf16[2,4,16,256]{3,2,1,0:T(8,128)(2,1)S(1)}, u32[]{:S(2)}, u32[]{:S(2)}) collective-permute-start(bf16[2,4,16,256]{3,2,1,0:T(8,128)(2,1)S(1)} %maximum_select_fusion.4), channel_id=1, source_target_pairs={{0,14},{2,12},{4,10},{6,8},{8,6},{10,4},{12,2},{14,0},{16,30},{18,... | collective-permute-start | bytes 196616 | tf_op jit(solution)/shard_map/ppermute | solution.py:307
  10.7 4.1 %collective-permute-start.3 = (bf16[2,4,16,256]{3,2,1,0:T(8,128)(2,1)S(1)}, bf16[2,4,16,256]{3,2,1,0:T(8,128)(2,1)S(1)}, u32[]{:S(2)}, u32[]{:S(2)}) collective-permute-start(bf16[2,4,16,256]{3,2,1,0:T(8,128)(2,1)S(1)} %maximum_select_fusion.4), channel_id=1, source_target_pairs={{0,10},{2,8},{4,14},{6,12},{8,2},{10,0},{12,6},{14,4},{16,26},{18,... | collective-permute-start | bytes 196616 | tf_op jit(solution)/shard_map/ppermute | solution.py:307
  10.8 4.4 %collective-permute-start.4 = (bf16[2,4,16,256]{3,2,1,0:T(8,128)(2,1)S(1)}, bf16[2,4,16,256]{3,2,1,0:T(8,128)(2,1)S(1)}, u32[]{:S(2)}, u32[]{:S(2)}) collective-permute-start(bf16[2,4,16,256]{3,2,1,0:T(8,128)(2,1)S(1)} %maximum_select_fusion.4), channel_id=1, source_target_pairs={{0,4},{2,6},{4,0},{6,2},{8,12},{10,14},{12,8},{14,10},{16,20},{18,... | collective-permute-start | bytes 196616 | tf_op jit(solution)/shard_map/ppermute | solution.py:307
  15.3 1.6 %collective-permute-start.5 = (bf16[2,2,2,4,16,256]{5,4,3,2,1,0:T(8,128)(2,1)S(1)}, bf16[2,2,2,4,16,256]{5,4,3,2,1,0:T(8,128)(2,1)S(1)}, u32[]{:S(2)}, u32[]{:S(2)}) collective-permute-start(bf16[2,2,2,4,16,256]{5,4,3,2,1,0:T(8,128)(2,1)S(1)} %maximum_select_fusion.held), channel_id=1, source_target_pairs={{0,2},{2,0},{4,6},{6,4},{8,10},{10,8},{12,14},{14,12},{16,18},{18,... | collective-permute-start | bytes 786440 | tf_op jit(solution)/shard_map/ppermute | solution.py:307
  20.2 1.6 %collective-permute-start.6 = (bf16[8,4,16,256]{3,2,1,0:T(8,128)(2,1)S(1)}, bf16[8,4,16,256]{3,2,1,0:T(8,128)(2,1)S(1)}, u32[]{:S(2)}, u32[]{:S(2)}) collective-permute-start(bf16[8,4,16,256]{3,2,1,0:T(8,128)(2,1)S(1)} %get-tuple-element.183), channel_id=1, source_target_pairs={{0,2},{2,0},{4,6},{6,4},{8,10},{10,8},{12,14},{14,12},{16,18},{18,... | collective-permute-start | bytes 786440 | tf_op jit(solution)/shard_map/ppermute | solution.py:307
  22.0 4.3 %collective-permute-start.7 = (bf16[2,4,16,256]{3,2,1,0:T(8,128)(2,1)S(1)}, bf16[2,4,16,256]{3,2,1,0:T(8,128)(2,1)S(1)}, u32[]{:S(2)}, u32[]{:S(2)}) collective-permute-start(bf16[2,4,16,256]{3,2,1,0:T(8,128)(2,1)S(1)} %get-tuple-element.187), channel_id=1, source_target_pairs={{0,4},{2,6},{4,0},{6,2},{8,12},{10,14},{12,8},{14,10},{16,20},{18,... | collective-permute-start | bytes 196616 | tf_op jit(solution)/shard_map/ppermute | solution.py:307
  23.1 5.3 %collective-permute-start.8 = (bf16[2,4,16,256]{3,2,1,0:T(8,128)(2,1)S(1)}, bf16[2,4,16,256]{3,2,1,0:T(8,128)(2,1)S(1)}, u32[]{:S(2)}, u32[]{:S(2)}) collective-permute-start(bf16[2,4,16,256]{3,2,1,0:T(8,128)(2,1)S(1)} %get-tuple-element.188), channel_id=1, source_target_pairs={{0,14},{2,12},{4,10},{6,8},{8,6},{10,4},{12,2},{14,0},{16,30},{18,... | collective-permute-start | bytes 196616 | tf_op jit(solution)/shard_map/ppermute | solution.py:307
  24.6 4.1 %collective-permute-start.9 = (bf16[2,4,16,256]{3,2,1,0:T(8,128)(2,1)S(1)}, bf16[2,4,16,256]{3,2,1,0:T(8,128)(2,1)S(1)}, u32[]{:S(2)}, u32[]{:S(2)}) collective-permute-start(bf16[2,4,16,256]{3,2,1,0:T(8,128)(2,1)S(1)} %get-tuple-element.189), channel_id=1, source_target_pairs={{0,10},{2,8},{4,14},{6,12},{8,2},{10,0},{12,6},{14,4},{16,26},{18,... | collective-permute-start | bytes 196616 | tf_op jit(solution)/shard_map/ppermute | solution.py:307
  28.7 4.6 %copy-start.1 = (f32[4,16,256]{2,1,0:T(8,128)S(1)}, f32[4,16,256]{2,1,0:T(8,128)}, u32[]{:S(2)}) copy-start(f32[4,16,256]{2,1,0:T(8,128)} %param.26) | copy-start | bytes 196612
  28.8 4.6 %copy-start = (f32[4,16,256]{2,1,0:T(8,128)S(1)}, f32[4,16,256]{2,1,0:T(8,128)}, u32[]{:S(2)}) copy-start(f32[4,16,256]{2,1,0:T(8,128)} %param.27) | copy-start | bytes 196612
  28.8 4.5 %collective-permute-start.10 = (bf16[4,16,256]{2,1,0:T(8,128)(2,1)S(1)}, bf16[4,16,256]{2,1,0:T(8,128)(2,1)S(1)}, u32[]{:S(2)}, u32[]{:S(2)}) collective-permute-start(bf16[4,16,256]{2,1,0:T(8,128)(2,1)S(1)} %fusion.7), channel_id=1, source_target_pairs={{0,18},{1,19},{2,16},{3,17},{4,22},{5,23},{6,20},{7,21},{8,26},{9,... | collective-permute-start | bytes 98312 | tf_op jit(solution)/shard_map/ppermute | solution.py:400
